TPU v7x, 32 devices: a whole 2x2x4 slice. The times are simulated.
32 devices in a mesh: section: 2 (over y), dp: 4 (over x, core), tensor: 4 (over z).
Axes of the slice: x: 2, y: 2, z: 4, core: 2. Of those that a mesh axis runs over, the one named last changes fastest.
Arguments:
- inputs: bfloat16 [2, 4, 4096, 1024], P('section', None, ('dp', 'tensor')), may hold values from -6 to 6
- lengths: int32 [2, 4, 4], P(None, None, 'dp'), may hold values from 1 to 1024, 2560 in all within a row
- cotangent: bfloat16 [4, 4096, 1024], P(None, ('dp', 'tensor')), may hold values from -6 to 6
- qkv_weight: bfloat16 [2, 1024, 3072], P('section', None, 'tensor'), may hold values from -0.25 to 0.25
- attn_out_weight: bfloat16 [2, 1024, 1024], P('section', 'tensor'), may hold values from -1.5 to 1.5
- cross_weight: bfloat16 [2, 1024, 2048], P('section', None, 'tensor'), may hold values from -1.5 to 1.5
- ffn_in_weight: bfloat16 [2, 1024, 4096], P('section', None, 'tensor'), may hold values from -0.1875 to 0.1875
- ffn_in_bias: bfloat16 [2, 4096], P('section', 'tensor'), may hold values from -3 to 3
- ffn_out_weight: bfloat16 [2, 4096, 1024], P('section', 'tensor'), may hold values from -0.375 to 0.375
- ffn_out_bias: bfloat16 [2, 1024], P('section'), may hold values from -3 to 3
- norm_gain: bfloat16 [2, 3, 1024], P('section'), may hold values from 0.5 to 1.5
- norm_bias: bfloat16 [2, 3, 1024], P('section'), may hold values from -2 to 2
Outputs:
- outputs: bfloat16 [2, 4, 4096, 1024], P('section', None, ('dp', 'tensor'))
- input_grad: float32 [2, 4, 4096, 1024], P('section', None, ('dp', 'tensor'))
- qkv_grad: float32 [2, 1024, 3072], P('section', None, 'tensor')
- attn_out_grad: float32 [2, 1024, 1024], P('section', 'tensor')
- cross_grad: float32 [2, 1024, 2048], P('section', None, 'tensor')
- ffn_in_grad: float32 [2, 1024, 4096], P('section', None, 'tensor')
- ffn_in_bias_grad: float32 [2, 4096], P('section', 'tensor')
- ffn_out_grad: float32 [2, 4096, 1024], P('section', 'tensor')
- ffn_out_bias_grad: float32 [2, 1024], P('section')
- norm_gain_grad: float32 [2, 3, 1024], P('section')
- norm_bias_grad: float32 [2, 3, 1024], P('section')
Inputs may be any that keep to these rules, and one draw needn't show every extreme that they name: In each micro-batch and for each index of the first dimension the 4 lengths add up to 2560, and the longest is 1024.
All inputs are finite; a program needn't handle non-finite values. No bound on the sum of `lengths` on one device may be relied on, other than what follows from the above.
Results may differ from a plain program's by a relative error of at most 0.03.
Values may be sent and summed in bfloat16 or wider, within the bound.
A program may use at most 640 MiB of HBM per device.

v0:
```python
import jax
import jax.numpy as jnp
from jax import lax
from jax.sharding import PartitionSpec as P

HS = 64
QBLOCK = 512


ALPHA_ENC = 0.81 * (100.0**5) ** (1.0 / 16.0)
ALPHA_DEC = (3.0 * 100.0) ** 0.25
EPS = 1e-05
NEG = -1e30
ROW_DIMS = (((0,), (0,)), ((), ()))
COL_DIMS = (((1,), (1,)), ((), ()))


def from_behind(block, axis, distance):
    devices = range(lax.axis_size(axis))
    route = [(i - distance, i) for i in devices if i - distance in devices]
    return lax.ppermute(block, axis, route)


def layer_norm(values, gain_row, shift_row):
    centered = values - jnp.mean(values, axis=-1, keepdims=True)
    factor = lax.rsqrt(jnp.mean(centered * centered, axis=-1, keepdims=True) + EPS)
    normed = centered * factor
    return (normed * gain_row + shift_row, normed, factor)


def norm_back(gradient, normed, factor, gain_row):
    scaled = gradient * gain_row
    centred = (
        scaled
        - jnp.mean(scaled, axis=-1, keepdims=True)
        - normed * jnp.mean(scaled * normed, axis=-1, keepdims=True)
    )
    return (centred * factor, jnp.sum(gradient * normed, axis=0), jnp.sum(gradient, axis=0))


def visible(first_row, row_count, key_count, seq_lengths, causal):
    key_pos = lax.broadcasted_iota(jnp.int32, (1, row_count, key_count), 2)
    query_pos = first_row + lax.broadcasted_iota(jnp.int32, (1, row_count, key_count), 1)
    inside = key_pos < seq_lengths[:, None, None]
    return inside & ((key_pos <= query_pos) | jnp.logical_not(causal))


def attend(queries, keys_in, values, seq_lengths, causal):
    key_count = queries.shape[1]
    score_scale = queries.shape[3] ** (-0.5)
    row_block = min(QBLOCK, key_count)
    mixed_parts, lse_parts = ([], [])
    for first_row in range(0, key_count, row_block):
        allowed = visible(first_row, row_block, key_count, seq_lengths, causal)
        raw_scores = jnp.einsum(
            "bqhe,bkhe->bhqk",
            queries[:, first_row : first_row + row_block],
            keys_in,
            preferred_element_type=jnp.float32,
        )
        scores = jnp.where(allowed[:, None], raw_scores * score_scale, NEG)
        row_max = jnp.max(scores, axis=-1, keepdims=True)
        expo_vals = jnp.exp(scores - row_max)
        row_total = jnp.sum(expo_vals, axis=-1, keepdims=True)
        weights = (expo_vals / row_total).astype(jnp.bfloat16)
        mixed_block = jnp.einsum(
            "bhqk,bkhe->bqhe", weights, values, preferred_element_type=jnp.float32
        )
        mixed_parts.append(mixed_block.astype(jnp.bfloat16))
        lse_parts.append(row_max + jnp.log(row_total))
    return (jnp.concatenate(mixed_parts, axis=1), jnp.concatenate(lse_parts, axis=2))


def attend_back(grad_mixed, queries, keys_in, values, log_totals, seq_lengths, causal):
    key_count = queries.shape[1]
    score_scale = queries.shape[3] ** (-0.5)
    row_block = min(QBLOCK, key_count)
    query_parts = []
    grad_keys = jnp.zeros(keys_in.shape, jnp.float32)
    grad_values = jnp.zeros(values.shape, jnp.float32)
    for first_row in range(0, key_count, row_block):
        query_part = queries[:, first_row : first_row + row_block]
        grad_part = grad_mixed[:, first_row : first_row + row_block]
        allowed = visible(first_row, row_block, key_count, seq_lengths, causal)
        raw_scores = jnp.einsum(
            "bqhe,bkhe->bhqk", query_part, keys_in, preferred_element_type=jnp.float32
        )
        scores = jnp.where(allowed[:, None], raw_scores * score_scale, NEG)
        probs = jnp.exp(scores - log_totals[:, :, first_row : first_row + row_block])
        grad_probs = jnp.einsum(
            "bqhe,bkhe->bhqk", grad_part, values, preferred_element_type=jnp.float32
        )
        grad_scores = probs * (grad_probs - jnp.sum(probs * grad_probs, axis=-1, keepdims=True))
        grad_raw = (grad_scores * score_scale).astype(jnp.bfloat16)
        query_parts.append(
            jnp.einsum("bhqk,bkhe->bqhe", grad_raw, keys_in, preferred_element_type=jnp.float32)
        )
        grad_keys = grad_keys + jnp.einsum(
            "bhqk,bqhe->bkhe", grad_raw, query_part, preferred_element_type=jnp.float32
        )
        grad_values = grad_values + jnp.einsum(
            "bhqk,bqhe->bkhe",
            probs.astype(jnp.bfloat16),
            grad_part,
            preferred_element_type=jnp.float32,
        )
    return (jnp.concatenate(query_parts, axis=1), grad_keys, grad_values)


def ffn_forward(rows_in, in_proj, in_shift, down_proj):
    pre_act = jnp.dot(rows_in, in_proj, preferred_element_type=jnp.float32) + in_shift
    hidden = jax.nn.gelu(pre_act).astype(jnp.bfloat16)
    return (pre_act, jnp.dot(hidden, down_proj, preferred_element_type=jnp.float32))


def ffn_backward(grad_in, rows_in, pre_act, in_proj, down_proj):
    activated, slope_back = jax.vjp(jax.nn.gelu, pre_act)
    hidden = activated.astype(jnp.bfloat16)
    grad_down = lax.dot_general(hidden, grad_in, ROW_DIMS, preferred_element_type=jnp.float32)
    grad_hidden = lax.dot_general(grad_in, down_proj, COL_DIMS, preferred_element_type=jnp.float32)
    grad_pre = slope_back(grad_hidden)[0].astype(jnp.bfloat16)
    grad_shift = jnp.sum(grad_pre.astype(jnp.float32), axis=0)
    grad_inner = lax.dot_general(rows_in, grad_pre, ROW_DIMS, preferred_element_type=jnp.float32)
    grad_rows_out = lax.dot_general(grad_pre, in_proj, COL_DIMS, preferred_element_type=jnp.float32)
    return (grad_rows_out, grad_inner, grad_shift, grad_down)


def gather_rows(shard):
    return lax.all_gather(shard, "tensor", axis=0, tiled=True)


def sum_rows(partial_value):
    return lax.psum_scatter(partial_value, "tensor", scatter_dimension=0, tiled=True)


def ffn_input_rows(shard):
    return lax.all_gather(shard, "tensor", axis=0, tiled=True)


def ffn_sum_rows(partial_value):
    return lax.psum_scatter(
        partial_value.astype(jnp.bfloat16), "tensor", scatter_dimension=0, tiled=True
    ).astype(jnp.float32)


def grad_rows(shard):
    return lax.all_gather(shard, "tensor", axis=0, tiled=True)


def grad_sums(partial_value):
    return lax.psum_scatter(
        partial_value.astype(jnp.bfloat16), "tensor", scatter_dimension=0, tiled=True
    ).astype(jnp.float32)


def ffn_grad_rows(shard):
    return lax.all_gather(shard, "tensor", axis=0, tiled=True)


def ffn_grad_sums(partial_value):
    return lax.psum_scatter(
        partial_value.astype(jnp.bfloat16), "tensor", scatter_dimension=0, tiled=True
    ).astype(jnp.float32)


def body(
    inputs,
    lengths,
    cotangent,
    qkv_weight,
    attn_out_weight,
    cross_weight,
    ffn_in_weight,
    ffn_in_bias,
    ffn_out_weight,
    ffn_out_bias,
    norm_gain,
    norm_bias,
):
    tensor_count = lax.axis_size("tensor")
    section = lax.axis_index("section")
    tensor_index = lax.axis_index("tensor")
    decoder = section == 1
    alpha = jnp.where(decoder, ALPHA_DEC, ALPHA_ENC).astype(jnp.float32)
    batches, shard_rows, width = (inputs.shape[1], inputs.shape[2], inputs.shape[3])
    seq_count = lengths.shape[2]
    full_rows = shard_rows * tensor_count
    slots = full_rows // seq_count
    qkv_proj = qkv_weight[0]
    head_local = qkv_proj.shape[1] // (3 * HS)
    head_cols = head_local * HS
    out_proj = attn_out_weight[0]
    cross_proj = cross_weight[0]
    cross_split = cross_proj.reshape(width, head_local, 2, HS)
    first_cols = cross_split[:, :, 0].reshape(width, head_cols)
    second_cols = cross_split[:, :, 1].reshape(width, head_cols)
    in_proj = ffn_in_weight[0]
    in_shift = ffn_in_bias[0].astype(jnp.float32)
    down_proj = ffn_out_weight[0]
    hidden_width = in_proj.shape[1]
    down_shift = ffn_out_bias[0].astype(jnp.float32)
    gains = norm_gain[0].astype(jnp.float32)
    shifts = norm_bias[0].astype(jnp.float32)
    own_lengths = lax.dynamic_index_in_dim(lengths, section, 0, keepdims=False)
    source_lengths = lengths[0]
    row_index = tensor_index * shard_rows + lax.iota(jnp.int32, shard_rows)
    row_seq = row_index // slots
    row_pos = row_index % slots
    seq_ids = lax.iota(jnp.int32, seq_count)
    lse_shape = (seq_count, head_local, slots, 1)

    def zeros_float(shape):
        return jnp.zeros(shape, jnp.float32)

    def zeros_low(shape):
        return jnp.zeros(shape, jnp.bfloat16)

    def to_heads(flat_rows):
        return flat_rows.reshape(seq_count, slots, flat_rows.shape[1] // HS, HS)

    def to_rows(split_rows):
        return split_rows.reshape(full_rows, -1)

    def cross_forward(query_rows, kv_source, source_len):
        kv_split = kv_source.reshape(seq_count, slots, head_local, 2, HS)
        query_c = jnp.dot(query_rows, first_cols, preferred_element_type=jnp.float32).astype(
            jnp.bfloat16
        )
        mixed_c, lse_cross = attend(
            to_heads(query_c), kv_split[:, :, :, 0], kv_split[:, :, :, 1], source_len, False
        )
        mixed_c = to_rows(mixed_c)
        partial_value = lax.dot_general(
            mixed_c, second_cols, COL_DIMS, preferred_element_type=jnp.float32
        )
        return (query_c, mixed_c, lse_cross, partial_value)

    kv_held = zeros_low((full_rows, 2 * head_cols))
    kv_ticks, kept_ticks, out_ticks = ([], [], [])
    for tick_index in range(batches + 1):
        batch = jnp.clip(tick_index - section, 0, batches - 1)
        x_shard = lax.dynamic_index_in_dim(inputs[0], batch, 0, keepdims=False)
        own_len = lax.dynamic_index_in_dim(own_lengths, batch, 0, keepdims=False)
        source_len = lax.dynamic_index_in_dim(source_lengths, batch, 0, keepdims=False)
        x_full = gather_rows(x_shard)
        qkv = jnp.dot(x_full, qkv_proj, preferred_element_type=jnp.float32).astype(jnp.bfloat16)
        qkv_split = qkv.reshape(seq_count, slots, head_local, 3, HS)
        mixed, lse_self = attend(
            qkv_split[:, :, :, 0], qkv_split[:, :, :, 1], qkv_split[:, :, :, 2], own_len, decoder
        )
        mixed = to_rows(mixed)
        attn_sum = sum_rows(jnp.dot(mixed, out_proj, preferred_element_type=jnp.float32))
        resid_a, norm_a, factor_a = layer_norm(
            alpha * x_shard.astype(jnp.float32) + attn_sum, gains[0], shifts[0]
        )
        a_shard = resid_a.astype(jnp.bfloat16)
        a_full = gather_rows(a_shard)

        def enc_second():
            hidden_made, partial_value = ffn_forward(a_full, in_proj, in_shift, down_proj)
            return (
                hidden_made,
                zeros_low((full_rows, head_cols)),
                zeros_low((full_rows, head_cols)),
                zeros_float(lse_shape),
                partial_value,
            )

        def dec_second():
            query_c, mixed_c, lse_cross, partial_value = cross_forward(a_full, kv_held, source_len)
            return (
                zeros_float((full_rows, hidden_width)),
                query_c,
                mixed_c,
                lse_cross,
                partial_value,
            )

        hidden_enc, query_c, mixed_c, lse_cross, partial_value = lax.cond(
            decoder, dec_second, enc_second
        )
        second_sum = sum_rows(partial_value)
        resid_ye, norm_ye, factor_ye = layer_norm(
            alpha * resid_a + second_sum + down_shift, gains[2], shifts[2]
        )
        resid_c, norm_c, factor_c = layer_norm(alpha * resid_a + second_sum, gains[1], shifts[1])
        wide_rows = ffn_input_rows(jnp.where(decoder, resid_c, resid_ye).astype(jnp.bfloat16))

        def enc_third():
            kv_made = jnp.dot(wide_rows, cross_proj, preferred_element_type=jnp.float32).astype(
                jnp.bfloat16
            )
            return (
                kv_made,
                zeros_float((full_rows, hidden_width)),
                zeros_float((full_rows, width)),
            )

        def dec_third():
            hidden_made, partial_made = ffn_forward(wide_rows, in_proj, in_shift, down_proj)
            return (zeros_low((full_rows, 2 * head_cols)), hidden_made, partial_made)

        kv_out, hidden_dec, partial_third = lax.cond(decoder, dec_third, enc_third)
        third_sum = ffn_sum_rows(partial_third)
        resid_yd, norm_yd, factor_yd = layer_norm(
            alpha * resid_c + third_sum + down_shift, gains[2], shifts[2]
        )
        resid_y = jnp.where(decoder, resid_yd, resid_ye)
        norm_y = jnp.where(decoder, norm_yd, norm_ye)
        factor_y = jnp.where(decoder, factor_yd, factor_ye)
        hidden = jnp.where(decoder, hidden_dec, hidden_enc)
        ffn_rows = jnp.where(decoder, wide_rows, a_full)
        y_shard = resid_y.astype(jnp.bfloat16)
        kv_held = from_behind(kv_out, "section", 1)
        kv_ticks.append(kv_held)
        out_ticks.append(y_shard)
        kept_ticks.append(
            dict(
                x_rows=x_full,
                qkv=qkv,
                mixed=mixed,
                lse_self=lse_self,
                a_rows=a_full,
                kv_rows=wide_rows,
                ffn_rows=ffn_rows,
                hidden=hidden,
                query_c=query_c,
                mixed_c=mixed_c,
                lse_cross=lse_cross,
                norm_a=norm_a,
                factor_a=factor_a,
                norm_c=norm_c,
                factor_c=factor_c,
                norm_y=norm_y,
                factor_y=factor_y,
            )
        )
    kept_all = jax.tree.map(lambda *leaves: jnp.stack(leaves), *kept_ticks)
    kv_stack = jnp.stack(kv_ticks)
    outputs = lax.dynamic_slice_in_dim(jnp.stack(out_ticks), section, batches, 0)
    totals = dict(
        qkv=zeros_float(qkv_proj.shape),
        outer=zeros_float(out_proj.shape),
        cross=zeros_float(cross_proj.shape),
        inner=zeros_float(in_proj.shape),
        inner_shift=zeros_float(in_shift.shape),
        down=zeros_float(down_proj.shape),
        down_shift=zeros_float(down_shift.shape),
        gain=zeros_float(gains.shape),
        shift=zeros_float(shifts.shape),
    )
    zero_ffn = (
        zeros_float(in_proj.shape),
        zeros_float(in_shift.shape),
        zeros_float(down_proj.shape),
    )
    zero_cross = zeros_float((width, 2 * head_cols))
    dkv_held = zeros_low((full_rows, 2 * head_cols))
    grad_ticks = []
    for tick_index in range(batches + 1):
        batch_raw = batches - tick_index - section
        live = (batch_raw >= 0) & (batch_raw < batches)
        batch = jnp.clip(batch_raw, 0, batches - 1)
        kept = jax.tree.map(
            lambda leaf_value: lax.dynamic_index_in_dim(
                leaf_value, batch + section, 0, keepdims=False
            ),
            kept_all,
        )
        own_len = lax.dynamic_index_in_dim(own_lengths, batch, 0, keepdims=False)
        source_len = lax.dynamic_index_in_dim(source_lengths, batch, 0, keepdims=False)
        kv_now = lax.dynamic_index_in_dim(kv_stack, batch, 0, keepdims=False)
        kv_split = kv_now.reshape(seq_count, slots, head_local, 2, HS)
        own_rows = jnp.sum(
            jnp.where(row_seq[:, None] == seq_ids[None, :], own_len[None, :], 0), axis=1
        )
        grad_top = lax.dynamic_index_in_dim(cotangent, batch, 0, keepdims=False).astype(jnp.float32)
        grad_top = jnp.where((row_pos < own_rows)[:, None], grad_top, 0.0)
        grad_r3d, gain_yd, shift_yd = norm_back(
            grad_top, kept["norm_y"], kept["factor_y"], gains[2]
        )
        dkv_now = dkv_held

        def kv_back():
            partial_value = lax.dot_general(
                dkv_now, cross_proj, COL_DIMS, preferred_element_type=jnp.float32
            )
            grad_cross_enc = lax.dot_general(
                kept["kv_rows"], dkv_now, ROW_DIMS, preferred_element_type=jnp.float32
            )
            return (partial_value, grad_cross_enc)

        def cross_back(grad_full):
            grad_mixed_c = jnp.dot(
                grad_full, second_cols, preferred_element_type=jnp.float32
            ).astype(jnp.bfloat16)
            grad_second = lax.dot_general(
                grad_full, kept["mixed_c"], ROW_DIMS, preferred_element_type=jnp.float32
            )
            grad_qc, grad_kc, grad_vc = attend_back(
                to_heads(grad_mixed_c),
                to_heads(kept["query_c"]),
                kv_split[:, :, :, 0],
                kv_split[:, :, :, 1],
                kept["lse_cross"],
                source_len,
                False,
            )
            grad_qc = to_rows(grad_qc).astype(jnp.bfloat16)
            grad_first = lax.dot_general(
                kept["a_rows"], grad_qc, ROW_DIMS, preferred_element_type=jnp.float32
            )
            partial_value = lax.dot_general(
                grad_qc, first_cols, COL_DIMS, preferred_element_type=jnp.float32
            )
            grad_kv = (
                jnp.stack([grad_kc, grad_vc], axis=3)
                .astype(jnp.bfloat16)
                .reshape(full_rows, 2 * head_cols)
            )
            grad_cross_dec = jnp.stack(
                [
                    grad_first.reshape(width, head_local, HS),
                    grad_second.reshape(width, head_local, HS),
                ],
                axis=2,
            ).reshape(width, 2 * head_cols)
            return (partial_value, grad_cross_dec, grad_kv)

        first_full = grad_rows(jnp.where(decoder, grad_r3d, 0.0).astype(jnp.bfloat16))

        def enc_first():
            partial_value, grad_cross_enc = kv_back()
            return (partial_value, grad_cross_enc) + zero_ffn

        def dec_first():
            partial_value, inner_made, shift_made, down_made = ffn_backward(
                first_full, kept["ffn_rows"], kept["hidden"], in_proj, down_proj
            )
            return (partial_value, zero_cross, inner_made, shift_made, down_made)

        partial_one, cross_enc, inner_one, inner_shift_one, down_one = lax.cond(
            decoder, dec_first, enc_first
        )
        first_sum = grad_sums(partial_one)
        grad_r3e, gain_ye, shift_ye = norm_back(
            first_sum, kept["norm_y"], kept["factor_y"], gains[2]
        )
        grad_r2, gain_c, shift_c = norm_back(
            alpha * grad_r3d + first_sum, kept["norm_c"], kept["factor_c"], gains[1]
        )
        grad_r3 = jnp.where(decoder, grad_r3d, grad_r3e)
        gain_y = jnp.where(decoder, gain_yd, gain_ye)
        shift_y = jnp.where(decoder, shift_yd, shift_ye)
        middle_grad = jnp.where(decoder, grad_r2, grad_r3e)
        second_full = ffn_grad_rows(middle_grad.astype(jnp.bfloat16))

        def enc_second():
            partial_value, inner_made, shift_made, down_made = ffn_backward(
                second_full, kept["ffn_rows"], kept["hidden"], in_proj, down_proj
            )
            return (
                partial_value,
                inner_made,
                shift_made,
                down_made,
                zero_cross,
                zeros_low((full_rows, 2 * head_cols)),
            )

        def dec_second():
            partial_value, grad_cross_dec, grad_kv_made = cross_back(second_full)
            return (partial_value,) + zero_ffn + (grad_cross_dec, grad_kv_made)

        partial_two, inner_two, inner_shift_two, down_two, cross_dec, grad_kv = lax.cond(
            decoder, dec_second, enc_second
        )
        grad_a = alpha * middle_grad + ffn_grad_sums(partial_two)
        dkv_held = from_behind(grad_kv, "section", -1)
        grad_r1, gain_a, shift_a = norm_back(grad_a, kept["norm_a"], kept["factor_a"], gains[0])
        attn_full = grad_rows(grad_r1.astype(jnp.bfloat16))
        grad_mixed = lax.dot_general(
            attn_full, out_proj, COL_DIMS, preferred_element_type=jnp.float32
        ).astype(jnp.bfloat16)
        grad_outer = lax.dot_general(
            kept["mixed"], attn_full, ROW_DIMS, preferred_element_type=jnp.float32
        )
        qkv_split = kept["qkv"].reshape(seq_count, slots, head_local, 3, HS)
        grad_q, grad_k, grad_v = attend_back(
            to_heads(grad_mixed),
            qkv_split[:, :, :, 0],
            qkv_split[:, :, :, 1],
            qkv_split[:, :, :, 2],
            kept["lse_self"],
            own_len,
            decoder,
        )
        grad_qkv = (
            jnp.stack([grad_q, grad_k, grad_v], axis=3)
            .astype(jnp.bfloat16)
            .reshape(full_rows, 3 * head_cols)
        )
        grad_qkv_proj = lax.dot_general(
            kept["x_rows"], grad_qkv, ROW_DIMS, preferred_element_type=jnp.float32
        )
        grad_x = alpha * grad_r1 + grad_sums(
            lax.dot_general(grad_qkv, qkv_proj, COL_DIMS, preferred_element_type=jnp.float32)
        )
        grad_ticks.append(grad_x)
        gain_step = jnp.stack([gain_a, jnp.where(decoder, gain_c, 0.0), gain_y])
        shift_step = jnp.stack([shift_a, jnp.where(decoder, shift_c, 0.0), shift_y])
        steps = dict(
            qkv=grad_qkv_proj,
            outer=grad_outer,
            cross=cross_enc + cross_dec,
            inner=inner_one + inner_two,
            inner_shift=inner_shift_one + inner_shift_two,
            down=down_one + down_two,
            down_shift=jnp.sum(grad_r3, axis=0),
            gain=gain_step,
            shift=shift_step,
        )
        totals = {name: totals[name] + jnp.where(live, steps[name], 0.0) for name in totals}
    input_grad = lax.dynamic_slice_in_dim(jnp.stack(grad_ticks[::-1]), section, batches, 0)
    inner_total, inner_shift_total, down_total = (
        totals["inner"],
        totals["inner_shift"],
        totals["down"],
    )
    summed = (
        lax.psum(totals["qkv"].astype(jnp.bfloat16), "dp").astype(jnp.float32),
        lax.psum(totals["outer"].astype(jnp.bfloat16), "dp").astype(jnp.float32),
        lax.psum(totals["cross"].astype(jnp.bfloat16), "dp").astype(jnp.float32),
        lax.psum(inner_total.astype(jnp.bfloat16), "dp").astype(jnp.float32),
        lax.psum(inner_shift_total.astype(jnp.bfloat16), "dp").astype(jnp.float32),
        lax.psum(down_total.astype(jnp.bfloat16), "dp").astype(jnp.float32),
    )
    vectors = lax.psum((totals["gain"], totals["shift"], totals["down_shift"]), ("dp", "tensor"))
    return (
        outputs[None],
        input_grad[None],
        summed[0][None],
        summed[1][None],
        summed[2][None],
        summed[3][None],
        summed[4][None],
        summed[5][None],
        vectors[2][None],
        vectors[0][None],
        vectors[1][None],
    )


def solution(mesh):
    placed = (
        P("section", None, ("dp", "tensor"), None),
        P(None, None, "dp"),
        P(None, ("dp", "tensor"), None),
        P("section", None, "tensor"),
        P("section", "tensor", None),
        P("section", None, "tensor"),
        P("section", None, "tensor"),
        P("section", "tensor"),
        P("section", "tensor", None),
        P("section", None),
        P("section", None, None),
        P("section", None, None),
    )
    return jax.shard_map(
        body,
        mesh=mesh,
        in_specs=placed,
        out_specs=(
            P("section", None, ("dp", "tensor"), None),
            P("section", None, ("dp", "tensor"), None),
            P("section", None, "tensor"),
            P("section", "tensor", None),
            P("section", None, "tensor"),
            P("section", None, "tensor"),
            P("section", "tensor"),
            P("section", "tensor", None),
            P("section", None),
            P("section", None, None),
            P("section", None, None),
        ),
        check_vma=False,
    )
```

profile of v0, /device:TPU:9, one launch (start us, length us, event | category | flops | bytes accessed | tf_op | source)
XLA Modules:
  0.0 4643.1 jit_solution(5402405449880307948)
XLA Ops:
  18.5 37.4 all-gather.86.cloned.1.call-done
  125.6 57.5 %reduce-scatter.31.cloned.1.call-done = f32[256,1024]{1,0:T(8,128)} async-done(((f32[1024,1024]{1,0:T(8,128)}), f32[256,1024]{1,0:T(8,128)}) %reduce-scatter.31.cloned.1.call-update) | async-done | bytes 1048592 | tf_op jit(solution)/shard_map/reduce_scatter | solution.py:133
  185.0 78.2 %reduce-scatter.37.cloned.1.call-done = f32[256,1024]{1,0:T(8,128)} async-done(((f32[1024,1024]{1,0:T(8,128)}), f32[256,1024]{1,0:T(8,128)}) %reduce-scatter.37.cloned.1.call-update) | async-done | bytes 1048592 | tf_op jit(solution)/shard_map/reduce_scatter | solution.py:133
  272.2 39.6 all-gather.36.cloned.1.call-done
  329.5 87.6 %reduce-scatter.33.cloned.1.call-done = f32[256,1024]{1,0:T(8,128)} async-done(((f32[1024,1024]{1,0:T(8,128)}), f32[256,1024]{1,0:T(8,128)}) %reduce-scatter.33.cloned.1.call-update) | async-done | bytes 1048592 | tf_op jit(solution)/shard_map/reduce_scatter | solution.py:133
  422.9 40.4 all-gather.90.cloned.1.call-done
  671.8 57.6 %reduce-scatter.43.cloned.1.call-done = f32[256,1024]{1,0:T(8,128)} async-done(((f32[1024,1024]{1,0:T(8,128)}), f32[256,1024]{1,0:T(8,128)}) %reduce-scatter.43.cloned.1.call-update) | async-done | bytes 1048592 | tf_op jit(solution)/shard_map/reduce_scatter | solution.py:133
  732.2 76.8 %reduce-scatter.49.cloned.1.call-done = f32[256,1024]{1,0:T(8,128)} async-done(((f32[1024,1024]{1,0:T(8,128)}), f32[256,1024]{1,0:T(8,128)}) %reduce-scatter.49.cloned.1.call-update) | async-done | bytes 1048592 | tf_op jit(solution)/shard_map/reduce_scatter | solution.py:133
  810.8 77.7 %reduce-scatter.55.cloned.1.call-done = f32[256,1024]{1,0:T(8,128)} async-done(((f32[1024,1024]{1,0:T(8,128)}), f32[256,1024]{1,0:T(8,128)}) %reduce-scatter.55.cloned.1.call-update) | async-done | bytes 1048592 | tf_op jit(solution)/shard_map/reduce_scatter | solution.py:133
  891.4 76.5 %reduce-scatter.39.cloned.1.call-done = f32[256,1024]{1,0:T(8,128)} async-done(((f32[1024,1024]{1,0:T(8,128)}), f32[256,1024]{1,0:T(8,128)}) %reduce-scatter.39.cloned.1.call-update) | async-done | bytes 1048592 | tf_op jit(solution)/shard_map/reduce_scatter | solution.py:133
  975.6 44.1 all-gather.42.cloned.1.call-done
  1082.2 90.7 %reduce-scatter.45.cloned.1.call-done = f32[256,1024]{1,0:T(8,128)} async-done(((f32[1024,1024]{1,0:T(8,128)}), f32[256,1024]{1,0:T(8,128)}) %reduce-scatter.45.cloned.1.call-update) | async-done | bytes 1048592 | tf_op jit(solution)/shard_map/reduce_scatter | solution.py:133
  1177.4 44.1 all-gather.46.cloned.1.call-done
  1312.5 81.0 %reduce-scatter.51.cloned.1.call-done = f32[256,1024]{1,0:T(8,128)} async-done(((f32[1024,1024]{1,0:T(8,128)}), f32[256,1024]{1,0:T(8,128)}) %reduce-scatter.51.cloned.1.call-update) | async-done | bytes 1048592 | tf_op jit(solution)/shard_map/reduce_scatter | solution.py:133
  1406.8 36.1 all-gather.50.cloned.1.call-done
  1534.0 46.1 reduce-scatter.41.cloned.1.call-done
  1580.0 45.9 reduce-scatter.53.cloned.1.call-done
  1625.9 80.9 %reduce-scatter.57.cloned.1.call-done = f32[256,1024]{1,0:T(8,128)} async-done(((f32[1024,1024]{1,0:T(8,128)}), f32[256,1024]{1,0:T(8,128)}) %reduce-scatter.57.cloned.1.call-update) | async-done | bytes 1048592 | tf_op jit(solution)/shard_map/reduce_scatter | solution.py:133
  1712.8 44.6 all-gather.54.cloned.1.call-done
  1906.3 43.6 reduce-scatter.61.cloned.1.call-done
  2007.4 36.2 conditional.31
  2048.7 144.5 %collective-permute-done.5 = bf16[1024,512]{1,0:T(8,128)(2,1)} collective-permute-done((bf16[1024,512]{1,0:T(8,128)(2,1)}, bf16[1024,512]{1,0:T(8,128)(2,1)}, u32[]{:S(2)}, u32[]{:S(2)}) %collective-permute-start.5) | collective-permute-done | bytes 1048608 | tf_op jit(solution)/shard_map/ppermute | solution.py:21
  2207.4 52.3 %reduce-scatter.63.cloned.1.call-done = bf16[256,1024]{1,0:T(8,128)(2,1)} async-done(((bf16[1024,1024]{1,0:T(8,128)(2,1)}), bf16[256,1024]{1,0:T(8,128)(2,1)}) %reduce-scatter.63.cloned.1.call-update) | async-done | bytes 524304 | tf_op jit(solution)/shard_map/reduce_scatter | solution.py:151
  2269.8 42.8 all-gather.62.cloned.1.call-done
  2312.6 36.3 conditional.33
  2358.8 139.8 %collective-permute-done.6 = bf16[1024,512]{1,0:T(8,128)(2,1)} collective-permute-done((bf16[1024,512]{1,0:T(8,128)(2,1)}, bf16[1024,512]{1,0:T(8,128)(2,1)}, u32[]{:S(2)}, u32[]{:S(2)}) %collective-permute-start.6) | collective-permute-done | bytes 1048608 | tf_op jit(solution)/shard_map/ppermute | solution.py:21
  2512.7 50.4 %reduce-scatter.65.cloned.1.call-done = bf16[256,1024]{1,0:T(8,128)(2,1)} async-done(((bf16[1024,1024]{1,0:T(8,128)(2,1)}), bf16[256,1024]{1,0:T(8,128)(2,1)}) %reduce-scatter.65.cloned.1.call-update) | async-done | bytes 524304 | tf_op jit(solution)/shard_map/reduce_scatter | solution.py:151
  2570.8 45.2 all-gather.66.cloned.1.call-done
  2615.9 36.4 conditional.35
  2662.2 139.4 %collective-permute-done.7 = bf16[1024,512]{1,0:T(8,128)(2,1)} collective-permute-done((bf16[1024,512]{1,0:T(8,128)(2,1)}, bf16[1024,512]{1,0:T(8,128)(2,1)}, u32[]{:S(2)}, u32[]{:S(2)}) %collective-permute-start.7) | collective-permute-done | bytes 1048608 | tf_op jit(solution)/shard_map/ppermute | solution.py:21
  2815.9 50.2 %reduce-scatter.67.cloned.1.call-done = bf16[256,1024]{1,0:T(8,128)(2,1)} async-done(((bf16[1024,1024]{1,0:T(8,128)(2,1)}), bf16[256,1024]{1,0:T(8,128)(2,1)}) %reduce-scatter.67.cloned.1.call-update) | async-done | bytes 524304 | tf_op jit(solution)/shard_map/reduce_scatter | solution.py:151
  2874.5 45.6 all-gather.70.cloned.1.call-done
  2920.1 36.3 conditional.37
  2966.2 139.1 %collective-permute-done.8 = bf16[1024,512]{1,0:T(8,128)(2,1)} collective-permute-done((bf16[1024,512]{1,0:T(8,128)(2,1)}, bf16[1024,512]{1,0:T(8,128)(2,1)}, u32[]{:S(2)}, u32[]{:S(2)}) %collective-permute-start.8) | collective-permute-done | bytes 1048608 | tf_op jit(solution)/shard_map/ppermute | solution.py:21
  3122.8 47.7 %reduce-scatter.69.cloned.1.call-done = bf16[256,1024]{1,0:T(8,128)(2,1)} async-done(((bf16[1024,1024]{1,0:T(8,128)(2,1)}), bf16[256,1024]{1,0:T(8,128)(2,1)}) %reduce-scatter.69.cloned.1.call-update) | async-done | bytes 524304 | tf_op jit(solution)/shard_map/reduce_scatter | solution.py:151
  3184.6 43.8 all-gather.74.cloned.1.call-done
  3228.3 41.0 conditional.39
  3288.1 30.0 reduce-scatter.83.cloned.1.call-done
  3318.0 45.3 reduce-scatter.79.cloned.1.call-done
  3363.3 45.5 reduce-scatter.75.cloned.1.call-done
  3408.8 46.1 reduce-scatter.71.cloned.1.call-done
  4308.4 58.0 %all-reduce = (f32[1,1024]{1,0:T(1,128)}, f32[1,3,1024]{2,1,0:T(4,128)S(1)}, f32[1,3,1024]{2,0,1:T(1,128)}) all-reduce(f32[1,1024]{1,0:T(1,128)S(1)} %bitcast.2493, f32[1,3,1024]{2,1,0:T(4,128)S(1)} %fusion.1824, f32[1,3,1024]{2,0,1:T(1,128)S(1)} %broadcast_in_dim.796), channel_id=1, replica_groups=mesh['section'=2,'dp'=4,'tensor'=4] {'dp','tensor'}, use_global_device_ids=true, to_apply=%region_231.232 | all-reduce | flops 7168 | bytes 57344 | tf_op jit(solution)/shard_map/psum | solution.py:538
  4367.0 33.8 all-reduce.4.cloned.1.call-done
  4412.2 33.9 reduce-scatter.73.cloned.1.call-done
  4449.2 42.3 reduce-scatter.77.cloned.1.call-done
  4494.3 42.7 reduce-scatter.81.cloned.1.call-done
  4540.0 42.5 reduce-scatter.85.cloned.1.call-done
  4585.5 42.6 reduce-scatter.89.cloned.1.call-done
  (1687 shorter events, 2194.8 us)
Async XLA Ops:
  11.3 171.8 %reduce-scatter.31.cloned.1.call-start = ((), (), s32[]{:S(2)}) async-start(), calls=%async_computation.30 | async-start | bytes 5242880 | tf_op jit(solution)/shard_map/reduce_scatter | solution.py:133
  77.7 185.5 %reduce-scatter.37.cloned.1.call-start = ((), (), s32[]{:S(2)}) async-start(), calls=%async_computation.35 | async-start | bytes 5242880 | tf_op jit(solution)/shard_map/reduce_scatter | solution.py:133
  124.8 187.0 %all-gather.36.cloned.1.call-start = ((), (), s32[]{:S(2)}) async-start(), calls=%async_computation.31 | async-start | bytes 2621440 | tf_op jit(solution)/shard_map/all_gather | solution.py:129
  267.1 150.1 %reduce-scatter.33.cloned.1.call-start = ((), (), s32[]{:S(2)}) async-start(), calls=%async_computation.32 | async-start | bytes 5242880 | tf_op jit(solution)/shard_map/reduce_scatter | solution.py:133
  327.2 136.2 %all-gather.90.cloned.1.call-start = ((), (), s32[]{:S(2)}) async-start(), calls=%async_computation.87 | async-start | bytes 2621440 | tf_op jit(solution)/shard_map/all_gather | solution.py:129
  328.0 181.7 %all-gather.92.cloned.1.call-start = ((), (), s32[]{:S(2)}) async-start(), calls=%async_computation.88 | async-start | bytes 2621440 | tf_op jit(solution)/shard_map/all_gather | solution.py:129
  328.7 227.9 %all-gather.94.cloned.1.call-start = ((), (), s32[]{:S(2)}) async-start(), calls=%async_computation.89 | async-start | bytes 2621440 | tf_op jit(solution)/shard_map/all_gather | solution.py:129
  329.5 273.9 %all-gather.38.cloned.1.call-start = ((), (), s32[]{:S(2)}) async-start(), calls=%async_computation.33 | async-start | bytes 2621440 | tf_op jit(solution)/shard_map/all_gather | solution.py:137
  421.8 227.9 %all-gather.40.cloned.1.call-start = ((), (), s32[]{:S(2)}) async-start(), calls=%async_computation.36 | async-start | bytes 2621440 | tf_op jit(solution)/shard_map/all_gather | solution.py:129
  478.2 251.2 %reduce-scatter.43.cloned.1.call-start = ((), (), s32[]{:S(2)}) async-start(), calls=%async_computation.40 | async-start | bytes 5242880 | tf_op jit(solution)/shard_map/reduce_scatter | solution.py:133
  491.3 317.7 %reduce-scatter.49.cloned.1.call-start = ((), (), s32[]{:S(2)}) async-start(), calls=%async_computation.45 | async-start | bytes 5242880 | tf_op jit(solution)/shard_map/reduce_scatter | solution.py:133
  530.8 357.8 %reduce-scatter.55.cloned.1.call-start = ((), (), s32[]{:S(2)}) async-start(), calls=%async_computation.50 | async-start | bytes 5242880 | tf_op jit(solution)/shard_map/reduce_scatter | solution.py:133
  577.9 390.1 %reduce-scatter.39.cloned.1.call-start = ((), (), s32[]{:S(2)}) async-start(), calls=%async_computation.37 | async-start | bytes 5242880 | tf_op jit(solution)/shard_map/reduce_scatter | solution.py:133
  671.7 348.0 %all-gather.42.cloned.1.call-start = ((), (), s32[]{:S(2)}) async-start(), calls=%async_computation.38 | async-start | bytes 2621440 | tf_op jit(solution)/shard_map/all_gather | solution.py:137
  975.6 197.3 %reduce-scatter.45.cloned.1.call-start = ((), (), s32[]{:S(2)}) async-start(), calls=%async_computation.42 | async-start | bytes 5242880 | tf_op jit(solution)/shard_map/reduce_scatter | solution.py:133
  1082.2 139.3 %all-gather.46.cloned.1.call-start = ((), (), s32[]{:S(2)}) async-start(), calls=%async_computation.43 | async-start | bytes 2621440 | tf_op jit(solution)/shard_map/all_gather | solution.py:137
  1177.3 135.2 %reduce-scatter.47.cloned.1.call-start = ((), (), s32[]{:S(2)}) async-start(), calls=%async_computation.44 | async-start | bytes 2621440 | tf_op jit(solution)/shard_map/reduce_scatter | solution.py:141
  1234.6 158.9 %reduce-scatter.51.cloned.1.call-start = ((), (), s32[]{:S(2)}) async-start(), calls=%async_computation.47 | async-start | bytes 5242880 | tf_op jit(solution)/shard_map/reduce_scatter | solution.py:133
  1289.3 153.7 %all-gather.50.cloned.1.call-start = ((), (), s32[]{:S(2)}) async-start(), calls=%async_computation.48 | async-start | bytes 2621440 | tf_op jit(solution)/shard_map/all_gather | solution.py:137
  1398.9 135.1 %reduce-scatter.35.cloned.1.call-start = ((), (), s32[]{:S(2)}) async-start(), calls=%async_computation.34 | async-start | bytes 2621440 | tf_op jit(solution)/shard_map/reduce_scatter | solution.py:141
  1402.8 177.3 %reduce-scatter.41.cloned.1.call-start = ((), (), s32[]{:S(2)}) async-start(), calls=%async_computation.39 | async-start | bytes 2621440 | tf_op jit(solution)/shard_map/reduce_scatter | solution.py:141
  1406.8 219.1 %reduce-scatter.53.cloned.1.call-start = ((), (), s32[]{:S(2)}) async-start(), calls=%async_computation.49 | async-start | bytes 2621440 | tf_op jit(solution)/shard_map/reduce_scatter | solution.py:141
  1456.0 250.9 %reduce-scatter.57.cloned.1.call-start = ((), (), s32[]{:S(2)}) async-start(), calls=%async_computation.52 | async-start | bytes 5242880 | tf_op jit(solution)/shard_map/reduce_scatter | solution.py:133
  1505.0 252.4 %all-gather.54.cloned.1.call-start = ((), (), s32[]{:S(2)}) async-start(), calls=%async_computation.53 | async-start | bytes 2621440 | tf_op jit(solution)/shard_map/all_gather | solution.py:137
  1835.3 114.5 %reduce-scatter.61.cloned.1.call-start = ((), (), s32[]{:S(2)}) async-start(), calls=%async_computation.56 | async-start | bytes 2621440 | tf_op jit(solution)/shard_map/reduce_scatter | solution.py:151
  1971.0 288.7 %reduce-scatter.63.cloned.1.call-start = ((), (), s32[]{:S(2)}) async-start(), calls=%async_computation.59 | async-start | bytes 2621440 | tf_op jit(solution)/shard_map/reduce_scatter | solution.py:151
  2046.0 147.2 %collective-permute-start.5 = (bf16[1024,512]{1,0:T(8,128)(2,1)}, bf16[1024,512]{1,0:T(8,128)(2,1)}, u32[]{:S(2)}, u32[]{:S(2)}) collective-permute-start(bf16[1024,512]{1,0:T(8,128)(2,1)} %copy.136), channel_id=1, source_target_pairs={{16,0},{17,1},{18,2},{19,3},{20,4},{21,5},{22,6},{23,7},{24,8},{25... | collective-permute-start | bytes 3145736 | tf_op jit(solution)/shard_map/ppermute | solution.py:21
  2269.8 293.4 %reduce-scatter.65.cloned.1.call-start = ((), (), s32[]{:S(2)}) async-start(), calls=%async_computation.62 | async-start | bytes 2621440 | tf_op jit(solution)/shard_map/reduce_scatter | solution.py:151
  2351.2 147.3 %collective-permute-start.6 = (bf16[1024,512]{1,0:T(8,128)(2,1)}, bf16[1024,512]{1,0:T(8,128)(2,1)}, u32[]{:S(2)}, u32[]{:S(2)}) collective-permute-start(bf16[1024,512]{1,0:T(8,128)(2,1)} %copy.139), channel_id=1, source_target_pairs={{16,0},{17,1},{18,2},{19,3},{20,4},{21,5},{22,6},{23,7},{24,8},{25... | collective-permute-start | bytes 3145736 | tf_op jit(solution)/shard_map/ppermute | solution.py:21
  2570.7 295.4 %reduce-scatter.67.cloned.1.call-start = ((), (), s32[]{:S(2)}) async-start(), calls=%async_computation.65 | async-start | bytes 2621440 | tf_op jit(solution)/shard_map/reduce_scatter | solution.py:151
  2654.6 147.0 %collective-permute-start.7 = (bf16[1024,512]{1,0:T(8,128)(2,1)}, bf16[1024,512]{1,0:T(8,128)(2,1)}, u32[]{:S(2)}, u32[]{:S(2)}) collective-permute-start(bf16[1024,512]{1,0:T(8,128)(2,1)} %copy.142), channel_id=1, source_target_pairs={{16,0},{17,1},{18,2},{19,3},{20,4},{21,5},{22,6},{23,7},{24,8},{25... | collective-permute-start | bytes 3145736 | tf_op jit(solution)/shard_map/ppermute | solution.py:21
  2874.4 296.1 %reduce-scatter.69.cloned.1.call-start = ((), (), s32[]{:S(2)}) async-start(), calls=%async_computation.68 | async-start | bytes 2621440 | tf_op jit(solution)/shard_map/reduce_scatter | solution.py:151
  2958.7 146.6 %collective-permute-start.8 = (bf16[1024,512]{1,0:T(8,128)(2,1)}, bf16[1024,512]{1,0:T(8,128)(2,1)}, u32[]{:S(2)}, u32[]{:S(2)}) collective-permute-start(bf16[1024,512]{1,0:T(8,128)(2,1)} %copy.145), channel_id=1, source_target_pairs={{16,0},{17,1},{18,2},{19,3},{20,4},{21,5},{22,6},{23,7},{24,8},{25... | collective-permute-start | bytes 3145736 | tf_op jit(solution)/shard_map/ppermute | solution.py:21
  3182.4 135.6 %reduce-scatter.83.cloned.1.call-start = ((), (), s32[]{:S(2)}) async-start(), calls=%async_computation.79 | async-start | bytes 2621440 | tf_op jit(solution)/shard_map/reduce_scatter | solution.py:161
  3183.0 180.4 %reduce-scatter.79.cloned.1.call-start = ((), (), s32[]{:S(2)}) async-start(), calls=%async_computation.76 | async-start | bytes 2621440 | tf_op jit(solution)/shard_map/reduce_scatter | solution.py:161
  3183.5 225.2 %reduce-scatter.75.cloned.1.call-start = ((), (), s32[]{:S(2)}) async-start(), calls=%async_computation.73 | async-start | bytes 2621440 | tf_op jit(solution)/shard_map/reduce_scatter | solution.py:161
  3184.1 270.7 %reduce-scatter.71.cloned.1.call-start = ((), (), s32[]{:S(2)}) async-start(), calls=%async_computation.70 | async-start | bytes 2621440 | tf_op jit(solution)/shard_map/reduce_scatter | solution.py:161
  3269.4 336.1 %all-gather.84.cloned.1.call-start = ((), (), s32[]{:S(2)}) async-start(), calls=%async_computation.83 | async-start | bytes 2621440 | tf_op jit(solution)/shard_map/all_gather | solution.py:147
  3467.3 147.0 %all-gather.82.cloned.1.call-start = ((), (), s32[]{:S(2)}) async-start(), calls=%async_computation.80 | async-start | bytes 2621440 | tf_op jit(solution)/shard_map/all_gather | solution.py:147
  3479.8 143.4 %all-gather.80.cloned.1.call-start = ((), (), s32[]{:S(2)}) async-start(), calls=%async_computation.77 | async-start | bytes 2621440 | tf_op jit(solution)/shard_map/all_gather | solution.py:147
  3509.6 142.5 %all-gather.76.cloned.1.call-start = ((), (), s32[]{:S(2)}) async-start(), calls=%async_computation.71 | async-start | bytes 2621440 | tf_op jit(solution)/shard_map/all_gather | solution.py:147
  3571.9 301.0 %all-gather.78.cloned.1.call-start = ((), (), s32[]{:S(2)}) async-start(), calls=%async_computation.74 | async-start | bytes 2621440 | tf_op jit(solution)/shard_map/all_gather | solution.py:147
  3605.5 795.4 %all-reduce.4.cloned.1.call-start = ((), (), s32[]{:S(2)}) async-start(), calls=%async_computation.90 | async-start | bytes 14680064 | tf_op jit(solution)/shard_map/psum | solution.py:531
  4262.7 183.4 %reduce-scatter.73.cloned.1.call-start = ((), (), s32[]{:S(2)}) async-start(), calls=%async_computation.72 | async-start | bytes 2621440 | tf_op jit(solution)/shard_map/reduce_scatter | solution.py:151
  4267.3 224.2 %reduce-scatter.77.cloned.1.call-start = ((), (), s32[]{:S(2)}) async-start(), calls=%async_computation.75 | async-start | bytes 2621440 | tf_op jit(solution)/shard_map/reduce_scatter | solution.py:151
  4272.0 265.0 %reduce-scatter.81.cloned.1.call-start = ((), (), s32[]{:S(2)}) async-start(), calls=%async_computation.78 | async-start | bytes 2621440 | tf_op jit(solution)/shard_map/reduce_scatter | solution.py:151
  4276.9 305.6 %reduce-scatter.85.cloned.1.call-start = ((), (), s32[]{:S(2)}) async-start(), calls=%async_computation.81 | async-start | bytes 2621440 | tf_op jit(solution)/shard_map/reduce_scatter | solution.py:151
  4280.3 347.8 %reduce-scatter.89.cloned.1.call-start = ((), (), s32[]{:S(2)}) async-start(), calls=%async_computation.84 | async-start | bytes 2621440 | tf_op jit(solution)/shard_map/reduce_scatter | solution.py:151
  (511 other events, 23556.8 us)
Sparse Core Ops, SparseCore 0:
  10.7 45.2 all-gather.85
  58.1 44.6 all-gather.87
  105.7 77.3 reduce-scatter.30
  185.9 77.2 reduce-scatter.36
  267.2 44.5 all-gather.35
  327.3 89.7 reduce-scatter.32
  418.8 44.5 all-gather.89
  465.0 44.6 all-gather.91
  511.9 44.6 all-gather.93
  558.7 44.6 all-gather.37
  605.0 44.6 all-gather.39
  651.9 77.3 reduce-scatter.42
  731.7 77.2 reduce-scatter.48
  811.2 77.2 reduce-scatter.54
  890.7 77.2 reduce-scatter.38
  975.1 44.5 all-gather.41
  1021.8 44.6 all-gather.43
  1082.3 90.5 reduce-scatter.44
  1176.9 44.5 all-gather.45
  1222.8 44.6 all-gather.47
  1314.9 78.5 reduce-scatter.50
  1398.4 44.5 all-gather.49
  1444.4 44.5 all-gather.51
  1628.3 78.5 reduce-scatter.56
  1712.8 44.5 all-gather.53
  1770.5 47.4 reduce-scatter.58
  1835.5 45.8 all-gather.55
  1905.7 44.1 reduce-scatter.60
  1956.6 45.7 all-gather.57
  2004.0 44.6 all-gather.59
  2207.5 52.2 reduce-scatter.62
  2266.8 45.7 all-gather.61
  2314.1 44.6 all-gather.63
  2512.8 50.3 reduce-scatter.64
  2570.1 45.7 all-gather.65
  2617.5 44.6 all-gather.67
  2816.0 50.1 reduce-scatter.66
  2873.9 46.0 all-gather.69
  2921.6 44.6 all-gather.71
  3120.1 50.3 reduce-scatter.68
  3181.9 46.3 all-gather.73
  3467.4 45.7 all-gather.83
  3514.8 44.6 all-gather.81
  3561.0 44.6 all-gather.79
  3607.4 44.6 all-gather.75
  3653.7 44.6 all-gather.77
  4262.8 137.9 all-reduce.3
  4539.3 43.1 reduce-scatter.84
  (13 shorter events, 556.2 us)
where the time goes:
time: 4660 us; the launch traced here: 4640 us
  waiting for transfers between devices  2840 us (61%)
  matrix products  1020 us (22%)
  other arithmetic  316 us (7%)
  local copies, waits for them, and re-layouts  273 us (6%)
  blocking collectives  64.2 us (1%)
  starting transfers between devices  53.5 us (1%)
  loops' own time  48.2 us (1%)
    reduce_scatter x10, waiting for transfers between devices, sum_rows(): lax.psum_scatter(partial_value, 'tensor', scatter_dimension=0, tiled=True)  765 us
    ppermute x9, waiting for transfers between devices, from_behind(): return lax.ppermute(block, axis, route)  574 us
    reduce_scatter x10, waiting for transfers between devices, grad_sums(): lax.psum_scatter(partial_value.astype(jnp.bfloat16), 'tensor', scatter_di...  448 us
    all_gather x10, waiting for transfers between devices, gather_rows(): return lax.all_gather(shard, 'tensor', axis=0, tiled=True)  276 us
    dot_general x10, matrix products, attend_back(): jnp.einsum('bhqk,bqhe->bkhe', grad_raw, query_part, preferred_element_typ...  243 us
    dot_general x10, matrix products, attend_back(): jnp.einsum('bhqk,bkhe->bqhe', grad_raw, keys_in, preferred_element_type=j...  232 us
    all_gather x5, waiting for transfers between devices, ffn_input_rows(): return lax.all_gather(shard, 'tensor', axis=0, tiled=True)  194 us
    all_gather x5, waiting for transfers between devices, ffn_grad_rows(): return lax.all_gather(shard, 'tensor', axis=0, tiled=True)  177 us
  transfers between devices with their start and end apart: 70, of which 59 were waited for; matrix products, arithmetic and copies ran while one was open for 21% of the time, Pallas kernels for 0%

commit v1 on v0

--- a/solution.py
+++ b/solution.py
@@ -1,6 +1,8 @@
 import jax
 import jax.numpy as jnp
 from jax import lax
+from jax.experimental import pallas as pl
+from jax.experimental.pallas import tpu as pltpu
 from jax.sharding import PartitionSpec as P
 
 HS = 64
@@ -13,6 +15,10 @@
 NEG = -1e30
 ROW_DIMS = (((0,), (0,)), ((), ()))
 COL_DIMS = (((1,), (1,)), ((), ()))
+LANES = 2 * HS
+ROWS = 256
+SCALE = HS ** (-0.5)
+GELU_C = (2.0 / 3.141592653589793) ** 0.5
 
 
 def from_behind(block, axis, distance):
@@ -551,6 +557,595 @@
     )
 
 
+def split_lanes(rows):
+    return lax.broadcasted_iota(jnp.int32, (rows, 2 * HS), 1) < HS
+
+
+def swap_halves(tile):
+    return jnp.concatenate([tile[:, HS:], tile[:, :HS]], axis=1)
+
+
+def pair_of(packed, left):
+    first, second, third = (packed[:, :LANES], packed[:, LANES : 2 * LANES], packed[:, 2 * LANES :])
+    queries = jnp.where(left, first, second)
+    keys_in = jnp.where(left, swap_halves(first), swap_halves(third))
+    values = jnp.where(left, second, third)
+    return (queries, keys_in, values)
+
+
+def key_limit(position, length, causal):
+    return jnp.minimum(length, jnp.where(causal != 0, position + 1, position.dtype.type(1 << 20)))
+
+
+def attend_pair(scalars, queries_at, keys_in, values, mixed_ref, lse_ref, slots, left):
+    length, causal = (scalars[0], scalars[1])
+    zero = jnp.zeros((), keys_in.dtype)
+    key_halves = (jnp.where(left, keys_in, zero), jnp.where(left, zero, keys_in))
+    value_halves = (jnp.where(left, values, zero), jnp.where(left, zero, values))
+    left_block = split_lanes(ROWS)
+    key_pos = lax.broadcasted_iota(jnp.int32, (ROWS, slots), 1)
+
+    def block(index, carry):
+        first_row = pl.multiple_of(index * ROWS, ROWS)
+        queries = queries_at(first_row)
+        position = first_row + lax.broadcasted_iota(jnp.int32, (ROWS, 1), 0)
+        allowed = key_pos < key_limit(position, length, causal)
+        total, tops, sums = (None, [], [])
+        for half in range(2):
+            raw = lax.dot_general(
+                queries, key_halves[half], COL_DIMS, preferred_element_type=jnp.float32
+            )
+            scores = jnp.where(allowed, raw * SCALE, NEG)
+            top = jnp.max(scores, axis=1, keepdims=True)
+            expo = jnp.exp(scores - top)
+            tops.append(top)
+            sums.append(jnp.sum(expo, axis=1, keepdims=True))
+            part = jnp.dot(
+                expo.astype(jnp.bfloat16), value_halves[half], preferred_element_type=jnp.float32
+            )
+            total = part if half == 0 else total + part
+        norm = jnp.where(left_block, sums[0], sums[1])
+        mixed_ref[pl.ds(first_row, ROWS), :] = (total / norm).astype(jnp.bfloat16)
+        logs = jnp.where(left_block, tops[0] + jnp.log(sums[0]), tops[1] + jnp.log(sums[1]))
+        lse_ref[0, :, pl.ds(first_row, ROWS)] = jnp.transpose(logs)[HS - 4 : HS + 4]
+        return carry
+
+    lax.fori_loop(0, slots // ROWS, block, 0)
+
+
+def self_forward_kernel(scalars, packed_ref, mixed_ref, lse_ref, queries_ref):
+    slots = packed_ref.shape[0]
+    left = split_lanes(slots)
+    queries, keys_in, values = pair_of(packed_ref[...], left)
+    queries_ref[...] = queries
+    attend_pair(
+        scalars,
+        lambda row: queries_ref[pl.ds(row, ROWS), :],
+        keys_in,
+        values,
+        mixed_ref,
+        lse_ref,
+        slots,
+        left,
+    )
+
+
+def cross_forward_kernel(scalars, query_ref, key_ref, value_ref, mixed_ref, lse_ref):
+    slots = query_ref.shape[0]
+    attend_pair(
+        scalars,
+        lambda row: query_ref[pl.ds(row, ROWS), :],
+        key_ref[...],
+        value_ref[...],
+        mixed_ref,
+        lse_ref,
+        slots,
+        split_lanes(slots),
+    )
+
+
+def attend_pair_back(
+    scalars, queries_at, keys_in, values, mixed_ref, grad_ref, lse_ref, put_query, key_acc, value_acc
+):
+    length, causal = (scalars[0], scalars[1])
+    slots = keys_in.shape[0]
+    left = split_lanes(slots)
+    left_block = split_lanes(ROWS)
+    zero = jnp.zeros((), keys_in.dtype)
+    key_halves = (jnp.where(left, keys_in, zero), jnp.where(left, zero, keys_in))
+    value_halves = (jnp.where(left, values, zero), jnp.where(left, zero, values))
+    key_pos = lax.broadcasted_iota(jnp.int32, (slots, ROWS), 0)
+    key_acc[...] = jnp.zeros_like(key_acc)
+    value_acc[...] = jnp.zeros_like(value_acc)
+
+    def block(index, carry):
+        first_row = pl.multiple_of(index * ROWS, ROWS)
+        queries = queries_at(first_row)
+        grads = grad_ref[pl.ds(first_row, ROWS), :]
+        mixed = mixed_ref[pl.ds(first_row, ROWS), :]
+        product = jnp.transpose(grads.astype(jnp.float32) * mixed.astype(jnp.float32))
+        position = first_row + lax.broadcasted_iota(jnp.int32, (1, ROWS), 1)
+        allowed = key_pos < key_limit(position, length, causal)
+        logs = lse_ref[0, :, pl.ds(first_row, ROWS)]
+        query_total = None
+        for half in range(2):
+            mine = left_block if half == 0 else jnp.logical_not(left_block)
+            query_half = jnp.where(mine, queries, zero)
+            grad_half = jnp.where(mine, grads, zero)
+            raw = lax.dot_general(
+                key_halves[half], queries, COL_DIMS, preferred_element_type=jnp.float32
+            )
+            scores = jnp.where(allowed, raw * SCALE, NEG)
+            probs = jnp.exp(scores - logs[3 + half : 4 + half])
+            grad_probs = lax.dot_general(
+                value_halves[half], grads, COL_DIMS, preferred_element_type=jnp.float32
+            )
+            delta = jnp.sum(product[half * HS : half * HS + HS], axis=0, keepdims=True)
+            grad_raw = (probs * (grad_probs - delta) * SCALE).astype(jnp.bfloat16)
+            value_acc[...] += jnp.dot(
+                probs.astype(jnp.bfloat16), grad_half, preferred_element_type=jnp.float32
+            )
+            key_acc[...] += jnp.dot(grad_raw, query_half, preferred_element_type=jnp.float32)
+            part = lax.dot_general(
+                grad_raw, key_halves[half], ROW_DIMS, preferred_element_type=jnp.float32
+            )
+            query_total = part if half == 0 else query_total + part
+        put_query(first_row, query_total.astype(jnp.bfloat16))
+        return carry
+
+    lax.fori_loop(0, slots // ROWS, block, 0)
+
+
+def self_backward_kernel(
+    scalars, packed_ref, mixed_ref, grad_ref, lse_ref, out_ref, queries_ref, dq_ref, key_acc, value_acc
+):
+    slots = packed_ref.shape[0]
+    left = split_lanes(slots)
+    queries, keys_in, values = pair_of(packed_ref[...], left)
+    queries_ref[...] = queries
+
+    def put_query(row, block):
+        dq_ref[pl.ds(row, ROWS), :] = block
+
+    attend_pair_back(
+        scalars,
+        lambda row: queries_ref[pl.ds(row, ROWS), :],
+        keys_in,
+        values,
+        mixed_ref,
+        grad_ref,
+        lse_ref,
+        put_query,
+        key_acc,
+        value_acc,
+    )
+    grad_query = dq_ref[...]
+    grad_key = swap_halves(key_acc[...].astype(jnp.bfloat16))
+    grad_value = value_acc[...].astype(jnp.bfloat16)
+    out_ref[:, :LANES] = jnp.where(left, grad_query, grad_key)
+    out_ref[:, LANES : 2 * LANES] = jnp.where(left, grad_value, grad_query)
+    out_ref[:, 2 * LANES :] = jnp.where(left, grad_key, grad_value)
+
+
+def cross_backward_kernel(
+    scalars,
+    query_ref,
+    key_ref,
+    value_ref,
+    mixed_ref,
+    grad_ref,
+    lse_ref,
+    dq_ref,
+    dk_ref,
+    dv_ref,
+    key_acc,
+    value_acc,
+):
+    def put_query(row, block):
+        dq_ref[pl.ds(row, ROWS), :] = block
+
+    attend_pair_back(
+        scalars,
+        lambda row: query_ref[pl.ds(row, ROWS), :],
+        key_ref[...],
+        value_ref[...],
+        mixed_ref,
+        grad_ref,
+        lse_ref,
+        put_query,
+        key_acc,
+        value_acc,
+    )
+    dk_ref[...] = key_acc[...].astype(jnp.bfloat16)
+    dv_ref[...] = value_acc[...].astype(jnp.bfloat16)
+
+
+def head_call(kernel, scalars, arrays, widths, out_widths, scratch, lse_in, lse_out):
+    slots = arrays[0].shape[0]
+    pairs = arrays[0].shape[1] // widths[0]
+
+    def spec(width):
+        return pl.BlockSpec((slots, width), lambda pair, *_: (0, pair))
+
+    lse_spec = pl.BlockSpec((1, 8, slots), lambda pair, *_: (pair, 0, 0))
+    in_specs = [spec(width) for width in widths]
+    operands = list(arrays)
+    if lse_in is not None:
+        in_specs.append(lse_spec)
+        operands.append(lse_in)
+    out_specs = [spec(width) for width in out_widths]
+    out_shape = [
+        jax.ShapeDtypeStruct((slots, pairs * width), jnp.bfloat16) for width in out_widths
+    ]
+    if lse_out:
+        out_specs.append(lse_spec)
+        out_shape.append(jax.ShapeDtypeStruct((pairs, 8, slots), jnp.float32))
+    products = 7 if lse_in is None else 17
+    return pl.pallas_call(
+        kernel,
+        grid_spec=pltpu.PrefetchScalarGridSpec(
+            num_scalar_prefetch=1,
+            grid=(pairs,),
+            in_specs=in_specs,
+            out_specs=out_specs,
+            scratch_shapes=scratch,
+        ),
+        out_shape=out_shape,
+        compiler_params=pltpu.CompilerParams(
+            dimension_semantics=("arbitrary",), vmem_limit_bytes=48 * 1024 * 1024
+        ),
+        cost_estimate=pl.CostEstimate(
+            flops=products * pairs * slots * slots * LANES * 8,
+            bytes_accessed=sum(a.size * 2 for a in arrays) * 2,
+            transcendentals=2 * pairs * slots * slots,
+        ),
+    )(scalars, *operands)
+
+
+def self_attention(scalars, packed):
+    slots = packed.shape[0]
+    return head_call(
+        self_forward_kernel,
+        scalars,
+        [packed],
+        [3 * LANES],
+        [LANES],
+        [pltpu.VMEM((slots, LANES), jnp.bfloat16)],
+        None,
+        True,
+    )
+
+
+def cross_attention(scalars, queries, keys_in, values):
+    return head_call(
+        cross_forward_kernel, scalars, [queries, keys_in, values], [LANES] * 3, [LANES], [], None, True
+    )
+
+
+def self_attention_back(scalars, packed, mixed, grads, lse):
+    slots = packed.shape[0]
+    return head_call(
+        self_backward_kernel,
+        scalars,
+        [packed, mixed, grads],
+        [3 * LANES, LANES, LANES],
+        [3 * LANES],
+        [
+            pltpu.VMEM((slots, LANES), jnp.bfloat16),
+            pltpu.VMEM((slots, LANES), jnp.bfloat16),
+            pltpu.VMEM((slots, LANES), jnp.float32),
+            pltpu.VMEM((slots, LANES), jnp.float32),
+        ],
+        lse,
+        False,
+    )[0]
+
+
+def cross_attention_back(scalars, queries, keys_in, values, mixed, grads, lse):
+    slots = queries.shape[0]
+    return head_call(
+        cross_backward_kernel,
+        scalars,
+        [queries, keys_in, values, mixed, grads],
+        [LANES] * 5,
+        [LANES] * 3,
+        [pltpu.VMEM((slots, LANES), jnp.float32), pltpu.VMEM((slots, LANES), jnp.float32)],
+        lse,
+        False,
+    )
+
+
+def rows_nt(rows, weight_rows):
+    return lax.dot_general(rows, weight_rows, COL_DIMS, preferred_element_type=jnp.float32)
+
+
+def rows_nn(rows, weight_rows):
+    return jnp.dot(rows, weight_rows, preferred_element_type=jnp.float32)
+
+
+def rows_tn(left_rows, right_rows):
+    return lax.dot_general(left_rows, right_rows, ROW_DIMS, preferred_element_type=jnp.float32)
+
+
+def gelu_slope(values):
+    inner = GELU_C * (values + 0.044715 * values * values * values)
+    bend = jnp.tanh(inner)
+    rise = GELU_C * (1.0 + 3 * 0.044715 * values * values)
+    return 0.5 * (1.0 + bend) + 0.5 * values * (1.0 - bend * bend) * rise
+
+
+def low(values):
+    return values.astype(jnp.bfloat16)
+
+
+def sequence_body(
+    inputs,
+    lengths,
+    cotangent,
+    qkv_weight,
+    attn_out_weight,
+    cross_weight,
+    ffn_in_weight,
+    ffn_in_bias,
+    ffn_out_weight,
+    ffn_out_bias,
+    norm_gain,
+    norm_bias,
+):
+    section = lax.axis_index("section")
+    tensor_index = lax.axis_index("tensor")
+    unit = lax.axis_index("dp")
+    units = lax.axis_size("dp")
+    decoder = section == 1
+    alpha = jnp.where(decoder, ALPHA_DEC, ALPHA_ENC).astype(jnp.float32)
+    batches, shard_rows, width = (inputs.shape[1], inputs.shape[2], inputs.shape[3])
+    slots = batches * shard_rows
+    gains = norm_gain[0].astype(jnp.float32)
+    shifts = norm_bias[0].astype(jnp.float32)
+    down_shift = ffn_out_bias[0].astype(jnp.float32)
+    everyone = ("dp", "tensor")
+
+    def own_unit(array, axis):
+        size = array.shape[axis] // units
+        return lax.dynamic_slice_in_dim(array, unit * size, size, axis)
+
+    def gathered(rows):
+        return lax.all_gather(rows, everyone, axis=0, tiled=True)
+
+    def to_sequence(shards):
+        return lax.all_to_all(shards, "tensor", 0, 0, tiled=True).reshape(slots, width)
+
+    def to_shards(rows):
+        return lax.all_to_all(
+            rows.reshape(batches, shard_rows, width), "tensor", 0, 0, tiled=True
+        )
+
+    x = to_sequence(inputs[0])
+    head_units = cross_weight.shape[2] // (2 * HS) // units
+    qkv_rows = gathered(own_unit(qkv_weight[0], 1).T)
+    out_rows = gathered(own_unit(attn_out_weight[0], 0))
+    cross_unit = own_unit(cross_weight[0], 1).T.reshape(head_units, 2, HS, width)
+    cross_first = gathered(cross_unit[:, 0].reshape(head_units * HS, width))
+    cross_second = gathered(cross_unit[:, 1].reshape(head_units * HS, width))
+    in_rows = gathered(own_unit(ffn_in_weight[0], 1).T)
+    down_rows = gathered(own_unit(ffn_out_weight[0], 0))
+    in_shift = gathered(own_unit(ffn_in_bias[0], 0)[None]).reshape(-1).astype(jnp.float32)
+
+    source_len = lax.dynamic_index_in_dim(lengths[0, :, 0], tensor_index, 0, keepdims=False)
+    target_len = lax.dynamic_index_in_dim(lengths[1, :, 0], tensor_index, 0, keepdims=False)
+    own_len = jnp.where(decoder, target_len, source_len)
+    self_scalars = jnp.stack([own_len, decoder.astype(jnp.int32)])
+    cross_scalars = jnp.stack([source_len, jnp.zeros_like(source_len)])
+
+    qkv = low(rows_nt(x, qkv_rows))
+    mixed, lse_self = self_attention(self_scalars, qkv)
+    resid_a, norm_a, factor_a = layer_norm(
+        alpha * x.astype(jnp.float32) + rows_nn(mixed, out_rows), gains[0], shifts[0]
+    )
+    a_low = low(resid_a)
+
+    wide = jnp.bfloat16
+    square = jnp.zeros((slots, width), wide)
+
+    query_sent = lax.cond(decoder, lambda: low(rows_nt(a_low, cross_first)), lambda: square)
+    query_held = lax.ppermute(query_sent, "section", [(1, 0)])
+
+    def feed(rows_low, rows_wide, gain_row, shift_row):
+        pre_act = rows_nt(rows_low, in_rows) + in_shift
+        hidden = low(jax.nn.gelu(pre_act))
+        made = layer_norm(
+            alpha * rows_wide + rows_nn(hidden, down_rows) + down_shift, gain_row, shift_row
+        )
+        return (pre_act, hidden) + made
+
+    def feed_back(grad_sum, pre_act):
+        grad_low = low(grad_sum)
+        grad_pre = low(rows_nt(grad_low, down_rows) * gelu_slope(pre_act))
+        return (grad_low, grad_pre, alpha * grad_sum + rows_nn(grad_pre, in_rows))
+
+    def enc_feed():
+        pre_act, hidden, memory, norm_y, factor_y = feed(a_low, resid_a, gains[2], shifts[2])
+        memory_low = low(memory)
+        keys_in = low(rows_nt(memory_low, cross_first))
+        values = low(rows_nt(memory_low, cross_second))
+        mixed_c, lse_c = cross_attention(cross_scalars, query_held, keys_in, values)
+        return (pre_act, hidden, memory_low, norm_y, factor_y, keys_in, values, mixed_c, lse_c)
+
+    def no_feed():
+        shapes = jax.eval_shape(enc_feed)
+        return jax.tree.map(lambda leaf: jnp.zeros(leaf.shape, leaf.dtype), shapes)
+
+    pre_e, hidden_e, memory_low, norm_e, factor_e, keys_in, values, mixed_c, lse_c = lax.cond(
+        decoder, no_feed, enc_feed
+    )
+    mixed_held = lax.ppermute(mixed_c, "section", [(0, 1)])
+
+    own_pos = lax.broadcasted_iota(jnp.int32, (slots, 1), 0)
+    cotangent_rows = to_sequence(cotangent)
+
+    def dec_middle():
+        resid_c, norm_c, factor_c = layer_norm(
+            alpha * resid_a + rows_nn(mixed_held, cross_second), gains[1], shifts[1]
+        )
+        c_low = low(resid_c)
+        pre_act, hidden, decoded, norm_y, factor_y = feed(c_low, resid_c, gains[2], shifts[2])
+        grad_top = jnp.where(own_pos < target_len, cotangent_rows.astype(jnp.float32), 0.0)
+        grad_y, gain_y, shift_y = norm_back(grad_top, norm_y, factor_y, gains[2])
+        grad_low, grad_pre, grad_c = feed_back(grad_y, pre_act)
+        grad_mid, gain_c, shift_c = norm_back(grad_c, norm_c, factor_c, gains[1])
+        mid_low = low(grad_mid)
+        grad_mixed_c = low(rows_nt(mid_low, cross_second))
+        return (
+            low(decoded),
+            hidden,
+            c_low,
+            grad_low,
+            grad_pre,
+            grad_mid,
+            mid_low,
+            grad_mixed_c,
+            (gain_c, gain_y),
+            (shift_c, shift_y),
+            jnp.sum(grad_y, axis=0),
+        )
+
+    def no_middle():
+        shapes = jax.eval_shape(dec_middle)
+        return jax.tree.map(lambda leaf: jnp.zeros(leaf.shape, leaf.dtype), shapes)
+
+    (
+        decoded_low,
+        hidden_d,
+        c_low,
+        grad_low_d,
+        grad_pre_d,
+        grad_mid,
+        mid_low,
+        grad_mixed_c,
+        gains_d,
+        shifts_d,
+        down_shift_d,
+    ) = lax.cond(decoder, dec_middle, no_middle)
+    grad_mixed_held = lax.ppermute(grad_mixed_c, "section", [(1, 0)])
+    outputs = to_shards(jnp.where(decoder, decoded_low, memory_low))
+
+    def enc_cross():
+        return tuple(
+            cross_attention_back(
+                cross_scalars, query_held, keys_in, values, mixed_c, grad_mixed_held, lse_c
+            )
+        )
+
+    def no_cross():
+        return (square, square, square)
+
+    grad_query, grad_key, grad_value = lax.cond(decoder, no_cross, enc_cross)
+    grad_query_held = lax.ppermute(grad_query, "section", [(0, 1)])
+
+    def enc_back():
+        grad_memory = rows_nn(grad_key, cross_first) + rows_nn(grad_value, cross_second)
+        grad_y, gain_y, shift_y = norm_back(grad_memory, norm_e, factor_e, gains[2])
+        grad_low, grad_pre, grad_a = feed_back(grad_y, pre_e)
+        zero_row = jnp.zeros_like(gain_y)
+        return (
+            grad_low,
+            grad_pre,
+            hidden_e,
+            a_low,
+            grad_a,
+            (zero_row, gain_y),
+            (zero_row, shift_y),
+            jnp.sum(grad_y, axis=0),
+            grad_key,
+            memory_low,
+            grad_value,
+            memory_low,
+        )
+
+    def dec_back():
+        grad_a = alpha * grad_mid + rows_nn(grad_query_held, cross_first)
+        return (
+            grad_low_d,
+            grad_pre_d,
+            hidden_d,
+            c_low,
+            grad_a,
+            gains_d,
+            shifts_d,
+            down_shift_d,
+            grad_query_held,
+            a_low,
+            mixed_held,
+            mid_low,
+        )
+
+    (
+        grad_low,
+        grad_pre,
+        hidden,
+        feed_rows,
+        grad_a,
+        gain_cy,
+        shift_cy,
+        down_shift_step,
+        first_left,
+        first_right,
+        second_left,
+        second_right,
+    ) = lax.cond(decoder, dec_back, enc_back)
+
+    def summed(grad_rows_all, block):
+        scattered = lax.psum_scatter(
+            low(grad_rows_all), everyone, scatter_dimension=0, tiled=True
+        )
+        return lax.all_gather(scattered, "dp", axis=0, tiled=True).astype(jnp.float32)
+
+    first_grad = summed(rows_tn(first_left, first_right), HS)
+    second_grad = summed(rows_tn(second_left, second_right), HS)
+    down_grad = summed(rows_tn(hidden, grad_low), 0)
+    in_grad = summed(rows_tn(grad_pre, feed_rows), 0)
+    in_shift_grad = lax.psum_scatter(
+        jnp.sum(grad_pre.astype(jnp.float32), axis=0), everyone, scatter_dimension=0, tiled=True
+    )
+    in_shift_grad = lax.all_gather(in_shift_grad, "dp", axis=0, tiled=True)
+
+    grad_r, gain_a, shift_a = norm_back(grad_a, norm_a, factor_a, gains[0])
+    r_low = low(grad_r)
+    grad_mixed = low(rows_nt(r_low, out_rows))
+    out_grad = summed(rows_tn(mixed, r_low), 0)
+    grad_qkv = self_attention_back(self_scalars, qkv, mixed, grad_mixed, lse_self)
+    grad_x = alpha * grad_r + rows_nn(grad_qkv, qkv_rows)
+    input_grad = to_shards(low(grad_x)).astype(jnp.float32)
+    qkv_grad = summed(rows_tn(grad_qkv, x), 0)
+
+    vectors = lax.psum(
+        (
+            jnp.stack([gain_a, gain_cy[0], gain_cy[1]]),
+            jnp.stack([shift_a, shift_cy[0], shift_cy[1]]),
+            down_shift_step,
+        ),
+        everyone,
+    )
+    cross_grad = (
+        jnp.stack([first_grad.reshape(-1, HS, width), second_grad.reshape(-1, HS, width)], axis=1)
+        .reshape(-1, width)
+        .T
+    )
+    return (
+        outputs[None],
+        input_grad[None],
+        qkv_grad.T[None],
+        out_grad[None],
+        cross_grad[None],
+        in_grad.T[None],
+        in_shift_grad[None],
+        down_grad[None],
+        vectors[2][None],
+        vectors[0][None],
+        vectors[1][None],
+    )
+
+
 def solution(mesh):
     placed = (
         P("section", None, ("dp", "tensor"), None),
@@ -566,22 +1161,29 @@
         P("section", None, None),
         P("section", None, None),
     )
-    return jax.shard_map(
-        body,
-        mesh=mesh,
-        in_specs=placed,
-        out_specs=(
-            P("section", None, ("dp", "tensor"), None),
-            P("section", None, ("dp", "tensor"), None),
-            P("section", None, "tensor"),
-            P("section", "tensor", None),
-            P("section", None, "tensor"),
-            P("section", None, "tensor"),
-            P("section", "tensor"),
-            P("section", "tensor", None),
-            P("section", None),
-            P("section", None, None),
-            P("section", None, None),
-        ),
-        check_vma=False,
-    )
+    returned = (
+        P("section", None, ("dp", "tensor"), None),
+        P("section", None, ("dp", "tensor"), None),
+        P("section", None, "tensor"),
+        P("section", "tensor", None),
+        P("section", None, "tensor"),
+        P("section", None, "tensor"),
+        P("section", "tensor"),
+        P("section", "tensor", None),
+        P("section", None),
+        P("section", None, None),
+        P("section", None, None),
+    )
+    sizes = dict(mesh.shape)
+
+    def whole(*arrays):
+        batches, sequences = arrays[1].shape[1:]
+        heads = arrays[3].shape[2] // (3 * HS)
+        group = sizes["dp"] * sizes["tensor"]
+        one_each = batches == sizes["tensor"] and sequences == sizes["dp"] and heads % group == 0
+        chosen = sequence_body if one_each else body
+        return jax.shard_map(
+            chosen, mesh=mesh, in_specs=placed, out_specs=returned, check_vma=False
+        )(*arrays)
+
+    return whole

time: 4660 us -> 1670 us (0.36)
  waiting for transfers between devices: 2840 us -> 909 us
  matrix products: 1020 us -> 184 us
  other arithmetic: 316 us -> 44.6 us
  Pallas kernels: 0 us -> 214 us
  local copies, waits for them, and re-layouts: 273 us -> 81.2 us
  blocking collectives: 64.2 us -> 168 us
    reduce_scatter x30 -> x6, waiting for transfers between devices: 1540 us -> 378 us  [summed(): lax.psum_scatter(low(grad_rows_all), everyone, scatter_dimension=0, tiled...]
    dot_general x145 -> x18, matrix products: 1020 us -> 184 us  [the longest x6 68.6 us: rows_nt(): lax.dot_general(rows, weight_rows, COL_DIMS, preferred_element_type=jnp.f...]
    all_gather x30 -> x9, waiting for transfers between devices: 688 us -> 197 us  [the longest x6 157 us: gathered(): return lax.all_gather(rows, everyone, axis=0, tiled=True)]
    ppermute x9 -> x4, waiting for transfers between devices: 574 us -> 256 us  [the longest x1 170 us: sequence_body(): grad_mixed_held = lax.ppermute(grad_mixed_c, 'section', [(1, 0)])]
    pallas_call x0 -> x4, Pallas kernels: none -> 214 us  [head_call(): pl.pallas_call(kernel, grid_spec=pltpu.PrefetchScalarGridSpec(num_scalar_...]
    all_gather x0 -> x5, blocking collectives: none -> 114 us  [the longest x1 77.9 us: gathered(): return lax.all_gather(rows, everyone, axis=0, tiled=True)]
    all_to_all x0 -> x4, waiting for transfers between devices: none -> 77 us  [the longest x2 77 us: to_sequence(): lax.all_to_all(shards, 'tensor', 0, 0, tiled=True).reshape(slots, width)]
    unnamed x31 -> x0, other arithmetic: 73 us -> none
  transfers between devices with their start and end apart: 70 -> 23, of which waited for: 59 -> 16; matrix products, arithmetic and copies ran while one was open for 21% -> 11% of each run, Pallas kernels for 0% -> 5%
where the time goes in v1:
time: 1670 us; the launch traced here: 1660 us
  waiting for transfers between devices  909 us (54%)
  Pallas kernels  214 us (13%)
  matrix products  184 us (11%)
  blocking collectives  168 us (10%)
  local copies, waits for them, and re-layouts  81.2 us (5%)
  other arithmetic  44.6 us (3%)
  starting transfers between devices  28 us (2%)
  between operations  16.7 us (1%)
    reduce_scatter x6, waiting for transfers between devices, summed(): lax.psum_scatter(low(grad_rows_all), everyone, scatter_dimension=0, tiled...  378 us
    pallas_call x4, Pallas kernels, head_call(): pl.pallas_call(kernel, grid_spec=pltpu.PrefetchScalarGridSpec(num_scalar_...  214 us
    ppermute x1, waiting for transfers between devices, sequence_body(): grad_mixed_held = lax.ppermute(grad_mixed_c, 'section', [(1, 0)])  170 us
    all_gather x6, waiting for transfers between devices, gathered(): return lax.all_gather(rows, everyone, axis=0, tiled=True)  157 us
    all_gather x1, blocking collectives, gathered(): return lax.all_gather(rows, everyone, axis=0, tiled=True)  77.9 us
    all_to_all x2, waiting for transfers between devices, to_sequence(): lax.all_to_all(shards, 'tensor', 0, 0, tiled=True).reshape(slots, width)  77 us
    dot_general x6, matrix products, rows_nt(): lax.dot_general(rows, weight_rows, COL_DIMS, preferred_element_type=jnp.f...  68.6 us
    dot_general x6, matrix products, rows_tn(): lax.dot_general(left_rows, right_rows, ROW_DIMS, preferred_element_type=j...  60 us
  transfers between devices with their start and end apart: 23, of which 16 were waited for; matrix products, arithmetic and copies ran while one was open for 11% of the time, Pallas kernels for 5%

profile of v1, /device:TPU:9, one launch (start us, length us, event | category | flops | bytes accessed | tf_op | source)
XLA Modules:
  0.0 1660.2 jit_solution(9768652404697933076)
XLA Ops:
  24.4 77.0 %all-to-all-done = bf16[4,256,1024]{2,1,0:T(8,128)(2,1)S(1)} async-done(((bf16[4,256,1024]{2,1,0:T(8,128)(2,1)}), bf16[4,256,1024]{2,1,0:T(8,128)(2,1)S(1)}, u32[]{:S(2)}, u32[]{:S(2)}) %all-to-all-start) | async-done | bytes 2097184 | tf_op jit(solution)/shard_map/all_to_all | solution.py:916
  106.2 11.4 convert_bitcast_fusion.packed_ref
  117.6 44.5 %shard_map.203 = (bf16[1024,1024]{1,0:T(8,128)(2,1)S(1)}, f32[8,8,1024]{2,1,0:T(8,128)S(1)}) custom-call(s32[2]{0:T(128)S(1)} %pad_add_fusion.scalars, bf16[1024,3072]{1,0:T(8,128)(2,1)} %convert_bitcast_fusion.packed_ref), custom_call_target="tpu_custom_call" | custom-call | flops 60129542144 | bytes 12582912 | tf_op jit(solution)/shard_map/pallas_call | solution.py:784
  172.4 22.0 %all-gather.30.cloned.1.call-done = bf16[1,1,1024,1024]{3,2,1,0:T(8,128)(2,1)} async-done(((bf16[1,1,64,1024]{3,2,1,0:T(8,128)(2,1)}), bf16[1,1,1024,1024]{3,2,1,0:T(8,128)(2,1)}) %all-gather.30.cloned.1.call-update) | async-done | bytes 2097168 | tf_op jit(solution)/shard_map/all_gather | solution.py:913
  201.3 6.0 all-to-all-start.1
  208.1 77.9 %all-gather.4 = bf16[16,1,256]{2,1,0:T(2,128)(2,1)S(1)} all-gather(bf16[1,1,256]{2,1,0:T(2,128)(2,1)S(1)} %fusion.44), channel_id=1, replica_groups=mesh['section'=2,'dp'=4,'tensor'=4] {'dp','tensor'}, dimensions={0}, use_global_device_ids=true | all-gather | bytes 8704 | tf_op jit(solution)/shard_map/all_gather | solution.py:913
  286.8 54.0 %all-gather.18.cloned.1.call-done = bf16[4096,1024]{1,0:T(8,128)(2,1)} async-done(((bf16[256,1024]{1,0:T(8,128)(2,1)}), bf16[4096,1024]{1,0:T(8,128)(2,1)}) %all-gather.18.cloned.1.call-update) | async-done | bytes 8388624 | tf_op jit(solution)/shard_map/all_gather | solution.py:913
  340.8 75.8 %all-gather.28.cloned.1.call-done = bf16[1,4096,1024]{2,1,0:T(8,128)(2,1)} async-done(((bf16[1,256,1024]{2,1,0:T(8,128)(2,1)}), bf16[1,4096,1024]{2,1,0:T(8,128)(2,1)}) %all-gather.28.cloned.1.call-update) | async-done | bytes 8388624 | tf_op jit(solution)/shard_map/all_gather | solution.py:913
  416.6 100.1 %conditional.6 = (f32[1024,4096]{1,0:T(8,128)}, bf16[1024,4096]{1,0:T(8,128)(2,1)}, bf16[1024,1024]{0,1:T(8,128)(2,1)}, f32[1024,1024]{0,1:T(8,128)}, f32[1024,1...) conditional(s32[]{:T(128)} %convert_element_type.132, ...), branch_computations={%region_4.7_spmd, %region_7.8_spmd} | conditional | flops 81661001728 | bytes 125911168 | solution.py:978
  416.6 19.7 %fusion.7 = (bf16[1024,4096]{1,0:T(8,128)(2,1)}, f32[1024,4096]{1,0:T(8,128)}) fusion(f32[4096]{0:T(1024)S(1)} %get-tuple-element.143, bf16[1024,1024]{1,0:T(8,128)(2,1)} %get-tuple-element.141, bf16[4096,1024]{1,0:T(8,128)(2,1)} %get-tuple-element.142), kind=kOutput, calls=%fused_computation.9 | convolution fusion | flops 8631877632 | bytes 35667968 | tf_op jit(solution)/shard_map/cond/branch_0_fun/dot_general | solution.py:859
  436.3 5.3 copy.100
  441.7 14.5 fusion.50
  461.5 5.6 convolution_convert_fusion.2.key_ref
  467.1 5.3 convolution_convert_fusion.1.value_ref
  472.4 44.1 %branch_0_fun.2 = (bf16[1024,1024]{1,0:T(8,128)(2,1)}, f32[8,8,1024]{2,1,0:T(8,128)S(1)}) custom-call(s32[2]{0:T(128)S(1)} %get-tuple-element.152.scalars, bf16[1024,1024]{1,0:T(8,128)(2,1)} %get-tuple-element.153.query_ref, bf16[1024,1024]{1,0:T(8,128)(2,1)} %convolution_convert_fusion.2.key_ref, bf16[1024,1024]{1,0:T(8,128)(2,1)} %convolution_convert_fusion.1.value_ref), custom_call_target="tpu_custom_call" | custom-call | flops 60129542144 | bytes 12582912 | tf_op jit(solution)/shard_map/cond/branch_0_fun/pallas_call | solution.py:784
  519.4 44.0 %collective-permute-done.1 = bf16[1024,1024]{1,0:T(8,128)(2,1)} collective-permute-done((bf16[1024,1024]{1,0:T(8,128)(2,1)}, bf16[1024,1024]{1,0:T(8,128)(2,1)}, u32[]{:S(2)}, u32[]{:S(2)}) %collective-permute-start.1) | collective-permute-done | bytes 2097184 | tf_op jit(solution)/shard_map/ppermute | solution.py:981
  563.4 25.8 %conditional.7 = (bf16[1024,1024]{0,1:T(8,128)(2,1)}, bf16[1024,4096]{1,0:T(8,128)(2,1)}, bf16[1024,1024]{0,1:T(8,128)(2,1)}, bf16[1024,1024]{0,1:T(8,128)(2,1)}...) conditional(s32[]{:T(128)} %convert_element_type.132, () %tuple.55, ...), branch_computations={%region_8.9_spmd, %region_9.23_spmd} | conditional | flops 38852886528 | bytes 287631584 | solution.py:1028
  590.6 169.5 %collective-permute-done.2 = bf16[1024,1024]{1,0:T(8,128)(2,1)S(1)} collective-permute-done((bf16[1024,1024]{1,0:T(8,128)(2,1)}, bf16[1024,1024]{1,0:T(8,128)(2,1)S(1)}, u32[]{:S(2)}, u32[]{:S(2)}) %collective-permute-start.2) | collective-permute-done | bytes 2097184 | tf_op jit(solution)/shard_map/ppermute | solution.py:1029
  760.2 62.6 %conditional.8 = ((bf16[1024,1024]{1,0:T(8,128)(2,1)}, bf16[1024,1024]{1,0:T(8,128)(2,1)}, bf16[1024,1024]{1,0:T(8,128)(2,1)})) conditional(s32[]{:T(128)} %convert_element_type.132, (s32[2]{0:T(128)S(1)}, bf16[1024,1024]{1,0:T(8,128)(2,1)}, bf16[1024,1024]{1,0:T(8,128)(2,1)}, bf16[1024,1024]{1,0:T(8,128)(2,1)}, bf16[1024,1024]{1,0:T(8,128)(2,1)}, ...), branch_computations={%region_23.24_spmd, %region_24.25_spmd} | conditional | flops 146028888064 | bytes 20971528 | solution.py:1042
  760.2 62.6 %branch_0_fun.3 = (bf16[1024,1024]{1,0:T(8,128)(2,1)}, bf16[1024,1024]{1,0:T(8,128)(2,1)}, bf16[1024,1024]{1,0:T(8,128)(2,1)}) custom-call(s32[2]{0:T(128)S(1)} %get-tuple-element.169.scalars, bf16[1024,1024]{1,0:T(8,128)(2,1)} %get-tuple-element.170.query_ref, bf16[1024,1024]{1,0:T(8,128)(2,1)} %get-tuple-element.171.key_ref, ...), custom_call_target="tpu_custom_call" | custom-call | flops 146028888064 | bytes 20971520 | tf_op jit(solution)/shard_map/cond/branch_0_fun/pallas_call | solution.py:784
  825.4 42.8 %collective-permute-done.3 = bf16[1024,1024]{1,0:T(8,128)(2,1)} collective-permute-done((bf16[1024,1024]{1,0:T(8,128)(2,1)}, bf16[1024,1024]{1,0:T(8,128)(2,1)}, u32[]{:S(2)}, u32[]{:S(2)}) %collective-permute-start.3) | collective-permute-done | bytes 2097184 | tf_op jit(solution)/shard_map/ppermute | solution.py:1043
  868.2 78.8 %conditional.9 = (bf16[1024,1024]{1,0:T(8,128)(2,1)}, bf16[1024,4096]{1,0:T(8,128)(2,1)}, bf16[1024,4096]{1,0:T(8,128)(2,1)}, bf16[1024,1024]{1,0:T(8,128)(2,1)}...) conditional(s32[]{:T(128)} %convert_element_type.132, ...), branch_computations={%region_25.32_spmd.clone, %region_32.34_spmd.clone} | conditional | flops 21573398528 | bytes 193016064 | solution.py:1095
  868.2 5.3 copy.119
  889.2 24.2 %fusion.15 = bf16[1024,4096]{1,0:T(8,128)(2,1)} fusion(f32[1024,4096]{1,0:T(8,128)} %get-tuple-element.681, bf16[1024,1024]{1,0:T(8,128)(2,1)} %convert_element_type.159, bf16[4096,1024]{1,0:T(8,128)(2,1)} %get-tuple-element.680), kind=kOutput, calls=%fused_computation.28 | convolution fusion | flops 8669626368 | bytes 35651584 | tf_op jit(solution)/shard_map/cond/branch_0_fun/dot_general | solution.py:859
  916.7 15.0 fusion.51
  947.1 5.3 multiply_reduce_fusion.12
  957.0 63.3 %shard_map.204 = bf16[1024,3072]{1,0:T(8,128)(2,1)} custom-call(s32[2]{0:T(128)S(1)} %pad_add_fusion.scalars, bf16[1024,3072]{1,0:T(8,128)(2,1)} %convert_bitcast_fusion.packed_ref, bf16[1024,1024]{1,0:T(8,128)(2,1)S(1)} %get-tuple-element.259.mixed_ref, bf16[1024,1024]{1,0:T(8,128)(2,1)S(1)} %fusion.39.grad_ref, f32[8,8,1024]{2,1,0:T(8,128)S(1)} %get-tuple-element.286.lse_ref), custom_call_target="tpu_custom_call" | custom-call | flops 146028888064 | bytes 20971520 | tf_op jit(solution)/shard_map/pallas_call | solution.py:784
  1020.3 11.5 convolution_convert_fusion.6
  1032.3 15.0 convolution_convert_fusion.5
  1047.4 15.7 convolution_convert_fusion.4
  1063.3 5.9 convolution_convert_fusion.7
  1069.4 5.9 convolution_convert_fusion.8
  1075.4 5.9 convolution_convert_fusion.9
  1081.4 34.1 %reduce-scatter.7.cloned.1.call-done = bf16[192,1024]{1,0:T(8,128)(2,1)} async-done(((bf16[3072,1024]{1,0:T(8,128)(2,1)}), bf16[192,1024]{1,0:T(8,128)(2,1)}) %reduce-scatter.7.cloned.1.call-update) | async-done | bytes 393232 | tf_op jit(solution)/shard_map/reduce_scatter | solution.py:1098
  1124.0 120.5 %reduce-scatter.15.cloned.1.call-done = bf16[256,1024]{1,0:T(8,128)(2,1)} async-done(((bf16[4096,1024]{1,0:T(8,128)(2,1)}), bf16[256,1024]{1,0:T(8,128)(2,1)}) %reduce-scatter.15.cloned.1.call-update) | async-done | bytes 524304 | tf_op jit(solution)/shard_map/reduce_scatter | solution.py:1098
  1244.5 12.2 add_convert_fusion.2
  1263.3 119.7 %reduce-scatter.17.cloned.1.call-done = bf16[256,1024]{1,0:T(8,128)(2,1)} async-done(((bf16[4096,1024]{1,0:T(8,128)(2,1)}), bf16[256,1024]{1,0:T(8,128)(2,1)}) %reduce-scatter.17.cloned.1.call-update) | async-done | bytes 524304 | tf_op jit(solution)/shard_map/reduce_scatter | solution.py:1098
  1387.7 54.5 %all-reduce.1 = (f32[4096]{0:T(1024)S(1)}, f32[1,1024]{1,0:T(1,128)}, f32[1,3,1024]{2,0,1:T(1,128)}, f32[1,3,1024]{2,0,1:T(1,128)}) all-reduce(f32[4096]{0:T(1024)S(1)} %convert_reduce_fusion, f32[1,1024]{1,0:T(1,128)S(1)} %bitcast.208, ...), channel_id=11, replica_groups=mesh['section'=2,'dp'=4,'tensor'=4] {'dp','tensor'}, use_global_device_ids=true, to_apply=%region_42.43.clone | all-reduce | flops 11264 | bytes 90112
  1442.4 8.4 all-gather.5
  1450.7 7.8 all_gather.52
  1458.5 52.8 %reduce-scatter.11.cloned.1.call-done = bf16[64,1024]{1,0:T(8,128)(2,1)} async-done(((bf16[1024,1024]{1,0:T(8,128)(2,1)}), bf16[64,1024]{1,0:T(8,128)(2,1)}) %reduce-scatter.11.cloned.1.call-update) | async-done | bytes 131088 | tf_op jit(solution)/shard_map/reduce_scatter | solution.py:1098
  1511.3 9.8 all_gather.51
  1525.7 50.8 %reduce-scatter.9.cloned.1.call-done = bf16[64,1024]{1,0:T(8,128)(2,1)} async-done(((bf16[1024,1024]{1,0:T(8,128)(2,1)}), bf16[64,1024]{1,0:T(8,128)(2,1)}) %reduce-scatter.9.cloned.1.call-update) | async-done | bytes 131088 | tf_op jit(solution)/shard_map/reduce_scatter | solution.py:1098
  1576.5 10.0 all_gather.50
  1590.1 9.2 all-gather.20.cloned.1.call-done
  1606.3 17.0 %all-gather.22.cloned.1.call-done = bf16[1024,1024]{1,0:T(8,128)(2,1)} async-done(((bf16[256,1024]{1,0:T(8,128)(2,1)}), bf16[1024,1024]{1,0:T(8,128)(2,1)}) %all-gather.22.cloned.1.call-update) | async-done | bytes 2097168 | tf_op jit(solution)/shard_map/all_gather | solution.py:1101
  1627.4 5.5 copy.115
  1632.9 14.4 all-gather.24.cloned.1.call-done
  (214 shorter events, 149.2 us)
Async XLA Ops:
  7.2 6.7 copy-start
  7.2 99.0 %all-gather.16.cloned.1.call-start = ((), (), s32[]{:S(2)}) async-start(), calls=%async_computation.10 | async-start | bytes 6684672 | tf_op jit(solution)/shard_map/all_gather | solution.py:913
  9.7 152.4 %all-gather.26.cloned.1.call-start = ((), (), s32[]{:S(2)}) async-start(), calls=%async_computation.21 | async-start | bytes 2228224 | tf_op jit(solution)/shard_map/all_gather | solution.py:913
  11.4 183.0 %all-gather.30.cloned.1.call-start = ((), (), s32[]{:S(2)}) async-start(), calls=%async_computation.23 | async-start | bytes 2228224 | tf_op jit(solution)/shard_map/all_gather | solution.py:913
  13.3 273.4 %all-gather.32.cloned.1.call-start = ((), (), s32[]{:S(2)}) async-start(), calls=%async_computation.24 | async-start | bytes 2228224 | tf_op jit(solution)/shard_map/all_gather | solution.py:913
  13.9 326.9 %all-gather.18.cloned.1.call-start = ((), (), s32[]{:S(2)}) async-start(), calls=%async_computation.11 | async-start | bytes 8912896 | tf_op jit(solution)/shard_map/all_gather | solution.py:913
  13.9 7.9 copy-start.23
  13.9 7.9 copy-start.24
  14.0 7.9 copy-start.39
  15.1 401.5 %all-gather.28.cloned.1.call-start = ((), (), s32[]{:S(2)}) async-start(), calls=%async_computation.22 | async-start | bytes 8912896 | tf_op jit(solution)/shard_map/all_gather | solution.py:913
  17.0 84.3 %all-to-all-start = ((bf16[4,256,1024]{2,1,0:T(8,128)(2,1)}), bf16[4,256,1024]{2,1,0:T(8,128)(2,1)S(1)}, u32[]{:S(2)}, u32[]{:S(2)}) async-start(bf16[4,256,1024]{2,1,0:T(8,128)(2,1)} %bitcast.169), calls=%async_computation | async-start | bytes 4194304 | tf_op jit(solution)/shard_map/all_to_all | solution.py:916
  21.8 145.6 %copy-start.18 = (f32[1,1,1024]{2,1,0:T(1,128)}, f32[1,1,1024]{2,1,0:T(1,128)S(1)}, u32[]{:S(2)}) copy-start(f32[1,1,1024]{2,1,0:T(1,128)S(1)} %slice.51) | copy-start | bytes 12292
  196.0 90.0 %copy-start.38 = (bf16[1,1024]{1,0:T(2,128)(2,1)S(1)}, bf16[1,1024]{1,0:T(2,128)(2,1)}, u32[]{:S(2)}) copy-start(bf16[1,1024]{1,0:T(2,128)(2,1)} %param.31) | copy-start | bytes 6148
  196.0 90.8 %collective-permute-start = (bf16[1024,1024]{1,0:T(8,128)(2,1)}, bf16[1024,1024]{1,0:T(8,128)(2,1)}, u32[]{:S(2)}, u32[]{:S(2)}) collective-permute-start(bf16[1024,1024]{1,0:T(8,128)(2,1)} %get-tuple-element.913), channel_id=1, source_target_pairs={{16,0},{17,1},{18,2},{19,3},{20,4},{21,5},{22,6},{23,7},{24,8},{25... | collective-permute-start | bytes 6291464 | tf_op jit(solution)/shard_map/ppermute | solution.py:951
  201.3 318.0 %all-to-all-start.1 = ((bf16[4,256,1024]{1,2,0:T(8,128)(2,1)}), bf16[4,256,1024]{1,2,0:T(8,128)(2,1)}, u32[]{:S(2)}, u32[]{:S(2)}) async-start(bf16[4,256,1024]{1,2,0:T(8,128)(2,1)} %copy.101), calls=%async_computation.1 | async-start | bytes 4194304 | tf_op jit(solution)/shard_map/all_to_all | solution.py:916
  207.3 908.1 %reduce-scatter.7.cloned.1.call-start = ((), (), s32[]{:S(2)}) async-start(), calls=%async_computation.12 | async-start | bytes 6684672 | tf_op jit(solution)/shard_map/reduce_scatter | solution.py:1098
  286.7 276.7 %copy-start.22 = (f32[3,1024]{1,0:T(4,128)}, f32[3,1024]{1,0:T(4,128)S(1)}, u32[]{:S(2)}) copy-start(f32[3,1024]{1,0:T(4,128)S(1)} %get-tuple-element.794) | copy-start | bytes 36868
  461.5 5.6 copy-start.42
  516.7 46.7 %collective-permute-start.1 = (bf16[1024,1024]{1,0:T(8,128)(2,1)}, bf16[1024,1024]{1,0:T(8,128)(2,1)}, u32[]{:S(2)}, u32[]{:S(2)}) collective-permute-start(bf16[1024,1024]{1,0:T(8,128)(2,1)} %get-tuple-element.260), channel_id=1, source_target_pairs={{0,16},{1,17},{2,18},{3,19},{4,20},{5,21},{6,22},{7,23},{8,24},{9,... | collective-permute-start | bytes 6291464 | tf_op jit(solution)/shard_map/ppermute | solution.py:981
  589.2 170.9 %copy-start.26 = (f32[1024]{0:T(1024)}, f32[1024]{0:T(1024)S(1)}, u32[]{:S(2)}) copy-start(f32[1024]{0:T(1024)S(1)} %get-tuple-element.879) | copy-start | bytes 12292
  589.2 170.9 %copy-start.28 = (f32[1024]{0:T(1024)}, f32[1024]{0:T(1024)S(1)}, u32[]{:S(2)}) copy-start(f32[1024]{0:T(1024)S(1)} %get-tuple-element.880) | copy-start | bytes 12292
  589.3 170.9 %copy-start.30 = (f32[1024]{0:T(1024)}, f32[1024]{0:T(1024)S(1)}, u32[]{:S(2)}) copy-start(f32[1024]{0:T(1024)S(1)} %get-tuple-element.881) | copy-start | bytes 12292
  589.3 170.9 %copy-start.32 = (f32[1024]{0:T(1024)}, f32[1024]{0:T(1024)S(1)}, u32[]{:S(2)}) copy-start(f32[1024]{0:T(1024)S(1)} %get-tuple-element.882) | copy-start | bytes 12292
  589.3 170.9 %copy-start.34 = (f32[1024]{0:T(1024)}, f32[1024]{0:T(1024)S(1)}, u32[]{:S(2)}) copy-start(f32[1024]{0:T(1024)S(1)} %get-tuple-element.887) | copy-start | bytes 12292
  589.3 170.8 %collective-permute-start.2 = (bf16[1024,1024]{1,0:T(8,128)(2,1)}, bf16[1024,1024]{1,0:T(8,128)(2,1)S(1)}, u32[]{:S(2)}, u32[]{:S(2)}) collective-permute-start(bf16[1024,1024]{1,0:T(8,128)(2,1)} %get-tuple-element.265), channel_id=1, source_target_pairs={{16,0},{17,1},{18,2},{19,3},{20,4},{21,5},{22,6},{23,7},{24,8},{25... | collective-permute-start | bytes 6291464 | tf_op jit(solution)/shard_map/ppermute | solution.py:1029
  822.7 45.5 %collective-permute-start.3 = (bf16[1024,1024]{1,0:T(8,128)(2,1)}, bf16[1024,1024]{1,0:T(8,128)(2,1)}, u32[]{:S(2)}, u32[]{:S(2)}) collective-permute-start(bf16[1024,1024]{1,0:T(8,128)(2,1)} %get-tuple-element.274), channel_id=1, source_target_pairs={{0,16},{1,17},{2,18},{3,19},{4,20},{5,21},{6,22},{7,23},{8,24},{9,... | collective-permute-start | bytes 6291464 | tf_op jit(solution)/shard_map/ppermute | solution.py:1043
  868.2 78.8 %copy-start.17 = (f32[1024]{0:T(1024)S(1)}, f32[1024]{0:T(1024)}, u32[]{:S(2)}) copy-start(f32[1024]{0:T(1024)} %copy-done.16) | copy-start | bytes 12292
  868.2 78.8 %copy-start.19 = (f32[1,1,1024]{2,1,0:T(1,128)S(1)}, f32[1,1,1024]{2,1,0:T(1,128)}, u32[]{:S(2)}) copy-start(f32[1,1,1024]{2,1,0:T(1,128)} %copy-done.18) | copy-start | bytes 12292
  868.2 78.8 %copy-start.21 = (f32[1024]{0:T(1024)S(1)}, f32[1024]{0:T(1024)}, u32[]{:S(2)}) copy-start(f32[1024]{0:T(1024)} %copy-done.20) | copy-start | bytes 12292
  947.1 5.9 copy-start.6
  957.0 63.3 %copy-start.15 = (bf16[4,256,1024]{2,1,0:T(8,128)(2,1)S(1)}, bf16[4,256,1024]{2,1,0:T(8,128)(2,1)}, u32[]{:S(2)}) copy-start(bf16[4,256,1024]{2,1,0:T(8,128)(2,1)} %copy-done.14) | copy-start | bytes 6291460
  1031.8 212.7 %reduce-scatter.15.cloned.1.call-start = ((), (), s32[]{:S(2)}) async-start(), calls=%async_computation.17 | async-start | bytes 8912896 | tf_op jit(solution)/shard_map/reduce_scatter | solution.py:1098
  1047.4 335.6 %reduce-scatter.17.cloned.1.call-start = ((), (), s32[]{:S(2)}) async-start(), calls=%async_computation.19 | async-start | bytes 8912896 | tf_op jit(solution)/shard_map/reduce_scatter | solution.py:1098
  1063.2 387.5 %reduce-scatter.13.cloned.1.call-start = ((), (), s32[]{:S(2)}) async-start(), calls=%async_computation.16 | async-start | bytes 2228224 | tf_op jit(solution)/shard_map/reduce_scatter | solution.py:1098
  1069.2 442.1 %reduce-scatter.11.cloned.1.call-start = ((), (), s32[]{:S(2)}) async-start(), calls=%async_computation.15 | async-start | bytes 2228224 | tf_op jit(solution)/shard_map/reduce_scatter | solution.py:1098
  1075.4 501.1 %reduce-scatter.9.cloned.1.call-start = ((), (), s32[]{:S(2)}) async-start(), calls=%async_computation.14 | async-start | bytes 2228224 | tf_op jit(solution)/shard_map/reduce_scatter | solution.py:1098
  1081.4 517.9 %all-gather.20.cloned.1.call-start = ((), (), s32[]{:S(2)}) async-start(), calls=%async_computation.13 | async-start | bytes 1966080 | tf_op jit(solution)/shard_map/all_gather | solution.py:1101
  1119.9 136.9 %all-to-all-start.2 = ((bf16[4,256,1024]{2,1,0:T(8,128)(2,1)}), bf16[4,256,1024]{2,1,0:T(8,128)(2,1)S(1)}, u32[]{:S(2)}, u32[]{:S(2)}) async-start(bf16[4,256,1024]{2,1,0:T(8,128)(2,1)} %bitcast.168), calls=%async_computation.2 | async-start | bytes 4194304 | tf_op jit(solution)/shard_map/all_to_all | solution.py:919
  1124.0 499.3 %all-gather.22.cloned.1.call-start = ((), (), s32[]{:S(2)}) async-start(), calls=%async_computation.18 | async-start | bytes 2621440 | tf_op jit(solution)/shard_map/all_gather | solution.py:1101
  1256.7 126.3 %copy-start.25 = (f32[1024]{0:T(1024)S(1)}, f32[1024]{0:T(1024)}, u32[]{:S(2)}) copy-start(f32[1024]{0:T(1024)} %get-tuple-element.745) | copy-start | bytes 12292
  1256.7 126.3 %copy-start.27 = (f32[1,1024]{1,0:T(1,128)S(1)}, f32[1,1024]{1,0:T(1,128)}, u32[]{:S(2)}) copy-start(f32[1,1024]{1,0:T(1,128)} %get-tuple-element.668) | copy-start | bytes 12292
  1256.7 126.3 %copy-start.29 = (f32[1,1024]{1,0:T(1,128)S(1)}, f32[1,1024]{1,0:T(1,128)}, u32[]{:S(2)}) copy-start(f32[1,1024]{1,0:T(1,128)} %get-tuple-element.669) | copy-start | bytes 12292
  1256.7 126.3 %copy-start.31 = (f32[1,1024]{1,0:T(1,128)S(1)}, f32[1,1024]{1,0:T(1,128)}, u32[]{:S(2)}) copy-start(f32[1,1024]{1,0:T(1,128)} %get-tuple-element.670) | copy-start | bytes 12292
  1256.7 126.3 %copy-start.33 = (f32[1,1024]{1,0:T(1,128)S(1)}, f32[1,1024]{1,0:T(1,128)}, u32[]{:S(2)}) copy-start(f32[1,1024]{1,0:T(1,128)} %get-tuple-element.671) | copy-start | bytes 12292
  1256.8 126.3 %copy-start.37 = (f32[1,1024]{1,0:T(1,128)S(1)}, f32[1,1024]{1,0:T(1,128)}, u32[]{:S(2)}) copy-start(f32[1,1024]{1,0:T(1,128)} %copy-done.36) | copy-start | bytes 12292
  1258.1 329.5 %all-to-all-start.3 = ((bf16[4,256,1024]{2,1,0:T(8,128)(2,1)}), bf16[4,256,1024]{2,1,0:T(8,128)(2,1)S(1)}, u32[]{:S(2)}, u32[]{:S(2)}) async-start(bf16[4,256,1024]{2,1,0:T(8,128)(2,1)} %bitcast.173), calls=%async_computation.3 | async-start | bytes 4194304 | tf_op jit(solution)/shard_map/all_to_all | solution.py:919
  1262.0 385.3 %all-gather.24.cloned.1.call-start = ((), (), s32[]{:S(2)}) async-start(), calls=%async_computation.20 | async-start | bytes 2621440 | tf_op jit(solution)/shard_map/all_gather | solution.py:1101
  1627.4 26.1 %copy-start.1 = (bf16[1,1024,1024]{2,1,0:T(8,128)(2,1)S(1)}, bf16[1,1024,1024]{2,1,0:T(8,128)(2,1)}, u32[]{:S(2)}) copy-start(bf16[1,1024,1024]{2,1,0:T(8,128)(2,1)} %param.28) | copy-start | bytes 6291460
  (18 other events, 64.4 us)
Sparse Core Ops, SparseCore 0:
  10.9 95.2 all-gather.15
  109.0 42.4 all-gather.25
  154.3 40.0 all-gather.29
  196.5 64.6 all-gather.31
  263.8 76.9 all-gather.17
  343.4 73.1 all-gather.27
  1031.9 83.4 reduce-scatter.6
  1120.1 124.3 reduce-scatter.14
  1249.1 133.8 reduce-scatter.16
  1387.6 59.2 reduce-scatter.12
  1450.7 60.5 reduce-scatter.10
  1515.9 60.5 reduce-scatter.8
  1578.1 21.1 all-gather.19
  1600.7 22.5 all-gather.21
  1624.7 22.5 all-gather.23

commit v2 on v1

--- a/solution.py
+++ b/solution.py
@@ -1,3 +1,5 @@
+import functools
+
 import jax
 import jax.numpy as jnp
 from jax import lax
@@ -17,6 +19,8 @@
 COL_DIMS = (((1,), (1,)), ((), ()))
 LANES = 2 * HS
 ROWS = 256
+CHUNK = 32
+MESH = pl.DeviceIdType.MESH
 SCALE = HS ** (-0.5)
 GELU_C = (2.0 / 3.141592653589793) ** 0.5
 
@@ -736,8 +740,7 @@
     grad_ref,
     lse_ref,
     dq_ref,
-    dk_ref,
-    dv_ref,
+    dkv_ref,
     key_acc,
     value_acc,
 ):
@@ -756,31 +759,34 @@
         key_acc,
         value_acc,
     )
-    dk_ref[...] = key_acc[...].astype(jnp.bfloat16)
-    dv_ref[...] = value_acc[...].astype(jnp.bfloat16)
-
-
-def head_call(kernel, scalars, arrays, widths, out_widths, scratch, lse_in, lse_out):
-    slots = arrays[0].shape[0]
-    pairs = arrays[0].shape[1] // widths[0]
-
-    def spec(width):
-        return pl.BlockSpec((slots, width), lambda pair, *_: (0, pair))
+    dkv_ref[0] = key_acc[...].astype(jnp.bfloat16)
+    dkv_ref[1] = value_acc[...].astype(jnp.bfloat16)
+
+
+def head_call(kernel, scalars, pairs, blocks, outs, scratch, lse_in, lse_out):
+    slots = blocks[0][0].shape[0]
+
+    def spec(width, shift):
+        return pl.BlockSpec((slots, width), lambda pair, *_: (0, pair + shift))
 
     lse_spec = pl.BlockSpec((1, 8, slots), lambda pair, *_: (pair, 0, 0))
-    in_specs = [spec(width) for width in widths]
-    operands = list(arrays)
+    in_specs = [spec(width, shift) for _, width, shift in blocks]
+    operands = [array for array, _, _ in blocks]
     if lse_in is not None:
         in_specs.append(lse_spec)
         operands.append(lse_in)
-    out_specs = [spec(width) for width in out_widths]
-    out_shape = [
-        jax.ShapeDtypeStruct((slots, pairs * width), jnp.bfloat16) for width in out_widths
-    ]
+    out_specs, out_shape = ([], [])
+    for stacked, width in outs:
+        if stacked:
+            out_specs.append(pl.BlockSpec((2, slots, width), lambda pair, *_: (0, 0, pair)))
+            out_shape.append(jax.ShapeDtypeStruct((2, slots, pairs * width), jnp.bfloat16))
+        else:
+            out_specs.append(spec(width, 0))
+            out_shape.append(jax.ShapeDtypeStruct((slots, pairs * width), jnp.bfloat16))
     if lse_out:
         out_specs.append(lse_spec)
         out_shape.append(jax.ShapeDtypeStruct((pairs, 8, slots), jnp.float32))
-    products = 7 if lse_in is None else 17
+    products = 2 if lse_in is None else 5
     return pl.pallas_call(
         kernel,
         grid_spec=pltpu.PrefetchScalarGridSpec(
@@ -795,8 +801,8 @@
             dimension_semantics=("arbitrary",), vmem_limit_bytes=48 * 1024 * 1024
         ),
         cost_estimate=pl.CostEstimate(
-            flops=products * pairs * slots * slots * LANES * 8,
-            bytes_accessed=sum(a.size * 2 for a in arrays) * 2,
+            flops=products * pairs * slots * slots * LANES * 16,
+            bytes_accessed=2 * sum(array.size for array in operands),
             transcendentals=2 * pairs * slots * slots,
         ),
     )(scalars, *operands)
@@ -807,18 +813,26 @@
     return head_call(
         self_forward_kernel,
         scalars,
-        [packed],
-        [3 * LANES],
-        [LANES],
+        packed.shape[1] // (3 * LANES),
+        [(packed, 3 * LANES, 0)],
+        [(False, LANES)],
         [pltpu.VMEM((slots, LANES), jnp.bfloat16)],
         None,
         True,
     )
 
 
-def cross_attention(scalars, queries, keys_in, values):
+def cross_attention(scalars, queries, key_values):
+    pairs = queries.shape[1] // LANES
     return head_call(
-        cross_forward_kernel, scalars, [queries, keys_in, values], [LANES] * 3, [LANES], [], None, True
+        cross_forward_kernel,
+        scalars,
+        pairs,
+        [(queries, LANES, 0), (key_values, LANES, 0), (key_values, LANES, pairs)],
+        [(False, LANES)],
+        [],
+        None,
+        True,
     )
 
 
@@ -827,9 +841,9 @@
     return head_call(
         self_backward_kernel,
         scalars,
-        [packed, mixed, grads],
-        [3 * LANES, LANES, LANES],
-        [3 * LANES],
+        packed.shape[1] // (3 * LANES),
+        [(packed, 3 * LANES, 0), (mixed, LANES, 0), (grads, LANES, 0)],
+        [(False, 3 * LANES)],
         [
             pltpu.VMEM((slots, LANES), jnp.bfloat16),
             pltpu.VMEM((slots, LANES), jnp.bfloat16),
@@ -841,14 +855,21 @@
     )[0]
 
 
-def cross_attention_back(scalars, queries, keys_in, values, mixed, grads, lse):
+def cross_attention_back(scalars, queries, key_values, mixed, grads, lse):
     slots = queries.shape[0]
+    pairs = queries.shape[1] // LANES
     return head_call(
         cross_backward_kernel,
         scalars,
-        [queries, keys_in, values, mixed, grads],
-        [LANES] * 5,
-        [LANES] * 3,
+        pairs,
+        [
+            (queries, LANES, 0),
+            (key_values, LANES, 0),
+            (key_values, LANES, pairs),
+            (mixed, LANES, 0),
+            (grads, LANES, 0),
+        ],
+        [(False, LANES), (True, LANES)],
         [pltpu.VMEM((slots, LANES), jnp.float32), pltpu.VMEM((slots, LANES), jnp.float32)],
         lse,
         False,
@@ -867,15 +888,490 @@
     return lax.dot_general(left_rows, right_rows, ROW_DIMS, preferred_element_type=jnp.float32)
 
 
-def gelu_slope(values):
-    inner = GELU_C * (values + 0.044715 * values * values * values)
-    bend = jnp.tanh(inner)
-    rise = GELU_C * (1.0 + 3 * 0.044715 * values * values)
-    return 0.5 * (1.0 + bend) + 0.5 * values * (1.0 - bend * bend) * rise
-
-
 def low(values):
     return values.astype(jnp.bfloat16)
+
+
+def gelu_and_slope(values):
+    square = values * values
+    bend = jnp.tanh(GELU_C * values * (1.0 + 0.044715 * square))
+    rise = GELU_C * (1.0 + 3 * 0.044715 * square)
+    gate = 0.5 * (1.0 + bend)
+    return (values * gate, gate + 0.5 * values * (1.0 - bend * bend) * rise)
+
+
+def after(value, *earlier):
+    return lax.optimization_barrier((value, earlier))[0]
+
+
+def around(value, distance):
+    count = lax.axis_size("tensor")
+    return lax.ppermute(value, "tensor", [(i, (i + distance) % count) for i in range(count)])
+
+
+def partner(value, bit):
+    return lax.ppermute(value, "dp", [(i, i ^ bit) for i in range(lax.axis_size("dp"))])
+
+
+def exchange(blocks, store_type):
+    count = lax.axis_size("tensor")
+    place = lax.axis_index("tensor")
+    arrived = [lax.dynamic_index_in_dim(blocks, place, 0)]
+    for distance in range(1, count):
+        sent = lax.dynamic_index_in_dim(blocks, (place + distance) % count, 0)
+        arrived.append(around(sent, distance))
+    placed = jnp.zeros(blocks.shape, store_type)
+    for distance in range(count):
+        block = arrived[distance].astype(store_type)
+        placed = lax.dynamic_update_slice_in_dim(placed, block, (place - distance) % count, 0)
+    return placed
+
+
+def mesh_place():
+    return (
+        lax.axis_index("dp"),
+        lax.axis_index("tensor"),
+        lax.axis_size("tensor"),
+    )
+
+
+def greet(unit, place, count):
+    partners = [{"tensor": lax.rem(place + d, count)} for d in range(1, count)]
+    partners.append({"dp": lax.rem(unit + 2, 4)})
+    partners.append({"dp": unit + 1 - 2 * lax.rem(unit, 2)})
+    barrier = pltpu.get_barrier_semaphore()
+    for partner_id in partners:
+        pl.semaphore_signal(barrier, inc=1, device_id=partner_id, device_id_type=MESH)
+    pl.semaphore_wait(barrier, len(partners))
+    return partners
+
+
+def remote(source, target, send_sem, recv_sem, device_id):
+    return pltpu.make_async_remote_copy(
+        src_ref=source,
+        dst_ref=target,
+        send_sem=send_sem,
+        recv_sem=recv_sem,
+        device_id=device_id,
+        device_id_type=MESH,
+    )
+
+
+def at_slot(ref, axis, slot):
+    return ref.at[slot] if axis == 0 else ref.at[:, slot]
+
+
+def gather_kernel(axes, *refs):
+    groups = len(axes)
+    blocks, own, across = (refs[0], refs[1 : 1 + groups], refs[1 + groups : 1 + 2 * groups])
+    rest = refs[1 + 2 * groups :]
+    rows, near, far = (rest[0], rest[1 : 1 + groups], rest[1 + groups : 1 + 2 * groups])
+    local_sem, block_send, block_recv, ring_send, ring_recv = rest[1 + 2 * groups : 6 + 2 * groups]
+    side_send, side_recv, core_send, core_recv = rest[6 + 2 * groups :]
+    unit, place, count = mesh_place()
+    partners = greet(unit, place, count)
+    right, side, core = (partners[0], partners[-2], partners[-1])
+    started = []
+
+    def begin(copy):
+        copy.start()
+        started.append(copy)
+        return copy
+
+    local = []
+
+    def begin_local(source, target, index):
+        copy = pltpu.make_async_copy(source, target, local_sem.at[index])
+        copy.start()
+        local.append(copy)
+
+    def slot(refs_of, group, index):
+        return at_slot(refs_of[group], axes[group], index)
+
+    def hop(group, step):
+        source = own[group] if step == 1 else slot(near, group, step - 1)
+        return begin(
+            remote(
+                source,
+                slot(near, group, step),
+                ring_send.at[group, step - 1],
+                ring_recv.at[group, step - 1],
+                right,
+            )
+        )
+
+    def to_side(group, step):
+        return begin(
+            remote(
+                slot(near, group, step),
+                slot(near, group, count + step),
+                side_send.at[group, step - 1],
+                side_recv.at[group, step - 1],
+                side,
+            )
+        )
+
+    def to_core(group, index, source):
+        return begin(
+            remote(
+                source,
+                slot(far, group, index),
+                core_send.at[group, index],
+                core_recv.at[group, index],
+                core,
+            )
+        )
+
+    hops = {(0, 1): hop(0, 1)}
+    block_copies = []
+    for distance in range(1, count):
+        block_copies.append(
+            begin(
+                remote(
+                    blocks.at[lax.rem(place + distance, count)],
+                    rows.at[place],
+                    block_send.at[distance - 1],
+                    block_recv.at[distance - 1],
+                    partners[distance - 1],
+                )
+            )
+        )
+    for group in range(1, groups):
+        hops[group, 1] = hop(group, 1)
+    begin_local(blocks.at[place], rows.at[place], 0)
+    cores, sides = ([], {})
+    for group in range(groups):
+        begin_local(own[group], slot(near, group, 0), 1 + 2 * group)
+        begin_local(across[group], slot(near, group, count), 2 + 2 * group)
+        cores.append(to_core(group, 0, own[group]))
+        cores.append(to_core(group, count, across[group]))
+    for step in range(1, count):
+        for group in range(groups):
+            hops[group, step].wait_recv()
+            if step + 1 < count:
+                hops[group, step + 1] = hop(group, step + 1)
+            sides[group, step] = to_side(group, step)
+            cores.append(to_core(group, step, slot(near, group, step)))
+            earlier = (group, step - 1)
+            if step > 1:
+                sides[earlier].wait_recv()
+                cores.append(to_core(group, count + step - 1, slot(near, group, count + step - 1)))
+    for group in range(groups):
+        last = count - 1
+        sides[group, last].wait_recv()
+        cores.append(to_core(group, count + last, slot(near, group, count + last)))
+    for copy in block_copies:
+        copy.wait_recv()
+    for copy in cores:
+        copy.wait_recv()
+    for copy in local:
+        copy.wait()
+    for copy in started:
+        copy.wait_send()
+
+
+def gather_all(blocks, own, across, axes):
+    count = lax.axis_size("tensor")
+    groups = len(axes)
+    anywhere = pl.BlockSpec(memory_space=pl.ANY)
+
+    def spread_shape(array, axis):
+        shape = list(array.shape)
+        shape.insert(axis, 2 * count)
+        return jax.ShapeDtypeStruct(tuple(shape), array.dtype)
+
+    halves = [spread_shape(array, axis) for array, axis in zip(own, axes)]
+    dma = pltpu.SemaphoreType.DMA
+    made = pl.pallas_call(
+        functools.partial(gather_kernel, axes),
+        in_specs=[anywhere] * (1 + 2 * groups),
+        out_specs=[anywhere] * (1 + 2 * groups),
+        out_shape=[jax.ShapeDtypeStruct(blocks.shape, blocks.dtype)] + halves + halves,
+        scratch_shapes=[
+            dma((1 + 2 * groups,)),
+            dma((count - 1,)),
+            dma((count - 1,)),
+            dma((groups, count - 1)),
+            dma((groups, count - 1)),
+            dma((groups, count - 1)),
+            dma((groups, count - 1)),
+            dma((groups, 2 * count)),
+            dma((groups, 2 * count)),
+        ],
+        compiler_params=pltpu.CompilerParams(collective_id=0, has_side_effects=True),
+    )(blocks, *own, *across)
+    return (made[0], made[1 : 1 + groups], made[1 + groups :])
+
+
+def reduce_kernel(axes, depths, *refs):
+    groups = len(axes)
+    blocks, small = refs[:2]
+    near, far = (refs[2 : 2 + groups], refs[2 + groups : 2 + 2 * groups])
+    rest = refs[2 + 2 * groups :]
+    rows, small_out, out = (rest[0], rest[1], rest[2 : 2 + groups])
+    (
+        near_buf,
+        sums,
+        side_in,
+        ring_in,
+        pair,
+        other,
+        small_core,
+        small_side,
+        small_far,
+        near_sem,
+        core_send,
+        core_recv,
+        side_send,
+        side_recv,
+        ring_send,
+        ring_recv,
+        pair_send,
+        pair_recv,
+        last_send,
+        last_recv,
+        out_sem,
+        block_sem,
+        block_send,
+        block_recv,
+        tiny_send,
+        tiny_recv,
+    ) = rest[2 + groups :]
+    unit, place, count = mesh_place()
+    partners = greet(unit, place, count)
+    side, core = (partners[-2], partners[-1])
+    units = (
+        unit,
+        lax.rem(unit + 2, 4),
+        unit + 1 - 2 * lax.rem(unit, 2),
+        lax.rem(unit + 3 - 2 * lax.rem(unit, 2), 4),
+    )
+    sends = []
+
+    def begin(copy):
+        copy.start()
+        sends.append(copy)
+        return copy
+
+    chunks = []
+    for group in range(groups):
+        if axes[group] == 0:
+            for first in range(0, depths[group], CHUNK):
+                chunks.append((group, (pl.ds(first, CHUNK),)))
+        else:
+            for part in range(2):
+                for first in range(0, depths[group], CHUNK):
+                    chunks.append((group, (part, pl.ds(first, CHUNK))))
+
+    def rows_of(ref, chunk, slots):
+        group, place_in = chunk
+        if axes[group] == 0:
+            return ref[group].at[slots, place_in[0]]
+        return ref[group].at[place_in[0], slots, place_in[1]]
+
+    everything = slice(None)
+    block_copies = []
+    for distance in range(1, count):
+        block_copies.append(
+            begin(
+                remote(
+                    blocks.at[lax.rem(place + distance, count)],
+                    rows.at[place],
+                    block_send.at[distance - 1],
+                    block_recv.at[distance - 1],
+                    partners[distance - 1],
+                )
+            )
+        )
+    own_block = pltpu.make_async_copy(blocks.at[place], rows.at[place], block_sem.at[0])
+    own_block.start()
+    tiny = begin(remote(small, small_core, tiny_send.at[0], tiny_recv.at[0], core))
+    state = {}
+    outs = []
+
+    def wide(value):
+        return value.astype(jnp.float32)
+
+    def enter(index):
+        chunk = chunks[index]
+        copy = pltpu.make_async_copy(
+            rows_of(near, chunk, everything), near_buf.at[index % 3], near_sem.at[index]
+        )
+        copy.start()
+        state["near", index] = copy
+        state["core", index] = begin(
+            remote(
+                rows_of(far, chunk, everything),
+                sums.at[index],
+                core_send.at[index],
+                core_recv.at[index],
+                core,
+            )
+        )
+
+    def first_sum(index):
+        state["near", index].wait()
+        state["core", index].wait_recv()
+        upper = pl.ds(count, count)
+        total = wide(near_buf[index % 3, upper]) + wide(sums[index, upper])
+        sums[index, upper] = total.astype(jnp.bfloat16)
+        state["side", index] = begin(
+            remote(
+                sums.at[index, upper],
+                side_in.at[index],
+                side_send.at[index],
+                side_recv.at[index],
+                side,
+            )
+        )
+
+    def second_sum(index):
+        state["side", index].wait_recv()
+        lower = pl.ds(0, count)
+        total = wide(near_buf[index % 3, lower]) + wide(sums[index, lower]) + wide(side_in[index])
+        sums[index, lower] = total.astype(jnp.bfloat16)
+        for distance in range(1, count):
+            state["ring", index, distance] = begin(
+                remote(
+                    sums.at[index, distance],
+                    ring_in.at[index, distance - 1],
+                    ring_send.at[index, distance - 1],
+                    ring_recv.at[index, distance - 1],
+                    partners[count - distance - 1],
+                )
+            )
+
+    def third_sum(index):
+        total = wide(sums[index, 0])
+        for distance in range(1, count):
+            state["ring", index, distance].wait_recv()
+            total = total + wide(ring_in[index, distance - 1])
+        pair[index, 0] = total.astype(jnp.bfloat16)
+        state["pair", index] = begin(
+            remote(
+                pair.at[index, 0],
+                pair.at[index, 1],
+                pair_send.at[index],
+                pair_recv.at[index],
+                side,
+            )
+        )
+
+    def spread_pair(index):
+        state["pair", index].wait_recv()
+        state["last", index] = begin(
+            remote(pair.at[index], other.at[index], last_send.at[index], last_recv.at[index], core)
+        )
+
+    def leave(index):
+        state["last", index].wait_recv()
+        chunk = chunks[index]
+        found = (pair.at[index, 0], pair.at[index, 1], other.at[index, 0], other.at[index, 1])
+        for bits in range(4):
+            copy = pltpu.make_async_copy(
+                found[bits], rows_of(out, chunk, units[bits]), out_sem.at[index, bits]
+            )
+            copy.start()
+            outs.append(copy)
+
+    stages = (enter, first_sum, second_sum, third_sum, spread_pair, leave)
+    for tick in range(len(chunks) + len(stages) - 1):
+        for number, stage in enumerate(stages):
+            if 0 <= tick - number < len(chunks):
+                stage(tick - number)
+        if tick == 2:
+            tiny.wait_recv()
+            small_core[...] += small[...]
+            tiny = begin(remote(small_core, small_side, tiny_send.at[1], tiny_recv.at[1], side))
+        if tick == 4:
+            tiny.wait_recv()
+            small_side[...] += small_core[...]
+            tiny = [
+                begin(
+                    remote(
+                        small_side,
+                        small_far.at[distance - 1],
+                        tiny_send.at[1 + distance],
+                        tiny_recv.at[1 + distance],
+                        partners[distance - 1],
+                    )
+                )
+                for distance in range(1, count)
+            ]
+        if tick == 6:
+            total = small_side[...]
+            for distance in range(1, count):
+                tiny[distance - 1].wait_recv()
+                total = total + small_far[distance - 1]
+            small_out[...] = total
+    for copy in block_copies:
+        copy.wait_recv()
+    own_block.wait()
+    for copy in outs:
+        copy.wait()
+    for copy in sends:
+        copy.wait_send()
+
+
+def reduce_all(blocks, small, near, far, axes):
+    count = lax.axis_size("tensor")
+    units = lax.axis_size("dp")
+    groups = len(axes)
+    anywhere = pl.BlockSpec(memory_space=pl.ANY)
+    vmem = pl.BlockSpec(memory_space=pltpu.VMEM)
+    width = blocks.shape[-1]
+    depths = [array.shape[axis + 1] for array, axis in zip(near, axes)]
+    total = sum(depth * (1 + axis) for depth, axis in zip(depths, axes)) // CHUNK
+
+    def own_shape(array, axis):
+        shape = list(array.shape)
+        shape[axis] = units
+        return jax.ShapeDtypeStruct(tuple(shape), array.dtype)
+
+    dma = pltpu.SemaphoreType.DMA
+    bf16 = jnp.bfloat16
+    made = pl.pallas_call(
+        functools.partial(reduce_kernel, axes, depths),
+        in_specs=[anywhere, vmem] + [anywhere] * (2 * groups),
+        out_specs=[anywhere, vmem] + [anywhere] * groups,
+        out_shape=[
+            jax.ShapeDtypeStruct(blocks.shape, blocks.dtype),
+            jax.ShapeDtypeStruct(small.shape, small.dtype),
+        ]
+        + [own_shape(array, axis) for array, axis in zip(near, axes)],
+        scratch_shapes=[
+            pltpu.VMEM((3, 2 * count, CHUNK, width), bf16),
+            pltpu.VMEM((total, 2 * count, CHUNK, width), bf16),
+            pltpu.VMEM((total, count, CHUNK, width), bf16),
+            pltpu.VMEM((total, count - 1, CHUNK, width), bf16),
+            pltpu.VMEM((total, 2, CHUNK, width), bf16),
+            pltpu.VMEM((total, 2, CHUNK, width), bf16),
+            pltpu.VMEM(small.shape, small.dtype),
+            pltpu.VMEM(small.shape, small.dtype),
+            pltpu.VMEM((count - 1,) + small.shape, small.dtype),
+            dma((total,)),
+            dma((total,)),
+            dma((total,)),
+            dma((total,)),
+            dma((total,)),
+            dma((total, count - 1)),
+            dma((total, count - 1)),
+            dma((total,)),
+            dma((total,)),
+            dma((total,)),
+            dma((total,)),
+            dma((total, 4)),
+            dma((1,)),
+            dma((count - 1,)),
+            dma((count - 1,)),
+            dma((count + 1,)),
+            dma((count + 1,)),
+        ],
+        compiler_params=pltpu.CompilerParams(
+            collective_id=1, has_side_effects=True, vmem_limit_bytes=56 * 1024 * 1024
+        ),
+    )(blocks, small, *near, *far)
+    return (made[0], made[1], made[2:])
 
 
 def sequence_body(
@@ -894,6 +1390,7 @@
 ):
     section = lax.axis_index("section")
     tensor_index = lax.axis_index("tensor")
+    tensor_count = lax.axis_size("tensor")
     unit = lax.axis_index("dp")
     units = lax.axis_size("dp")
     decoder = section == 1
@@ -903,98 +1400,121 @@
     gains = norm_gain[0].astype(jnp.float32)
     shifts = norm_bias[0].astype(jnp.float32)
     down_shift = ffn_out_bias[0].astype(jnp.float32)
-    everyone = ("dp", "tensor")
-
-    def own_unit(array, axis):
+
+    def unit_of(array, axis, bits):
         size = array.shape[axis] // units
-        return lax.dynamic_slice_in_dim(array, unit * size, size, axis)
-
-    def gathered(rows):
-        return lax.all_gather(rows, everyone, axis=0, tiled=True)
-
-    def to_sequence(shards):
-        return lax.all_to_all(shards, "tensor", 0, 0, tiled=True).reshape(slots, width)
-
-    def to_shards(rows):
-        return lax.all_to_all(
-            rows.reshape(batches, shard_rows, width), "tensor", 0, 0, tiled=True
-        )
-
-    x = to_sequence(inputs[0])
-    head_units = cross_weight.shape[2] // (2 * HS) // units
-    qkv_rows = gathered(own_unit(qkv_weight[0], 1).T)
-    out_rows = gathered(own_unit(attn_out_weight[0], 0))
-    cross_unit = own_unit(cross_weight[0], 1).T.reshape(head_units, 2, HS, width)
-    cross_first = gathered(cross_unit[:, 0].reshape(head_units * HS, width))
-    cross_second = gathered(cross_unit[:, 1].reshape(head_units * HS, width))
-    in_rows = gathered(own_unit(ffn_in_weight[0], 1).T)
-    down_rows = gathered(own_unit(ffn_out_weight[0], 0))
-    in_shift = gathered(own_unit(ffn_in_bias[0], 0)[None]).reshape(-1).astype(jnp.float32)
+        piece = lax.dynamic_slice_in_dim(array, (unit ^ bits) * size, size, axis)
+        return piece.T if axis == 1 else piece
+
+    def units_of(bits):
+        return (
+            unit_of(qkv_weight[0], 1, bits),
+            unit_of(attn_out_weight[0], 0, bits),
+            unit_of(ffn_in_weight[0], 1, bits),
+            unit_of(ffn_out_weight[0], 0, bits),
+            unit_of(cross_weight[0], 1, bits).reshape(2, HS, width),
+            jnp.broadcast_to(unit_of(ffn_in_bias[0], 0, bits)[None], (16, bias_size)),
+        )
+
+    bias_size = ffn_in_bias.shape[1] // units
+    x, near, far = gather_all(inputs[0], units_of(0), units_of(2), (0, 0, 0, 0, 1, 0))
+    x = x.reshape(slots, width)
+    qkv_rows, out_rows, in_rows, down_rows = [
+        tuple(array.reshape(-1, width) for array in halves)
+        for halves in zip(near[:4], far[:4])
+    ]
+    cross_rows = tuple(array.reshape(2, -1, width) for array in (near[4], far[4]))
+    in_shift = tuple(
+        array[:, 0].reshape(-1).astype(jnp.float32) for array in (near[5], far[5])
+    )
 
     source_len = lax.dynamic_index_in_dim(lengths[0, :, 0], tensor_index, 0, keepdims=False)
     target_len = lax.dynamic_index_in_dim(lengths[1, :, 0], tensor_index, 0, keepdims=False)
     own_len = jnp.where(decoder, target_len, source_len)
     self_scalars = jnp.stack([own_len, decoder.astype(jnp.int32)])
     cross_scalars = jnp.stack([source_len, jnp.zeros_like(source_len)])
-
-    qkv = low(rows_nt(x, qkv_rows))
-    mixed, lse_self = self_attention(self_scalars, qkv)
+    sides = (0, 1)
+
+    qkv = [low(rows_nt(x, qkv_rows[side])) for side in sides]
+    mixed, lse_self = zip(*[self_attention(self_scalars, qkv[side]) for side in sides])
+    attn_sum = rows_nn(mixed[0], out_rows[0]) + rows_nn(mixed[1], out_rows[1])
     resid_a, norm_a, factor_a = layer_norm(
-        alpha * x.astype(jnp.float32) + rows_nn(mixed, out_rows), gains[0], shifts[0]
+        alpha * x.astype(jnp.float32) + attn_sum, gains[0], shifts[0]
     )
     a_low = low(resid_a)
-
-    wide = jnp.bfloat16
-    square = jnp.zeros((slots, width), wide)
-
-    query_sent = lax.cond(decoder, lambda: low(rows_nt(a_low, cross_first)), lambda: square)
-    query_held = lax.ppermute(query_sent, "section", [(1, 0)])
+    half_width = width // 2
+    half_zero = jnp.zeros((slots, half_width), jnp.bfloat16)
+
+    def zeros_like_of(branch):
+        shapes = jax.eval_shape(branch)
+        return lambda: jax.tree.map(lambda leaf: jnp.zeros(leaf.shape, leaf.dtype), shapes)
+
+    def dec_query():
+        return tuple(low(rows_nt(a_low, cross_rows[side][0])) for side in sides)
+
+    query_sent = lax.cond(decoder, dec_query, zeros_like_of(dec_query))
+    query_held = [lax.ppermute(piece, "section", [(1, 0)]) for piece in query_sent]
 
     def feed(rows_low, rows_wide, gain_row, shift_row):
-        pre_act = rows_nt(rows_low, in_rows) + in_shift
-        hidden = low(jax.nn.gelu(pre_act))
-        made = layer_norm(
-            alpha * rows_wide + rows_nn(hidden, down_rows) + down_shift, gain_row, shift_row
-        )
-        return (pre_act, hidden) + made
-
-    def feed_back(grad_sum, pre_act):
+        hidden, slopes, total = ([], [], alpha * rows_wide + down_shift)
+        for side in sides:
+            made, slope = gelu_and_slope(rows_nt(rows_low, in_rows[side]) + in_shift[side])
+            hidden.append(low(made))
+            slopes.append(low(slope))
+        for side in sides:
+            total = total + rows_nn(hidden[side], down_rows[side])
+        return (tuple(hidden), tuple(slopes)) + layer_norm(total, gain_row, shift_row)
+
+    def feed_back(grad_sum, slopes):
         grad_low = low(grad_sum)
-        grad_pre = low(rows_nt(grad_low, down_rows) * gelu_slope(pre_act))
-        return (grad_low, grad_pre, alpha * grad_sum + rows_nn(grad_pre, in_rows))
+        grad_pre = tuple(
+            low(rows_nt(grad_low, down_rows[side]) * slopes[side].astype(jnp.float32))
+            for side in sides
+        )
+        total = alpha * grad_sum
+        for side in sides:
+            total = total + rows_nn(grad_pre[side], in_rows[side])
+        return (grad_low, grad_pre, total)
 
     def enc_feed():
-        pre_act, hidden, memory, norm_y, factor_y = feed(a_low, resid_a, gains[2], shifts[2])
+        hidden, slopes, memory, norm_y, factor_y = feed(a_low, resid_a, gains[2], shifts[2])
         memory_low = low(memory)
-        keys_in = low(rows_nt(memory_low, cross_first))
-        values = low(rows_nt(memory_low, cross_second))
-        mixed_c, lse_c = cross_attention(cross_scalars, query_held, keys_in, values)
-        return (pre_act, hidden, memory_low, norm_y, factor_y, keys_in, values, mixed_c, lse_c)
-
-    def no_feed():
-        shapes = jax.eval_shape(enc_feed)
-        return jax.tree.map(lambda leaf: jnp.zeros(leaf.shape, leaf.dtype), shapes)
-
-    pre_e, hidden_e, memory_low, norm_e, factor_e, keys_in, values, mixed_c, lse_c = lax.cond(
-        decoder, no_feed, enc_feed
-    )
-    mixed_held = lax.ppermute(mixed_c, "section", [(0, 1)])
+        key_values = tuple(
+            low(rows_nt(memory_low, cross_rows[side].reshape(-1, width))) for side in sides
+        )
+        return (hidden, slopes, memory_low, norm_y, factor_y, key_values)
+
+    hidden_e, slopes_e, memory_low, norm_e, factor_e, key_values = lax.cond(
+        decoder, zeros_like_of(enc_feed), enc_feed
+    )
+
+    mixed_c, lse_c, mixed_held = ([], [], [])
+    for side in sides:
+
+        def enc_mix():
+            return tuple(cross_attention(cross_scalars, query_held[side], key_values[side]))
+
+        mix_made, lse_made = lax.cond(decoder, zeros_like_of(enc_mix), enc_mix)
+        mixed_c.append(mix_made)
+        lse_c.append(lse_made)
+        mixed_held.append(lax.ppermute(mix_made, "section", [(0, 1)]))
 
     own_pos = lax.broadcasted_iota(jnp.int32, (slots, 1), 0)
-    cotangent_rows = to_sequence(cotangent)
+    cotangent_rows = exchange(after(cotangent, qkv[0]), jnp.bfloat16).reshape(slots, width)
 
     def dec_middle():
-        resid_c, norm_c, factor_c = layer_norm(
-            alpha * resid_a + rows_nn(mixed_held, cross_second), gains[1], shifts[1]
-        )
+        crossed = rows_nn(mixed_held[0], cross_rows[0][1]) + rows_nn(
+            mixed_held[1], cross_rows[1][1]
+        )
+        resid_c, norm_c, factor_c = layer_norm(alpha * resid_a + crossed, gains[1], shifts[1])
         c_low = low(resid_c)
-        pre_act, hidden, decoded, norm_y, factor_y = feed(c_low, resid_c, gains[2], shifts[2])
+        hidden, slopes, decoded, norm_y, factor_y = feed(c_low, resid_c, gains[2], shifts[2])
         grad_top = jnp.where(own_pos < target_len, cotangent_rows.astype(jnp.float32), 0.0)
         grad_y, gain_y, shift_y = norm_back(grad_top, norm_y, factor_y, gains[2])
-        grad_low, grad_pre, grad_c = feed_back(grad_y, pre_act)
+        grad_low, grad_pre, grad_c = feed_back(grad_y, slopes)
         grad_mid, gain_c, shift_c = norm_back(grad_c, norm_c, factor_c, gains[1])
         mid_low = low(grad_mid)
-        grad_mixed_c = low(rows_nt(mid_low, cross_second))
+        grad_mixed_c = tuple(low(rows_nt(mid_low, cross_rows[side][1])) for side in sides)
         return (
             low(decoded),
             hidden,
@@ -1004,14 +1524,8 @@
             grad_mid,
             mid_low,
             grad_mixed_c,
-            (gain_c, gain_y),
-            (shift_c, shift_y),
-            jnp.sum(grad_y, axis=0),
-        )
-
-    def no_middle():
-        shapes = jax.eval_shape(dec_middle)
-        return jax.tree.map(lambda leaf: jnp.zeros(leaf.shape, leaf.dtype), shapes)
+            jnp.stack([gain_c, gain_y, shift_c, shift_y, jnp.sum(grad_y, axis=0)]),
+        )
 
     (
         decoded_low,
@@ -1022,127 +1536,158 @@
         grad_mid,
         mid_low,
         grad_mixed_c,
-        gains_d,
-        shifts_d,
-        down_shift_d,
-    ) = lax.cond(decoder, dec_middle, no_middle)
-    grad_mixed_held = lax.ppermute(grad_mixed_c, "section", [(1, 0)])
-    outputs = to_shards(jnp.where(decoder, decoded_low, memory_low))
-
-    def enc_cross():
-        return tuple(
-            cross_attention_back(
-                cross_scalars, query_held, keys_in, values, mixed_c, grad_mixed_held, lse_c
-            )
-        )
-
-    def no_cross():
-        return (square, square, square)
-
-    grad_query, grad_key, grad_value = lax.cond(decoder, no_cross, enc_cross)
-    grad_query_held = lax.ppermute(grad_query, "section", [(0, 1)])
+        vectors_d,
+    ) = lax.cond(decoder, dec_middle, zeros_like_of(dec_middle))
+    grad_mixed_held = [lax.ppermute(piece, "section", [(1, 0)]) for piece in grad_mixed_c]
+    grad_query_held, grad_kv = ([], [])
+    for side in sides:
+
+        def enc_cross():
+            return tuple(
+                cross_attention_back(
+                    cross_scalars,
+                    query_held[side],
+                    key_values[side],
+                    mixed_c[side],
+                    grad_mixed_held[side],
+                    lse_c[side],
+                )
+            )
+
+        query_made, kv_made = lax.cond(decoder, zeros_like_of(enc_cross), enc_cross)
+        grad_kv.append(kv_made)
+        grad_query_held.append(lax.ppermute(query_made, "section", [(0, 1)]))
 
     def enc_back():
-        grad_memory = rows_nn(grad_key, cross_first) + rows_nn(grad_value, cross_second)
+        grad_memory = None
+        for side in sides:
+            for part in range(2):
+                term = rows_nn(grad_kv[side][part], cross_rows[side][part])
+                grad_memory = term if grad_memory is None else grad_memory + term
         grad_y, gain_y, shift_y = norm_back(grad_memory, norm_e, factor_e, gains[2])
-        grad_low, grad_pre, grad_a = feed_back(grad_y, pre_e)
+        grad_low, grad_pre, grad_a = feed_back(grad_y, slopes_e)
         zero_row = jnp.zeros_like(gain_y)
-        return (
-            grad_low,
-            grad_pre,
-            hidden_e,
-            a_low,
-            grad_a,
-            (zero_row, gain_y),
-            (zero_row, shift_y),
-            jnp.sum(grad_y, axis=0),
-            grad_key,
-            memory_low,
-            grad_value,
-            memory_low,
-        )
+        rows = jnp.stack([zero_row, gain_y, zero_row, shift_y, jnp.sum(grad_y, axis=0)])
+        return (grad_low, grad_pre, grad_a, rows)
 
     def dec_back():
-        grad_a = alpha * grad_mid + rows_nn(grad_query_held, cross_first)
-        return (
-            grad_low_d,
-            grad_pre_d,
-            hidden_d,
-            c_low,
-            grad_a,
-            gains_d,
-            shifts_d,
-            down_shift_d,
-            grad_query_held,
-            a_low,
-            mixed_held,
-            mid_low,
-        )
-
-    (
-        grad_low,
-        grad_pre,
-        hidden,
-        feed_rows,
-        grad_a,
-        gain_cy,
-        shift_cy,
-        down_shift_step,
-        first_left,
-        first_right,
-        second_left,
-        second_right,
-    ) = lax.cond(decoder, dec_back, enc_back)
-
-    def summed(grad_rows_all, block):
-        scattered = lax.psum_scatter(
-            low(grad_rows_all), everyone, scatter_dimension=0, tiled=True
-        )
-        return lax.all_gather(scattered, "dp", axis=0, tiled=True).astype(jnp.float32)
-
-    first_grad = summed(rows_tn(first_left, first_right), HS)
-    second_grad = summed(rows_tn(second_left, second_right), HS)
-    down_grad = summed(rows_tn(hidden, grad_low), 0)
-    in_grad = summed(rows_tn(grad_pre, feed_rows), 0)
-    in_shift_grad = lax.psum_scatter(
-        jnp.sum(grad_pre.astype(jnp.float32), axis=0), everyone, scatter_dimension=0, tiled=True
-    )
-    in_shift_grad = lax.all_gather(in_shift_grad, "dp", axis=0, tiled=True)
+        grad_a = alpha * grad_mid
+        for side in sides:
+            grad_a = grad_a + rows_nn(grad_query_held[side], cross_rows[side][0])
+        return (grad_low_d, grad_pre_d, grad_a, vectors_d)
+
+    grad_low, grad_pre, grad_a, vectors = lax.cond(decoder, dec_back, enc_back)
+
+    outputs = exchange(
+        after(jnp.where(decoder, decoded_low, memory_low), grad_a).reshape(
+            batches, shard_rows, width
+        ),
+        jnp.bfloat16,
+    )
+
+    def cross_grads(side):
+        def enc():
+            return jnp.stack([low(rows_tn(grad_kv[side][part], memory_low)) for part in range(2)])
+
+        def dec():
+            return jnp.stack(
+                [
+                    low(rows_tn(grad_query_held[side], a_low)),
+                    low(rows_tn(mixed_held[side], mid_low)),
+                ]
+            )
+
+        return lax.cond(decoder, dec, enc)
+
+    def down_grads(side):
+        return lax.cond(
+            decoder,
+            lambda: low(rows_tn(hidden_d[side], grad_low)),
+            lambda: low(rows_tn(hidden_e[side], grad_low)),
+        )
+
+    def in_grads(side):
+        return lax.cond(
+            decoder,
+            lambda: low(rows_tn(grad_pre[side], c_low)),
+            lambda: low(rows_tn(grad_pre[side], a_low)),
+        )
+
+    def total_of(made):
+        far = made(1)
+        return (made(0), far)
+
+    down_made, in_made, cross_made = (
+        total_of(down_grads),
+        total_of(in_grads),
+        total_of(cross_grads),
+    )
 
     grad_r, gain_a, shift_a = norm_back(grad_a, norm_a, factor_a, gains[0])
     r_low = low(grad_r)
-    grad_mixed = low(rows_nt(r_low, out_rows))
-    out_grad = summed(rows_tn(mixed, r_low), 0)
-    grad_qkv = self_attention_back(self_scalars, qkv, mixed, grad_mixed, lse_self)
-    grad_x = alpha * grad_r + rows_nn(grad_qkv, qkv_rows)
-    input_grad = to_shards(low(grad_x)).astype(jnp.float32)
-    qkv_grad = summed(rows_tn(grad_qkv, x), 0)
-
-    vectors = lax.psum(
-        (
-            jnp.stack([gain_a, gain_cy[0], gain_cy[1]]),
-            jnp.stack([shift_a, shift_cy[0], shift_cy[1]]),
-            down_shift_step,
-        ),
-        everyone,
-    )
-    cross_grad = (
-        jnp.stack([first_grad.reshape(-1, HS, width), second_grad.reshape(-1, HS, width)], axis=1)
-        .reshape(-1, width)
-        .T
-    )
+    grad_mixed = [low(rows_nt(r_low, out_rows[side])) for side in sides]
+    out_made = total_of(lambda side: low(rows_tn(mixed[side], r_low)))
+    grad_qkv = [
+        self_attention_back(self_scalars, qkv[side], mixed[side], grad_mixed[side], lse_self[side])
+        for side in sides
+    ]
+    grad_x = alpha * grad_r
+    for side in sides:
+        grad_x = grad_x + rows_nn(grad_qkv[side], qkv_rows[side])
+    qkv_made = total_of(lambda side: low(rows_tn(grad_qkv[side], x)))
+
+    slot_bits = jnp.asarray([0, 2, 1, 3], jnp.int32)[:, None]
+    slot_unit = unit ^ slot_bits
+    slot_tensor = (tensor_index - lax.iota(jnp.int32, tensor_count)[None]) % tensor_count
+    slot_index = (slot_tensor * units + slot_unit).reshape(-1)
+    hot = (slot_index[None, :] == lax.iota(jnp.int32, slot_index.shape[0])[:, None]).astype(
+        jnp.float32
+    )
+    shift_rel = jnp.concatenate(
+        [jnp.sum(grad_pre[side].astype(jnp.float32), axis=0) for side in sides]
+    ).reshape(-1, bias_size)
+    shift_abs = jnp.dot(hot, shift_rel, precision=lax.Precision.HIGHEST).reshape(-1, width)
+    small = jnp.concatenate([jnp.stack([gain_a, shift_a]), vectors, shift_abs])
+    small = jnp.pad(small, ((0, -small.shape[0] % 8), (0, 0)))
+    made = (qkv_made, out_made, in_made, down_made, cross_made)
+    axes = (0, 0, 0, 0, 1)
+
+    def by_slot(array, axis):
+        shape = list(array.shape)
+        shape[axis : axis + 1] = [2 * tensor_count, shape[axis] // (2 * tensor_count)]
+        return array.reshape(shape)
+
+    input_rows, small, grads = reduce_all(
+        low(grad_x).reshape(batches, shard_rows, width),
+        small,
+        [by_slot(halves[0], axis) for halves, axis in zip(made, axes)],
+        [by_slot(halves[1], axis) for halves, axis in zip(made, axes)],
+        axes,
+    )
+    input_grad = input_rows.astype(jnp.float32)
+    qkv_grad, out_grad, in_grad, down_grad, cross_grad = [
+        array.astype(jnp.float32) for array in grads
+    ]
+    cross_grad = jnp.swapaxes(cross_grad, 0, 1)
+    in_shift_grad = lax.dynamic_index_in_dim(
+        small[7:11].reshape(tensor_count, -1), tensor_index, 0, keepdims=False
+    )
+
+    def columns(ordered):
+        return ordered.reshape(-1, width).T[None]
+
     return (
         outputs[None],
         input_grad[None],
-        qkv_grad.T[None],
-        out_grad[None],
-        cross_grad[None],
-        in_grad.T[None],
+        columns(qkv_grad),
+        out_grad.reshape(1, -1, width),
+        columns(cross_grad),
+        columns(in_grad),
         in_shift_grad[None],
-        down_grad[None],
-        vectors[2][None],
-        vectors[0][None],
-        vectors[1][None],
+        down_grad.reshape(1, -1, width),
+        small[6][None],
+        small[jnp.asarray([0, 2, 3])][None],
+        small[jnp.asarray([1, 4, 5])][None],
     )
 
 
@@ -1180,7 +1725,7 @@
         batches, sequences = arrays[1].shape[1:]
         heads = arrays[3].shape[2] // (3 * HS)
         group = sizes["dp"] * sizes["tensor"]
-        one_each = batches == sizes["tensor"] and sequences == sizes["dp"] and heads % group == 0
+        one_each = batches == sizes["tensor"] and sizes["dp"] == 4 and sequences == sizes["dp"] and heads % group == 0
         chosen = sequence_body if one_each else body
         return jax.shard_map(
             chosen, mesh=mesh, in_specs=placed, out_specs=returned, check_vma=False

time: 1670 us -> 1310 us (0.78)
  waiting for transfers between devices: 909 us -> 253 us
  Pallas kernels: 214 us -> 661 us
  blocking collectives: 168 us -> 0 us
  matrix products: 184 us -> 205 us
    pallas_call x0 -> x2, Pallas kernels: none -> 441 us  [the longest x1 267 us: reduce_all(): pl.pallas_call(functools.partial(reduce_kernel, axes, depths), in_specs=[...]
    reduce_scatter x6 -> x0, waiting for transfers between devices: 378 us -> none  [summed(): lax.psum_scatter(low(grad_rows_all), everyone, scatter_dimension=0, tiled...]
    all_gather x9 -> x0, waiting for transfers between devices: 197 us -> none  [the longest x6 157 us: gathered(): return lax.all_gather(rows, everyone, axis=0, tiled=True)]
    all_gather x5 -> x0, blocking collectives: 114 us -> none  [the longest x1 77.9 us: gathered(): return lax.all_gather(rows, everyone, axis=0, tiled=True)]
    all_to_all x4 -> x0, waiting for transfers between devices: 77 us -> none  [the longest x2 77 us: to_sequence(): lax.all_to_all(shards, 'tensor', 0, 0, tiled=True).reshape(slots, width)]
    unnamed x1 -> x0, blocking collectives: 54.5 us -> none
    ppermute x4 -> x14, starting transfers between devices: 8.06 us -> 27.5 us  [the longest x6 14.9 us: around(): lax.ppermute(value, 'tensor', [(i, (i + distance) % count) for i in range...]
    all_to_all x4 -> x0, starting transfers between devices: 18.8 us -> none  [the longest x2 10.8 us: to_sequence(): lax.all_to_all(shards, 'tensor', 0, 0, tiled=True).reshape(slots, width)]
  transfers between devices with their start and end apart: 23 -> 14, of which waited for: 16 -> 5; matrix products, arithmetic and copies ran while one was open for 11% -> 7% of each run, Pallas kernels for 5% -> 9%
where the time goes in v2:
time: 1310 us; the launch traced here: 1300 us
  Pallas kernels  661 us (50%)
  waiting for transfers between devices  253 us (19%)
  matrix products  205 us (16%)
  local copies, waits for them, and re-layouts  85.4 us (7%)
  other arithmetic  61 us (5%)
  starting transfers between devices  27.5 us (2%)
    pallas_call x1, Pallas kernels, reduce_all(): pl.pallas_call(functools.partial(reduce_kernel, axes, depths), in_specs=[...  267 us
    pallas_call x8, Pallas kernels, head_call(): pl.pallas_call(kernel, grid_spec=pltpu.PrefetchScalarGridSpec(num_scalar_...  220 us
    ppermute x4, waiting for transfers between devices, sequence_body(): lax.ppermute(piece, 'section', [(1, 0)])  174 us
    pallas_call x1, Pallas kernels, gather_all(): pl.pallas_call(functools.partial(gather_kernel, axes), in_specs=[anywhere...  174 us
    dot_general x12, matrix products, rows_nn(): return jnp.dot(rows, weight_rows, preferred_element_type=jnp.float32)  73.6 us
    dot_general x10, matrix products, rows_nt(): lax.dot_general(rows, weight_rows, COL_DIMS, preferred_element_type=jnp.f...  66.9 us
    dot_general x12, matrix products, rows_tn(): lax.dot_general(left_rows, right_rows, ROW_DIMS, preferred_element_type=j...  64.7 us
    ppermute x6, waiting for transfers between devices, around(): lax.ppermute(value, 'tensor', [(i, (i + distance) % count) for i in range...  63.7 us
  transfers between devices with their start and end apart: 14, of which 5 were waited for; matrix products, arithmetic and copies ran while one was open for 7% of the time, Pallas kernels for 9%

profile of v2, /device:TPU:9, one launch (start us, length us, event | category | flops | bytes accessed | tf_op | source)
XLA Modules:
  0.0 1305.0 jit_solution(17534264610730820348)
XLA Ops:
  14.7 173.7 %shard_map.230 = (bf16[4,256,1024]{2,1,0:T(8,128)(2,1)}, bf16[8,192,1024]{2,1,0:T(8,128)(2,1)}, bf16[8,64,1024]{2,1,0:T(8,128)(2,1)}, bf16[8,256,1024]{2,1,0:T(8...) custom-call(bf16[4,256,1024]{2,1,0:T(8,128)(2,1)} %bitcast.337, ...), custom_call_target="tpu_custom_call" | custom-call | tf_op jit(solution)/shard_map/pallas_call | solution.py:1085
  188.4 7.9 convolution_convert_fusion.24.packed_ref
  204.7 22.1 %shard_map.232 = (bf16[1024,512]{1,0:T(8,128)(2,1)S(1)}, f32[4,8,1024]{2,1,0:T(8,128)S(1)}) custom-call(s32[2]{0:T(128)S(1)} %pad_add_fusion.scalars, bf16[1024,1536]{1,0:T(8,128)(2,1)S(1)} %copy-done.6), custom_call_target="tpu_custom_call" | custom-call | flops 17179869184 | bytes 3145728 | tf_op jit(solution)/shard_map/pallas_call | solution.py:790
  226.9 22.1 %shard_map.231 = (bf16[1024,512]{1,0:T(8,128)(2,1)S(1)}, f32[4,8,1024]{2,1,0:T(8,128)S(1)}) custom-call(s32[2]{0:T(128)S(1)} %pad_add_fusion.scalars, bf16[1024,1536]{1,0:T(8,128)(2,1)S(1)} %copy-done.7), custom_call_target="tpu_custom_call" | custom-call | flops 17179869184 | bytes 3145728 | tf_op jit(solution)/shard_map/pallas_call | solution.py:790
  266.0 61.8 %conditional.15 = (bf16[1024,2048]{1,0:T(8,128)(2,1)}, bf16[1024,2048]{1,0:T(8,128)(2,1)}, bf16[1024,2048]{1,0:T(8,128)(2,1)}, bf16[1024,2048]{1,0:T(8,128)(2,1)...) conditional(s32[]{:T(128)} %convert_element_type.272, ...), branch_computations={%region_4.7_spmd, %region_7.8_spmd} | conditional | flops 21574453248 | bytes 157368512 | solution.py:1487
  266.0 13.8 %add_convert_fusion.1 = (bf16[1024,2048]{1,0:T(8,128)(2,1)}, bf16[1024,2048]{1,0:T(8,128)(2,1)S(1)}) fusion(f32[2048]{0:T(1024)S(1)} %get-tuple-element.383, bf16[1024,1024]{1,0:T(8,128)(2,1)S(1)} %get-tuple-element.381, bf16[2048,1024]{1,0:T(8,128)(2,1)} %get-tuple-element.382), kind=kOutput, calls=%fused_computation.9 | convolution fusion | flops 4336910336 | bytes 14688256 | tf_op jit(solution)/shard_map/cond/branch_0_fun/dot_general | solution.py:880
  279.8 6.1 fusion.70
  285.9 11.0 add_convert_fusion
  297.0 5.5 copy.97
  302.5 11.3 fusion.62
  329.2 23.2 %conditional.17 = ((bf16[1024,512]{1,0:T(8,128)(2,1)}, f32[4,8,1024]{2,1,0:T(8,128)S(1)})) conditional(s32[]{:T(128)} %convert_element_type.272, (s32[2]{0:T(128)S(1)}, bf16[1024,512]{1,0:T(8,128)(2,1)}, bf16[1024,1024]{1,0:T(8,128)(2,1)}) %tuple.131, () %tuple.132), branch_computations={%region_10.11_spmd, %region_11.12_spmd} | conditional | flops 17179869184 | bytes 5242888 | solution.py:1497
  329.2 23.2 %branch_0_fun.5 = (bf16[1024,512]{1,0:T(8,128)(2,1)}, f32[4,8,1024]{2,1,0:T(8,128)S(1)}) custom-call(s32[2]{0:T(128)S(1)} %get-tuple-element.398.scalars, bf16[1024,512]{1,0:T(8,128)(2,1)} %get-tuple-element.399.query_ref, bf16[1024,1024]{1,0:T(8,128)(2,1)} %get-tuple-element.400.key_ref.value_ref, bf16[1024,1024]{1,0:T(8,128)(2,1)} %get-tuple-element.400.key_ref.value_ref), custom_call_target="tpu_custom_call" | custom-call | flops 17179869184 | bytes 5242880 | tf_op jit(solution)/shard_map/cond/branch_0_fun/pallas_call | solution.py:790
  353.8 23.3 %conditional.16 = ((bf16[1024,512]{1,0:T(8,128)(2,1)}, f32[4,8,1024]{2,1,0:T(8,128)})) conditional(s32[]{:T(128)} %convert_element_type.272, (s32[2]{0:T(128)S(1)}, bf16[1024,512]{1,0:T(8,128)(2,1)}, bf16[1024,1024]{1,0:T(8,128)(2,1)}) %tuple.307, () %tuple.130), branch_computations={%region_8.9_spmd, %region_9.10_spmd} | conditional | flops 17179869184 | bytes 5242888 | solution.py:1497
  353.8 23.3 %branch_0_fun.4 = (bf16[1024,512]{1,0:T(8,128)(2,1)}, f32[4,8,1024]{2,1,0:T(8,128)}) custom-call(s32[2]{0:T(128)S(1)} %get-tuple-element.395.scalars, bf16[1024,512]{1,0:T(8,128)(2,1)} %get-tuple-element.396.query_ref, bf16[1024,1024]{1,0:T(8,128)(2,1)} %get-tuple-element.397.key_ref.value_ref, bf16[1024,1024]{1,0:T(8,128)(2,1)} %get-tuple-element.397.key_ref.value_ref), custom_call_target="tpu_custom_call" | custom-call | flops 17179869184 | bytes 5242880 | tf_op jit(solution)/shard_map/cond/branch_0_fun/pallas_call | solution.py:790
  380.6 11.5 collective-permute-start.4
  393.2 33.0 %collective-permute-done.4 = bf16[1,256,1024]{2,1,0:T(8,128)(2,1)} collective-permute-done((bf16[1,256,1024]{2,1,0:T(8,128)(2,1)}, bf16[1,256,1024]{2,1,0:T(8,128)(2,1)}, u32[]{:S(2)}, u32[]{:S(2)}) %collective-permute-start.4) | collective-permute-done | bytes 524320 | tf_op jit(solution)/shard_map/ppermute | solution.py:909
  426.2 11.2 collective-permute-done.5
  438.4 27.7 %conditional.18 = (bf16[1024,1024]{0,1:T(8,128)(2,1)}, bf16[1024,2048]{1,0:T(8,128)(2,1)}, bf16[1024,2048]{1,0:T(8,128)(2,1)}, bf16[1024,1024]{0,1:T(8,128)(2,1)...) conditional(s32[]{:T(128)} %convert_element_type.272, ...), branch_computations={%region_12.13_spmd, %region_13.27_spmd} | conditional | flops 38860226560 | bytes 509971552 | solution.py:1540
  468.8 174.3 %collective-permute-done.8 = bf16[1024,512]{1,0:T(8,128)(2,1)S(1)} collective-permute-done((bf16[1024,512]{1,0:T(8,128)(2,1)}, bf16[1024,512]{1,0:T(8,128)(2,1)S(1)}, u32[]{:S(2)}, u32[]{:S(2)}) %collective-permute-start.8) | collective-permute-done | bytes 1048608 | tf_op jit(solution)/shard_map/ppermute | solution.py:1541
  643.1 32.5 %conditional.20 = ((bf16[1024,512]{1,0:T(8,128)(2,1)}, bf16[2,1024,512]{2,1,0:T(8,128)(2,1)S(1)})) conditional(s32[]{:T(128)} %convert_element_type.272, (s32[2]{0:T(128)S(1)}, bf16[1024,512]{1,0:T(8,128)(2,1)}, bf16[1024,1024]{1,0:T(8,128)(2,1)}, bf16[1024,512]{1,0:T(8,128)(2,1)}, bf16[1024,512]{1,0:T(8,128)(2,1)S(1)}, ...), branch_computations={%region_29.30_spmd, %region_30.31_spmd} | conditional | flops 42949672960 | bytes 7405576 | solution.py:1557
  643.1 32.5 %branch_0_fun.7 = (bf16[1024,512]{1,0:T(8,128)(2,1)}, bf16[2,1024,512]{2,1,0:T(8,128)(2,1)S(1)}) custom-call(s32[2]{0:T(128)S(1)} %get-tuple-element.433.scalars, bf16[1024,512]{1,0:T(8,128)(2,1)} %get-tuple-element.434.query_ref, bf16[1024,1024]{1,0:T(8,128)(2,1)} %get-tuple-element.435.key_ref.value_ref, ...), custom_call_target="tpu_custom_call" | custom-call | flops 42949672960 | bytes 7405568 | tf_op jit(solution)/shard_map/cond/branch_0_fun/pallas_call | solution.py:790
  677.0 32.5 %conditional.19 = ((bf16[1024,512]{1,0:T(8,128)(2,1)}, bf16[2,1024,512]{2,1,0:T(8,128)(2,1)})) conditional(s32[]{:T(128)} %convert_element_type.272, (s32[2]{0:T(128)S(1)}, bf16[1024,512]{1,0:T(8,128)(2,1)}, bf16[1024,1024]{1,0:T(8,128)(2,1)}, bf16[1024,512]{1,0:T(8,128)(2,1)}, bf16[1024,512]{1,0:T(8,128)(2,1)}, ...), branch_computations={%region_27.28_spmd, %region_28.29_spmd} | conditional | flops 42949672960 | bytes 7405576 | solution.py:1557
  677.0 32.4 %branch_0_fun.6 = (bf16[1024,512]{1,0:T(8,128)(2,1)}, bf16[2,1024,512]{2,1,0:T(8,128)(2,1)}) custom-call(s32[2]{0:T(128)S(1)} %get-tuple-element.427.scalars, bf16[1024,512]{1,0:T(8,128)(2,1)} %get-tuple-element.428.query_ref, bf16[1024,1024]{1,0:T(8,128)(2,1)} %get-tuple-element.429.key_ref.value_ref, ...), custom_call_target="tpu_custom_call" | custom-call | flops 42949672960 | bytes 7405568 | tf_op jit(solution)/shard_map/cond/branch_0_fun/pallas_call | solution.py:790
  717.0 15.2 %collective-permute-done.9 = bf16[1024,512]{1,0:T(8,128)(2,1)} collective-permute-done((bf16[1024,512]{1,0:T(8,128)(2,1)}, bf16[1024,512]{1,0:T(8,128)(2,1)}, u32[]{:S(2)}, u32[]{:S(2)}) %collective-permute-start.9) | collective-permute-done | bytes 1048608 | tf_op jit(solution)/shard_map/ppermute | solution.py:1559
  732.2 65.2 %conditional.21 = (bf16[1024,1024]{1,0:T(8,128)(2,1)}, bf16[1024,2048]{1,0:T(8,128)(2,1)}, bf16[1024,2048]{1,0:T(8,128)(2,1)}, f32[1024,1024]{1,0:T(8,128)}, f32...) conditional(s32[]{:T(128)} %convert_element_type.272, (bf16[2,1024,512]{2,1,0:T(8,128)(2,1)S(1)}, ...), branch_computations={%region_31.38_spmd, %region_38.40_spmd} | conditional | flops 21509435392 | bytes 249676048 | solution.py:1579
  745.7 5.5 copy.103
  751.3 7.6 multiply_reduce_fusion.1
  765.6 8.7 multiply_convert_fusion.3
  774.2 6.6 fusion.71
  780.8 8.0 multiply_convert_fusion.2
  788.9 8.3 fusion.63
  797.5 13.7 %multiply_reduce_fusion.12 = (f32[1024]{0:T(1024)}, f32[1024]{0:T(1024)S(1)}, f32[1024]{0:T(1024)S(1)}) fusion(f32[1024,1024]{1,0:T(8,128)} %get-tuple-element.606, f32[1024,1024]{1,0:T(8,128)} %copy-done.8, f32[1024]{0:T(1024)S(1)} %copy-done.46, f32[1024]{0:T(1024)S(1)} %copy-done.44, f32[1024]{0:T(1024)S(1)} %bitcast.360), kind=kLoop, calls=%fused_computation.139 | loop fusion | flops 8385536 | bytes 8413184 | tf_op jit(solution)/shard_map/reduce_sum | solution.py:48
  828.5 32.0 %shard_map.233 = bf16[1024,1536]{1,0:T(8,128)(2,1)S(1)} custom-call(s32[2]{0:T(128)S(1)} %copy-done.5, bf16[1024,1536]{1,0:T(8,128)(2,1)} %convolution_convert_fusion.25.packed_ref, bf16[1024,512]{1,0:T(8,128)(2,1)S(1)} %copy-done.3, bf16[1024,512]{1,0:T(8,128)(2,1)S(1)} %convolution_convert_fusion.29.grad_ref, f32[4,8,1024]{2,1,0:T(8,128)S(1)} %get-tuple-element.608.lse_ref), custom_call_target="tpu_custom_call" | custom-call | flops 42949672960 | bytes 5308416 | tf_op jit(solution)/shard_map/pallas_call | solution.py:790
  870.4 32.1 %shard_map.234 = bf16[1024,1536]{1,0:T(8,128)(2,1)S(1)} custom-call(s32[2]{0:T(128)S(1)} %copy-done.5, bf16[1024,1536]{1,0:T(8,128)(2,1)} %convolution_convert_fusion.24.packed_ref, bf16[1024,512]{1,0:T(8,128)(2,1)S(1)} %copy-done.1, bf16[1024,512]{1,0:T(8,128)(2,1)S(1)} %convolution_convert_fusion.28.grad_ref, f32[4,8,1024]{2,1,0:T(8,128)S(1)} %get-tuple-element.609.lse_ref), custom_call_target="tpu_custom_call" | custom-call | flops 42949672960 | bytes 5308416 | tf_op jit(solution)/shard_map/pallas_call | solution.py:790
  907.7 7.8 conditional.27
  915.5 9.7 conditional.26
  915.5 9.5 convolution_convert_fusion.14
  925.2 9.9 conditional.25
  925.2 9.5 convolution_convert_fusion.12
  935.1 7.8 conditional.24
  942.9 9.6 conditional.23
  943.0 9.5 convolution_convert_fusion.6
  952.5 10.2 conditional.22
  952.7 9.5 convolution_convert_fusion.4
  962.7 7.9 add_convert_fusion.6
  971.3 267.2 %shard_map.235 = (bf16[4,256,1024]{2,1,0:T(8,128)(2,1)}, f32[16,1024]{1,0:T(8,128)}, bf16[4,192,1024]{2,1,0:T(8,128)(2,1)}, bf16[4,64,1024]{2,1,0:T(8,128)(2,1)}...) custom-call(bf16[4,256,1024]{2,1,0:T(8,128)(2,1)} %bitcast.345, ...), custom_call_target="tpu_custom_call" | custom-call | tf_op jit(solution)/shard_map/pallas_call | solution.py:1333
  1265.6 5.3 copy.115
  1281.3 19.5 %collective-permute-done.12 = bf16[1,256,1024]{2,1,0:T(8,128)(2,1)} collective-permute-done((bf16[1,256,1024]{2,1,0:T(8,128)(2,1)}, bf16[1,256,1024]{2,1,0:T(8,128)(2,1)}, u32[]{:S(2)}, u32[]{:S(2)}) %collective-permute-start.12) | collective-permute-done | bytes 524320 | tf_op jit(solution)/shard_map/ppermute | solution.py:909
  (285 shorter events, 204.0 us)
Async XLA Ops:
  4.1 8.7 copy-start.40
  188.4 7.9 copy-start.29
  188.4 7.9 copy-start.76
  204.7 22.1 %copy-start.4 = (s32[2]{0:T(128)}, s32[2]{0:T(128)S(1)}, u32[]{:S(2)}) copy-start(s32[2]{0:T(128)S(1)} %pad_add_fusion.scalars) | copy-start | bytes 28
  204.7 22.2 %copy-start.7 = (bf16[1024,1536]{1,0:T(8,128)(2,1)S(1)}, bf16[1024,1536]{1,0:T(8,128)(2,1)}, u32[]{:S(2)}) copy-start(bf16[1024,1536]{1,0:T(8,128)(2,1)} %convolution_convert_fusion.25.packed_ref) | copy-start | bytes 9437188
  226.9 26.4 %copy-start = (bf16[1024,512]{1,0:T(8,128)(2,1)}, bf16[1024,512]{1,0:T(8,128)(2,1)S(1)}, u32[]{:S(2)}) copy-start(bf16[1024,512]{1,0:T(8,128)(2,1)S(1)} %get-tuple-element.570.mixed_ref) | copy-start | bytes 3145732
  226.9 23.1 %copy-start.78 = (bf16[8,64,1024]{2,1,0:T(8,128)(2,1)S(1)}, bf16[8,64,1024]{2,1,0:T(8,128)(2,1)}, u32[]{:S(2)}) copy-start(bf16[8,64,1024]{2,1,0:T(8,128)(2,1)} %get-tuple-element.568) | copy-start | bytes 3145732
  262.6 66.1 %collective-permute-start.2 = (bf16[1024,512]{1,0:T(8,128)(2,1)S(1)}, bf16[1024,512]{1,0:T(8,128)(2,1)}, u32[]{:S(2)}, u32[]{:S(2)}) collective-permute-start(bf16[1024,512]{1,0:T(8,128)(2,1)S(1)} %get-tuple-element.583), channel_id=1, source_target_pairs={{16,0},{17,1},{18,2},{19,3},{20,4},{21,5},{22,6},{23,7},{24,8},{25... | collective-permute-start | bytes 3145736 | tf_op jit(solution)/shard_map/ppermute | solution.py:1456
  263.9 89.9 %collective-permute-start = (bf16[1024,512]{1,0:T(8,128)(2,1)}, bf16[1024,512]{1,0:T(8,128)(2,1)}, u32[]{:S(2)}, u32[]{:S(2)}) collective-permute-start(bf16[1024,512]{1,0:T(8,128)(2,1)} %get-tuple-element.574), channel_id=1, source_target_pairs={{16,0},{17,1},{18,2},{19,3},{20,4},{21,5},{22,6},{23,7},{24,8},{25... | collective-permute-start | bytes 3145736 | tf_op jit(solution)/shard_map/ppermute | solution.py:1456
  266.0 13.8 %copy-start.66 = (bf16[2048,1024]{1,0:T(8,128)(2,1)S(1)}, bf16[2048,1024]{1,0:T(8,128)(2,1)}, u32[]{:S(2)}) copy-start(bf16[2048,1024]{1,0:T(8,128)(2,1)} %get-tuple-element.389) | copy-start | bytes 12582916 | tf_op jit(solution)/shard_map/cond
  328.7 25.1 %copy-start.86 = (s32[2]{0:T(128)}, s32[2]{0:T(128)S(1)}, u32[]{:S(2)}) copy-start(s32[2]{0:T(128)S(1)} %pad_add_fusion.1) | copy-start | bytes 28
  352.4 85.0 %collective-permute-start.3 = (bf16[1024,512]{1,0:T(8,128)(2,1)}, bf16[1024,512]{1,0:T(8,128)(2,1)S(1)}, u32[]{:S(2)}, u32[]{:S(2)}) collective-permute-start(bf16[1024,512]{1,0:T(8,128)(2,1)} %get-tuple-element.585), channel_id=1, source_target_pairs={{0,16},{1,17},{2,18},{3,19},{4,20},{5,21},{6,22},{7,23},{8,24},{9,... | collective-permute-start | bytes 3145736 | tf_op jit(solution)/shard_map/ppermute | solution.py:1500
  353.8 25.6 %copy-start.21 = (bf16[4,256,1024]{2,1,0:T(8,128)(2,1)S(1)}, bf16[4,256,1024]{2,1,0:T(8,128)(2,1)}, u32[]{:S(2)}) copy-start(bf16[4,256,1024]{2,1,0:T(8,128)(2,1)} %param.45) | copy-start | bytes 6291460
  377.1 60.4 %collective-permute-start.1 = (bf16[1024,512]{1,0:T(8,128)(2,1)}, bf16[1024,512]{1,0:T(8,128)(2,1)}, u32[]{:S(2)}, u32[]{:S(2)}) collective-permute-start(bf16[1024,512]{1,0:T(8,128)(2,1)} %get-tuple-element.582), channel_id=1, source_target_pairs={{0,16},{1,17},{2,18},{3,19},{4,20},{5,21},{6,22},{7,23},{8,24},{9,... | collective-permute-start | bytes 3145736 | tf_op jit(solution)/shard_map/ppermute | solution.py:1500
  380.6 45.6 %collective-permute-start.4 = (bf16[1,256,1024]{2,1,0:T(8,128)(2,1)}, bf16[1,256,1024]{2,1,0:T(8,128)(2,1)}, u32[]{:S(2)}, u32[]{:S(2)}) collective-permute-start(bf16[1,256,1024]{2,1,0:T(8,128)(2,1)} %get-tuple-element.991), channel_id=1, source_target_pairs={{0,1},{1,2},{2,3},{3,0},{4,5},{5,6},{6,7},{7,4},{8,9},{9,10},{10,1... | collective-permute-start | bytes 1572872 | tf_op jit(solution)/shard_map/ppermute | solution.py:909
  392.0 45.4 %collective-permute-start.5 = (bf16[1,256,1024]{2,1,0:T(8,128)(2,1)}, bf16[1,256,1024]{2,1,0:T(8,128)(2,1)}, u32[]{:S(2)}, u32[]{:S(2)}) collective-permute-start(bf16[1,256,1024]{2,1,0:T(8,128)(2,1)} %get-tuple-element.990), channel_id=1, source_target_pairs={{0,2},{1,3},{2,0},{3,1},{4,6},{5,7},{6,4},{7,5},{8,10},{9,11},{10,... | collective-permute-start | bytes 1572872 | tf_op jit(solution)/shard_map/ppermute | solution.py:909
  392.0 45.4 %collective-permute-start.6 = (bf16[1,256,1024]{2,1,0:T(8,128)(2,1)}, bf16[1,256,1024]{2,1,0:T(8,128)(2,1)}, u32[]{:S(2)}, u32[]{:S(2)}) collective-permute-start(bf16[1,256,1024]{2,1,0:T(8,128)(2,1)} %get-tuple-element.989), channel_id=1, source_target_pairs={{0,3},{1,0},{2,1},{3,2},{4,7},{5,4},{6,5},{7,6},{8,11},{9,8},{10,9... | collective-permute-start | bytes 1572872 | tf_op jit(solution)/shard_map/ppermute | solution.py:909
  437.5 205.6 %copy-start.87 = (s32[2]{0:T(128)S(1)}, s32[2]{0:T(128)}, u32[]{:S(2)}) copy-start(s32[2]{0:T(128)} %copy-done.86) | copy-start | bytes 28
  466.2 176.9 %collective-permute-start.8 = (bf16[1024,512]{1,0:T(8,128)(2,1)}, bf16[1024,512]{1,0:T(8,128)(2,1)S(1)}, u32[]{:S(2)}, u32[]{:S(2)}) collective-permute-start(bf16[1024,512]{1,0:T(8,128)(2,1)} %get-tuple-element.592), channel_id=1, source_target_pairs={{16,0},{17,1},{18,2},{19,3},{20,4},{21,5},{22,6},{23,7},{24,8},{25... | collective-permute-start | bytes 3145736 | tf_op jit(solution)/shard_map/ppermute | solution.py:1541
  467.5 209.5 %collective-permute-start.7 = (bf16[1024,512]{1,0:T(8,128)(2,1)}, bf16[1024,512]{1,0:T(8,128)(2,1)}, u32[]{:S(2)}, u32[]{:S(2)}) collective-permute-start(bf16[1024,512]{1,0:T(8,128)(2,1)} %get-tuple-element.589), channel_id=1, source_target_pairs={{16,0},{17,1},{18,2},{19,3},{20,4},{21,5},{22,6},{23,7},{24,8},{25... | collective-permute-start | bytes 3145736 | tf_op jit(solution)/shard_map/ppermute | solution.py:1541
  675.6 41.4 %collective-permute-start.10 = (bf16[1024,512]{1,0:T(8,128)(2,1)}, bf16[1024,512]{1,0:T(8,128)(2,1)S(1)}, u32[]{:S(2)}, u32[]{:S(2)}) collective-permute-start(bf16[1024,512]{1,0:T(8,128)(2,1)} %get-tuple-element.601), channel_id=1, source_target_pairs={{0,16},{1,17},{2,18},{3,19},{4,20},{5,21},{6,22},{7,23},{8,24},{9,... | collective-permute-start | bytes 3145736 | tf_op jit(solution)/shard_map/ppermute | solution.py:1559
  677.0 35.0 %copy-start.62 = (s32[4]{0:T(128)S(1)}, s32[4]{0:T(128)}, u32[]{:S(2)}) copy-start(s32[4]{0:T(128)} %constant.285.clone) | copy-start | bytes 52
  677.0 35.7 %copy-start.61 = (s32[3]{0:T(128)S(1)}, s32[3]{0:T(128)}, u32[]{:S(2)}) copy-start(s32[3]{0:T(128)} %constant.309) | copy-start | bytes 40
  677.0 36.3 %copy-start.60 = (s32[3]{0:T(128)S(1)}, s32[3]{0:T(128)}, u32[]{:S(2)}) copy-start(s32[3]{0:T(128)} %constant.310) | copy-start | bytes 40
  709.5 22.7 %copy-start.23 = (bf16[2,8,64,1024]{3,2,1,0:T(8,128)(2,1)S(1)}, bf16[2,8,64,1024]{3,2,1,0:T(8,128)(2,1)}, u32[]{:S(2)}) copy-start(bf16[2,8,64,1024]{3,2,1,0:T(8,128)(2,1)} %get-tuple-element.573) | copy-start | bytes 6291460
  709.5 22.7 %copy-start.50 = (f32[1024,1]{0,1:T(1,128)S(1)}, f32[1024,1]{0,1:T(1,128)}, u32[]{:S(2)}) copy-start(f32[1024,1]{0,1:T(1,128)} %copy-done.49) | copy-start | bytes 12292
  709.5 22.7 %collective-permute-start.9 = (bf16[1024,512]{1,0:T(8,128)(2,1)}, bf16[1024,512]{1,0:T(8,128)(2,1)}, u32[]{:S(2)}, u32[]{:S(2)}) collective-permute-start(bf16[1024,512]{1,0:T(8,128)(2,1)} %get-tuple-element.600), channel_id=1, source_target_pairs={{0,16},{1,17},{2,18},{3,19},{4,20},{5,21},{6,22},{7,23},{8,24},{9,... | collective-permute-start | bytes 3145736 | tf_op jit(solution)/shard_map/ppermute | solution.py:1559
  712.7 19.5 %copy-start.83 = (bf16[2,1024,512]{2,1,0:T(8,128)(2,1)S(1)}, bf16[2,1024,512]{2,1,0:T(8,128)(2,1)}, u32[]{:S(2)}) copy-start(bf16[2,1024,512]{2,1,0:T(8,128)(2,1)} %get-tuple-element.591) | copy-start | bytes 6291460
  717.0 15.2 %copy-start.26 = (bf16[1024,512]{1,0:T(8,128)(2,1)}, bf16[1024,512]{1,0:T(8,128)(2,1)S(1)}, u32[]{:S(2)}) copy-start(bf16[1024,512]{1,0:T(8,128)(2,1)S(1)} %collective-permute-done.10) | copy-start | bytes 3145732
  732.2 65.3 %copy-start.44 = (f32[1024]{0:T(1024)S(1)}, f32[1024]{0:T(1024)}, u32[]{:S(2)}) copy-start(f32[1024]{0:T(1024)} %copy-done.43) | copy-start | bytes 12292
  732.2 65.3 %copy-start.46 = (f32[1024]{0:T(1024)S(1)}, f32[1024]{0:T(1024)}, u32[]{:S(2)}) copy-start(f32[1024]{0:T(1024)} %copy-done.45) | copy-start | bytes 12292
  732.2 65.3 %copy-start.48 = (f32[1,1,1024]{2,1,0:T(1,128)S(1)}, f32[1,1,1024]{2,1,0:T(1,128)}, u32[]{:S(2)}) copy-start(f32[1,1,1024]{2,1,0:T(1,128)} %copy-done.47) | copy-start | bytes 12292
  751.3 7.7 copy-start.15
  765.6 8.7 copy-start.65
  780.8 8.0 copy-start.17
  780.8 8.0 copy-start.72
  797.4 13.7 %copy-start.41 = (f32[5,1024]{1,0:T(8,128)}, f32[5,1024]{1,0:T(8,128)S(1)}, u32[]{:S(2)}) copy-start(f32[5,1024]{1,0:T(8,128)S(1)} %get-tuple-element.611) | copy-start | bytes 61444
  797.4 13.7 %copy-start.54 = (f32[1,1024]{1,0:T(1,128)}, f32[1,1024]{1,0:T(1,128)S(1)}, u32[]{:S(2)}) copy-start(f32[1,1024]{1,0:T(1,128)S(1)} %get-tuple-element.610) | copy-start | bytes 12292
  797.5 13.7 %copy-start.9 = (f32[1024,1024]{1,0:T(8,128)S(1)}, f32[1024,1024]{1,0:T(8,128)}, u32[]{:S(2)}) copy-start(f32[1024,1024]{1,0:T(8,128)} %copy-done.8) | copy-start | bytes 12582916
  828.5 32.0 %copy-start.30 = (bf16[4,256,1024]{2,1,0:T(8,128)(2,1)S(1)}, bf16[4,256,1024]{2,1,0:T(8,128)(2,1)}, u32[]{:S(2)}) copy-start(bf16[4,256,1024]{2,1,0:T(8,128)(2,1)} %get-tuple-element.565) | copy-start | bytes 6291460
  962.6 8.0 copy-start.42
  962.6 8.0 copy-start.53
  962.7 7.9 copy-start.55
  962.7 8.6 copy-start.19
  962.7 8.6 copy-start.20
  1254.8 24.6 %collective-permute-start.11 = (bf16[1,256,1024]{2,1,0:T(8,128)(2,1)}, bf16[1,256,1024]{2,1,0:T(8,128)(2,1)}, u32[]{:S(2)}, u32[]{:S(2)}) collective-permute-start(bf16[1,256,1024]{2,1,0:T(8,128)(2,1)} %get-tuple-element.988), channel_id=1, source_target_pairs={{0,1},{1,2},{2,3},{3,0},{4,5},{5,6},{6,7},{7,4},{8,9},{9,10},{10,1... | collective-permute-start | bytes 1572872 | tf_op jit(solution)/shard_map/ppermute | solution.py:909
  1258.1 42.7 %collective-permute-start.12 = (bf16[1,256,1024]{2,1,0:T(8,128)(2,1)}, bf16[1,256,1024]{2,1,0:T(8,128)(2,1)}, u32[]{:S(2)}, u32[]{:S(2)}) collective-permute-start(bf16[1,256,1024]{2,1,0:T(8,128)(2,1)} %get-tuple-element.987), channel_id=1, source_target_pairs={{0,2},{1,3},{2,0},{3,1},{4,6},{5,7},{6,4},{7,5},{8,10},{9,11},{10,... | collective-permute-start | bytes 1572872 | tf_op jit(solution)/shard_map/ppermute | solution.py:909
  1259.5 43.2 %collective-permute-start.13 = (bf16[1,256,1024]{2,1,0:T(8,128)(2,1)}, bf16[1,256,1024]{2,1,0:T(8,128)(2,1)}, u32[]{:S(2)}, u32[]{:S(2)}) collective-permute-start(bf16[1,256,1024]{2,1,0:T(8,128)(2,1)} %get-tuple-element.986), channel_id=1, source_target_pairs={{0,3},{1,0},{2,1},{3,2},{4,7},{5,4},{6,5},{7,6},{8,11},{9,8},{10,9... | collective-permute-start | bytes 1572872 | tf_op jit(solution)/shard_map/ppermute | solution.py:909
  (39 other events, 145.3 us)

commit v3 on v2

--- a/solution.py
+++ b/solution.py
@@ -20,6 +20,7 @@
 LANES = 2 * HS
 ROWS = 256
 CHUNK = 32
+BLOCK = 512
 MESH = pl.DeviceIdType.MESH
 SCALE = HS ** (-0.5)
 GELU_C = (2.0 / 3.141592653589793) ** 0.5
@@ -561,171 +562,258 @@
     )
 
 
-def split_lanes(rows):
-    return lax.broadcasted_iota(jnp.int32, (rows, 2 * HS), 1) < HS
+def lanes_of(rows):
+    return lax.broadcasted_iota(jnp.int32, (rows, LANES), 1)
 
 
 def swap_halves(tile):
-    return jnp.concatenate([tile[:, HS:], tile[:, :HS]], axis=1)
+    return pltpu.roll(tile, HS, 1)
 
 
 def pair_of(packed, left):
     first, second, third = (packed[:, :LANES], packed[:, LANES : 2 * LANES], packed[:, 2 * LANES :])
+    swap = lambda tile: jnp.concatenate([tile[:, HS:], tile[:, :HS]], axis=1)
     queries = jnp.where(left, first, second)
-    keys_in = jnp.where(left, swap_halves(first), swap_halves(third))
+    keys_in = jnp.where(left, swap(first), swap(third))
     values = jnp.where(left, second, third)
     return (queries, keys_in, values)
 
 
-def key_limit(position, length, causal):
-    return jnp.minimum(length, jnp.where(causal != 0, position + 1, position.dtype.type(1 << 20)))
-
-
-def attend_pair(scalars, queries_at, keys_in, values, mixed_ref, lse_ref, slots, left):
-    length, causal = (scalars[0], scalars[1])
-    zero = jnp.zeros((), keys_in.dtype)
-    key_halves = (jnp.where(left, keys_in, zero), jnp.where(left, zero, keys_in))
-    value_halves = (jnp.where(left, values, zero), jnp.where(left, zero, values))
-    left_block = split_lanes(ROWS)
-    key_pos = lax.broadcasted_iota(jnp.int32, (ROWS, slots), 1)
-
-    def block(index, carry):
-        first_row = pl.multiple_of(index * ROWS, ROWS)
-        queries = queries_at(first_row)
-        position = first_row + lax.broadcasted_iota(jnp.int32, (ROWS, 1), 0)
-        allowed = key_pos < key_limit(position, length, causal)
-        total, tops, sums = (None, [], [])
+def wide(value):
+    return value.astype(jnp.float32)
+
+
+def low(values):
+    return values.astype(jnp.bfloat16)
+
+
+def half_tiles(tile, fill_right, fill_left, left):
+    return (jnp.where(left, tile, fill_right), jnp.where(left, fill_left, tile))
+
+
+def key_tiles(keys_in, length, ones):
+    slots = keys_in.shape[0]
+    lane = lanes_of(slots)
+    hidden = lax.broadcasted_iota(jnp.int32, (slots, LANES), 0) >= length
+    left = lane < HS
+
+    def fill(start):
+        outside = jnp.where((lane == start) & hidden, NEG, 0.0)
+        return jnp.where((lane > start) & (lane <= start + ones), 1.0, outside)
+
+    first, second = half_tiles(wide(keys_in), fill(HS), fill(0), left)
+    return (low(first), low(second))
+
+
+def attend_forward(length, causal, queries_ref, key_refs, value_refs, mixed_ref, lse_ref):
+    slots = queries_ref.shape[0]
+    lane = lanes_of(ROWS)
+    left = lane < HS
+
+    def block(first_row, key_count, triangle):
+        queries = wide(queries_ref[pl.ds(first_row, ROWS), :]) * SCALE
+        query_halves = half_tiles(
+            queries, jnp.where(lane == HS, 1.0, 0.0), jnp.where(lane == 0, 1.0, 0.0), left
+        )
+        totals, tops = ([], [])
         for half in range(2):
-            raw = lax.dot_general(
-                queries, key_halves[half], COL_DIMS, preferred_element_type=jnp.float32
-            )
-            scores = jnp.where(allowed, raw * SCALE, NEG)
+            scores = lax.dot_general(
+                low(query_halves[half]),
+                key_refs[half][pl.ds(0, key_count), :],
+                COL_DIMS,
+                preferred_element_type=jnp.float32,
+            )
+            if triangle:
+                column = lax.broadcasted_iota(jnp.int32, (ROWS, key_count), 1)
+                row = first_row + lax.broadcasted_iota(jnp.int32, (ROWS, key_count), 0)
+                scores = jnp.where(column <= row, scores, NEG)
             top = jnp.max(scores, axis=1, keepdims=True)
-            expo = jnp.exp(scores - top)
             tops.append(top)
-            sums.append(jnp.sum(expo, axis=1, keepdims=True))
-            part = jnp.dot(
-                expo.astype(jnp.bfloat16), value_halves[half], preferred_element_type=jnp.float32
-            )
-            total = part if half == 0 else total + part
-        norm = jnp.where(left_block, sums[0], sums[1])
-        mixed_ref[pl.ds(first_row, ROWS), :] = (total / norm).astype(jnp.bfloat16)
-        logs = jnp.where(left_block, tops[0] + jnp.log(sums[0]), tops[1] + jnp.log(sums[1]))
-        lse_ref[0, :, pl.ds(first_row, ROWS)] = jnp.transpose(logs)[HS - 4 : HS + 4]
-        return carry
-
-    lax.fori_loop(0, slots // ROWS, block, 0)
-
-
-def self_forward_kernel(scalars, packed_ref, mixed_ref, lse_ref, queries_ref):
-    slots = packed_ref.shape[0]
-    left = split_lanes(slots)
+            totals.append(
+                jnp.dot(
+                    low(jnp.exp(scores - top)),
+                    value_refs[half][pl.ds(0, key_count), :],
+                    preferred_element_type=jnp.float32,
+                )
+            )
+        norm = swap_halves(jnp.where(left, totals[1], totals[0]))
+        mixed_ref[pl.ds(first_row, ROWS), :] = low(jnp.where(left, totals[0], totals[1]) / norm)
+        logs = jnp.where(left, tops[0], tops[1]) + jnp.log(norm)
+        lse_ref[pl.ds(first_row, ROWS), :] = swap_halves(logs)
+
+    @pl.when(causal == 0)
+    def _():
+        def step(index, carry):
+            block(pl.multiple_of(index * ROWS, ROWS), slots, False)
+            return carry
+
+        lax.fori_loop(0, slots // ROWS, step, 0)
+
+    @pl.when(causal != 0)
+    def _():
+        for first_row in range(0, slots, ROWS):
+            block(first_row, first_row + ROWS, True)
+
+
+def fill_forward(length, keys_in, values, key_refs, value_refs):
+    left = lanes_of(keys_in.shape[0]) < HS
+    for ref, tile in zip(key_refs, key_tiles(keys_in, length, 0)):
+        ref[...] = tile
+    one = jnp.ones((), values.dtype)
+    for ref, tile in zip(value_refs, half_tiles(values, one, one, left)):
+        ref[...] = tile
+
+
+def self_forward_kernel(scalars, packed_ref, mixed_ref, lse_ref, queries_ref, k0, k1, v0, v1):
+    left = lanes_of(packed_ref.shape[0]) < HS
     queries, keys_in, values = pair_of(packed_ref[...], left)
     queries_ref[...] = queries
-    attend_pair(
-        scalars,
-        lambda row: queries_ref[pl.ds(row, ROWS), :],
-        keys_in,
-        values,
-        mixed_ref,
-        lse_ref,
-        slots,
-        left,
-    )
-
-
-def cross_forward_kernel(scalars, query_ref, key_ref, value_ref, mixed_ref, lse_ref):
-    slots = query_ref.shape[0]
-    attend_pair(
-        scalars,
-        lambda row: query_ref[pl.ds(row, ROWS), :],
-        key_ref[...],
-        value_ref[...],
-        mixed_ref,
-        lse_ref,
-        slots,
-        split_lanes(slots),
-    )
-
-
-def attend_pair_back(
-    scalars, queries_at, keys_in, values, mixed_ref, grad_ref, lse_ref, put_query, key_acc, value_acc
+    fill_forward(scalars[0], keys_in, values, (k0, k1), (v0, v1))
+    attend_forward(scalars[0], scalars[1], queries_ref, (k0, k1), (v0, v1), mixed_ref, lse_ref)
+
+
+def cross_forward_kernel(
+    scalars, query_ref, key_ref, value_ref, mixed_ref, lse_ref, k0, k1, v0, v1
 ):
-    length, causal = (scalars[0], scalars[1])
-    slots = keys_in.shape[0]
-    left = split_lanes(slots)
-    left_block = split_lanes(ROWS)
-    zero = jnp.zeros((), keys_in.dtype)
-    key_halves = (jnp.where(left, keys_in, zero), jnp.where(left, zero, keys_in))
-    value_halves = (jnp.where(left, values, zero), jnp.where(left, zero, values))
-    key_pos = lax.broadcasted_iota(jnp.int32, (slots, ROWS), 0)
+    fill_forward(scalars[0], key_ref[...], value_ref[...], (k0, k1), (v0, v1))
+    attend_forward(scalars[0], 0, query_ref, (k0, k1), (v0, v1), mixed_ref, lse_ref)
+
+
+def attend_backward(
+    causal, queries_ref, key_refs, plain_refs, value_refs, mixed_ref, grad_ref, lse_ref, outs
+):
+    dq_ref, key_acc, value_acc = outs
+    slots = queries_ref.shape[0]
+    lane = lanes_of(ROWS)
+    left = lane < HS
     key_acc[...] = jnp.zeros_like(key_acc)
     value_acc[...] = jnp.zeros_like(value_acc)
 
-    def block(index, carry):
-        first_row = pl.multiple_of(index * ROWS, ROWS)
-        queries = queries_at(first_row)
-        grads = grad_ref[pl.ds(first_row, ROWS), :]
-        mixed = mixed_ref[pl.ds(first_row, ROWS), :]
-        product = jnp.transpose(grads.astype(jnp.float32) * mixed.astype(jnp.float32))
-        position = first_row + lax.broadcasted_iota(jnp.int32, (1, ROWS), 1)
-        allowed = key_pos < key_limit(position, length, causal)
-        logs = lse_ref[0, :, pl.ds(first_row, ROWS)]
-        query_total = None
+    def extra(start, terms, one):
+        filled = jnp.where(lane == start, one, 0.0)
+        for number, term in enumerate(terms):
+            filled = jnp.where(lane == start + 1 + number, -term, filled)
+        return filled
+
+    def parts(value, count):
+        found = []
+        for _ in range(count):
+            found.append(wide(low(value)))
+            value = value - found[-1]
+        return found
+
+    def block(first_row, key_count, triangle):
+        rows = pl.ds(first_row, ROWS)
+        keys = pl.ds(0, key_count)
+        queries = wide(queries_ref[rows, :]) * SCALE
+        grads = wide(grad_ref[rows, :])
+        product = grads * wide(mixed_ref[rows, :])
+        log_parts = parts(lse_ref[rows, :], 3)
+        query_total, key_total, value_total = (None, None, None)
         for half in range(2):
-            mine = left_block if half == 0 else jnp.logical_not(left_block)
-            query_half = jnp.where(mine, queries, zero)
-            grad_half = jnp.where(mine, grads, zero)
-            raw = lax.dot_general(
-                key_halves[half], queries, COL_DIMS, preferred_element_type=jnp.float32
-            )
-            scores = jnp.where(allowed, raw * SCALE, NEG)
-            probs = jnp.exp(scores - logs[3 + half : 4 + half])
+            mine = left if half == 0 else jnp.logical_not(left)
+            start = HS if half == 0 else 0
+            delta = jnp.sum(jnp.where(mine, product, 0.0), axis=1, keepdims=True)
+            query_aug = low(jnp.where(mine, queries, extra(start, log_parts, 1.0)))
+            grad_aug = low(jnp.where(mine, grads, extra(start, parts(delta, 2), 0.0)))
+            scores = lax.dot_general(
+                key_refs[half][keys, :], query_aug, COL_DIMS, preferred_element_type=jnp.float32
+            )
+            probs = jnp.exp(scores)
+            if triangle:
+                key_pos = lax.broadcasted_iota(jnp.int32, (key_count, ROWS), 0)
+                position = first_row + lax.broadcasted_iota(jnp.int32, (key_count, ROWS), 1)
+                probs = jnp.where(key_pos <= position, probs, 0.0)
             grad_probs = lax.dot_general(
-                value_halves[half], grads, COL_DIMS, preferred_element_type=jnp.float32
-            )
-            delta = jnp.sum(product[half * HS : half * HS + HS], axis=0, keepdims=True)
-            grad_raw = (probs * (grad_probs - delta) * SCALE).astype(jnp.bfloat16)
-            value_acc[...] += jnp.dot(
-                probs.astype(jnp.bfloat16), grad_half, preferred_element_type=jnp.float32
-            )
-            key_acc[...] += jnp.dot(grad_raw, query_half, preferred_element_type=jnp.float32)
-            part = lax.dot_general(
-                grad_raw, key_halves[half], ROW_DIMS, preferred_element_type=jnp.float32
-            )
-            query_total = part if half == 0 else query_total + part
-        put_query(first_row, query_total.astype(jnp.bfloat16))
-        return carry
-
-    lax.fori_loop(0, slots // ROWS, block, 0)
+                value_refs[half][keys, :], grad_aug, COL_DIMS, preferred_element_type=jnp.float32
+            )
+            grad_raw = low(probs * grad_probs)
+            value_part = jnp.dot(
+                low(probs), low(jnp.where(mine, grads, 0.0)), preferred_element_type=jnp.float32
+            )
+            key_part = jnp.dot(
+                grad_raw, low(jnp.where(mine, queries, 0.0)), preferred_element_type=jnp.float32
+            )
+            query_part = lax.dot_general(
+                grad_raw, plain_refs[half][keys, :], ROW_DIMS, preferred_element_type=jnp.float32
+            )
+            if half == 0:
+                query_total, key_total, value_total = (query_part, key_part, value_part)
+            else:
+                query_total = query_total + query_part
+                key_total = key_total + key_part
+                value_total = value_total + value_part
+        value_acc[keys, :] += value_total
+        key_acc[keys, :] += key_total
+        dq_ref[rows, :] = low(query_total)
+
+    @pl.when(causal == 0)
+    def _():
+        def step(index, carry):
+            block(pl.multiple_of(index * ROWS, ROWS), slots, False)
+            return carry
+
+        lax.fori_loop(0, slots // ROWS, step, 0)
+
+    @pl.when(causal != 0)
+    def _():
+        for first_row in range(0, slots, ROWS):
+            block(first_row, first_row + ROWS, True)
+
+
+def fill_backward(length, keys_in, values, key_refs, plain_refs, value_refs):
+    lane = lanes_of(keys_in.shape[0])
+    left = lane < HS
+    for ref, tile in zip(key_refs, key_tiles(keys_in, length, 3)):
+        ref[...] = tile
+    zero = jnp.zeros((), jnp.float32)
+    for ref, tile in zip(plain_refs, half_tiles(wide(keys_in) * SCALE, zero, zero, left)):
+        ref[...] = low(tile)
+
+    def ones(start):
+        return jnp.where((lane > start) & (lane <= start + 2), 1.0, 0.0)
+
+    for ref, tile in zip(value_refs, half_tiles(wide(values), ones(HS), ones(0), left)):
+        ref[...] = low(tile)
 
 
 def self_backward_kernel(
-    scalars, packed_ref, mixed_ref, grad_ref, lse_ref, out_ref, queries_ref, dq_ref, key_acc, value_acc
+    scalars,
+    packed_ref,
+    mixed_ref,
+    grad_ref,
+    lse_ref,
+    out_ref,
+    queries_ref,
+    dq_ref,
+    key_acc,
+    value_acc,
+    k0,
+    k1,
+    p0,
+    p1,
+    v0,
+    v1,
 ):
     slots = packed_ref.shape[0]
-    left = split_lanes(slots)
+    left = lanes_of(slots) < HS
     queries, keys_in, values = pair_of(packed_ref[...], left)
     queries_ref[...] = queries
-
-    def put_query(row, block):
-        dq_ref[pl.ds(row, ROWS), :] = block
-
-    attend_pair_back(
-        scalars,
-        lambda row: queries_ref[pl.ds(row, ROWS), :],
-        keys_in,
-        values,
+    fill_backward(scalars[0], keys_in, values, (k0, k1), (p0, p1), (v0, v1))
+    attend_backward(
+        scalars[1],
+        queries_ref,
+        (k0, k1),
+        (p0, p1),
+        (v0, v1),
         mixed_ref,
         grad_ref,
         lse_ref,
-        put_query,
-        key_acc,
-        value_acc,
+        (dq_ref, key_acc, value_acc),
     )
     grad_query = dq_ref[...]
-    grad_key = swap_halves(key_acc[...].astype(jnp.bfloat16))
-    grad_value = value_acc[...].astype(jnp.bfloat16)
+    grad_key = low(swap_halves(key_acc[...]))
+    grad_value = low(value_acc[...])
     out_ref[:, :LANES] = jnp.where(left, grad_query, grad_key)
     out_ref[:, LANES : 2 * LANES] = jnp.where(left, grad_value, grad_query)
     out_ref[:, 2 * LANES :] = jnp.where(left, grad_key, grad_value)
@@ -743,58 +831,48 @@
     dkv_ref,
     key_acc,
     value_acc,
+    k0,
+    k1,
+    p0,
+    p1,
+    v0,
+    v1,
 ):
-    def put_query(row, block):
-        dq_ref[pl.ds(row, ROWS), :] = block
-
-    attend_pair_back(
-        scalars,
-        lambda row: query_ref[pl.ds(row, ROWS), :],
-        key_ref[...],
-        value_ref[...],
+    fill_backward(scalars[0], key_ref[...], value_ref[...], (k0, k1), (p0, p1), (v0, v1))
+    attend_backward(
+        0,
+        query_ref,
+        (k0, k1),
+        (p0, p1),
+        (v0, v1),
         mixed_ref,
         grad_ref,
         lse_ref,
-        put_query,
-        key_acc,
-        value_acc,
-    )
-    dkv_ref[0] = key_acc[...].astype(jnp.bfloat16)
-    dkv_ref[1] = value_acc[...].astype(jnp.bfloat16)
-
-
-def head_call(kernel, scalars, pairs, blocks, outs, scratch, lse_in, lse_out):
+        (dq_ref, key_acc, value_acc),
+    )
+    dkv_ref[:, :LANES] = low(key_acc[...])
+    dkv_ref[:, LANES:] = low(value_acc[...])
+
+
+def head_call(kernel, scalars, pairs, blocks, outs, scratch, products):
     slots = blocks[0][0].shape[0]
 
-    def spec(width, shift):
-        return pl.BlockSpec((slots, width), lambda pair, *_: (0, pair + shift))
-
-    lse_spec = pl.BlockSpec((1, 8, slots), lambda pair, *_: (pair, 0, 0))
-    in_specs = [spec(width, shift) for _, width, shift in blocks]
-    operands = [array for array, _, _ in blocks]
-    if lse_in is not None:
-        in_specs.append(lse_spec)
-        operands.append(lse_in)
+    def spec(width, shift, stride):
+        return pl.BlockSpec((slots, width), lambda pair, *_: (0, stride * pair + shift))
+
     out_specs, out_shape = ([], [])
-    for stacked, width in outs:
-        if stacked:
-            out_specs.append(pl.BlockSpec((2, slots, width), lambda pair, *_: (0, 0, pair)))
-            out_shape.append(jax.ShapeDtypeStruct((2, slots, pairs * width), jnp.bfloat16))
-        else:
-            out_specs.append(spec(width, 0))
-            out_shape.append(jax.ShapeDtypeStruct((slots, pairs * width), jnp.bfloat16))
-    if lse_out:
-        out_specs.append(lse_spec)
-        out_shape.append(jax.ShapeDtypeStruct((pairs, 8, slots), jnp.float32))
-    products = 2 if lse_in is None else 5
+    for kind, width in outs:
+        out_specs.append(spec(width, 0, 1))
+        made = jnp.float32 if kind == "wide" else jnp.bfloat16
+        out_shape.append(jax.ShapeDtypeStruct((slots, pairs * width), made))
     return pl.pallas_call(
         kernel,
         grid_spec=pltpu.PrefetchScalarGridSpec(
             num_scalar_prefetch=1,
             grid=(pairs,),
-            in_specs=in_specs,
+            in_specs=[spec(width, shift, stride) for _, width, shift, stride in blocks],
             out_specs=out_specs,
-            scratch_shapes=scratch,
+            scratch_shapes=[pltpu.VMEM((slots, LANES), kind) for kind in scratch],
         ),
         out_shape=out_shape,
         compiler_params=pltpu.CompilerParams(
@@ -802,77 +880,77 @@
         ),
         cost_estimate=pl.CostEstimate(
             flops=products * pairs * slots * slots * LANES * 16,
-            bytes_accessed=2 * sum(array.size for array in operands),
+            bytes_accessed=2 * slots * pairs * sum(block[1] for block in blocks),
             transcendentals=2 * pairs * slots * slots,
         ),
-    )(scalars, *operands)
-
-
-def self_attention(scalars, packed):
-    slots = packed.shape[0]
+    )(scalars, *[block[0] for block in blocks])
+
+
+BF16 = jnp.bfloat16
+F32 = jnp.float32
+
+
+def self_attention(scalars, packed, first, pairs):
     return head_call(
         self_forward_kernel,
         scalars,
-        packed.shape[1] // (3 * LANES),
-        [(packed, 3 * LANES, 0)],
-        [(False, LANES)],
-        [pltpu.VMEM((slots, LANES), jnp.bfloat16)],
-        None,
-        True,
-    )
-
-
-def cross_attention(scalars, queries, key_values):
-    pairs = queries.shape[1] // LANES
+        pairs,
+        [(packed, 3 * LANES, first, 1)],
+        [("low", LANES), ("wide", LANES)],
+        [BF16] * 5,
+        2,
+    )
+
+
+def cross_attention(scalars, queries, key_values, first, pairs):
     return head_call(
         cross_forward_kernel,
         scalars,
         pairs,
-        [(queries, LANES, 0), (key_values, LANES, 0), (key_values, LANES, pairs)],
-        [(False, LANES)],
-        [],
-        None,
-        True,
-    )
-
-
-def self_attention_back(scalars, packed, mixed, grads, lse):
-    slots = packed.shape[0]
+        [
+            (queries, LANES, 0, 1),
+            (key_values, LANES, 2 * first, 2),
+            (key_values, LANES, 2 * first + 1, 2),
+        ],
+        [("low", LANES), ("wide", LANES)],
+        [BF16] * 4,
+        2,
+    )
+
+
+def self_attention_back(scalars, packed, mixed, grads, lse, first, pairs):
     return head_call(
         self_backward_kernel,
         scalars,
-        packed.shape[1] // (3 * LANES),
-        [(packed, 3 * LANES, 0), (mixed, LANES, 0), (grads, LANES, 0)],
-        [(False, 3 * LANES)],
+        pairs,
         [
-            pltpu.VMEM((slots, LANES), jnp.bfloat16),
-            pltpu.VMEM((slots, LANES), jnp.bfloat16),
-            pltpu.VMEM((slots, LANES), jnp.float32),
-            pltpu.VMEM((slots, LANES), jnp.float32),
+            (packed, 3 * LANES, first, 1),
+            (mixed, LANES, first, 1),
+            (grads, LANES, first, 1),
+            (lse, LANES, first, 1),
         ],
-        lse,
-        False,
+        [("low", 3 * LANES)],
+        [BF16, BF16, F32, F32] + [BF16] * 6,
+        5,
     )[0]
 
 
-def cross_attention_back(scalars, queries, key_values, mixed, grads, lse):
-    slots = queries.shape[0]
-    pairs = queries.shape[1] // LANES
+def cross_attention_back(scalars, queries, key_values, mixed, grads, lse, first, pairs):
     return head_call(
         cross_backward_kernel,
         scalars,
         pairs,
         [
-            (queries, LANES, 0),
-            (key_values, LANES, 0),
-            (key_values, LANES, pairs),
-            (mixed, LANES, 0),
-            (grads, LANES, 0),
+            (queries, LANES, 0, 1),
+            (key_values, LANES, 2 * first, 2),
+            (key_values, LANES, 2 * first + 1, 2),
+            (mixed, LANES, 0, 1),
+            (grads, LANES, 0, 1),
+            (lse, LANES, 0, 1),
         ],
-        [(False, LANES), (True, LANES)],
-        [pltpu.VMEM((slots, LANES), jnp.float32), pltpu.VMEM((slots, LANES), jnp.float32)],
-        lse,
-        False,
+        [("low", LANES), ("low", 2 * LANES)],
+        [F32, F32] + [BF16] * 6,
+        5,
     )
 
 
@@ -886,45 +964,211 @@
 
 def rows_tn(left_rows, right_rows):
     return lax.dot_general(left_rows, right_rows, ROW_DIMS, preferred_element_type=jnp.float32)
-
-
-def low(values):
-    return values.astype(jnp.bfloat16)
 
 
 def gelu_and_slope(values):
     square = values * values
     bend = jnp.tanh(GELU_C * values * (1.0 + 0.044715 * square))
     rise = GELU_C * (1.0 + 3 * 0.044715 * square)
-    gate = 0.5 * (1.0 + bend)
-    return (values * gate, gate + 0.5 * values * (1.0 - bend * bend) * rise)
-
-
-def after(value, *earlier):
-    return lax.optimization_barrier((value, earlier))[0]
-
-
-def around(value, distance):
-    count = lax.axis_size("tensor")
-    return lax.ppermute(value, "tensor", [(i, (i + distance) % count) for i in range(count)])
-
-
-def partner(value, bit):
-    return lax.ppermute(value, "dp", [(i, i ^ bit) for i in range(lax.axis_size("dp"))])
-
-
-def exchange(blocks, store_type):
-    count = lax.axis_size("tensor")
-    place = lax.axis_index("tensor")
-    arrived = [lax.dynamic_index_in_dim(blocks, place, 0)]
-    for distance in range(1, count):
-        sent = lax.dynamic_index_in_dim(blocks, (place + distance) % count, 0)
-        arrived.append(around(sent, distance))
-    placed = jnp.zeros(blocks.shape, store_type)
-    for distance in range(count):
-        block = arrived[distance].astype(store_type)
-        placed = lax.dynamic_update_slice_in_dim(placed, block, (place - distance) % count, 0)
-    return placed
+    gate = 0.5 + 0.5 * bend
+    return (values * gate, gate * (1.0 + values * (1.0 - bend) * rise))
+
+
+def feed_kernel(
+    alpha_ref,
+    low_ref,
+    wide_ref,
+    in_ref,
+    bias_ref,
+    down_ref,
+    down_shift_ref,
+    gain_ref,
+    shift_ref,
+    hidden_ref,
+    slope_ref,
+    made_ref,
+    norm_ref,
+    factor_ref,
+    acc,
+):
+    step = pl.program_id(0)
+    slots = low_ref.shape[0]
+
+    @pl.when(step == 0)
+    def _():
+        acc[...] = alpha_ref[0] * wide_ref[...] + down_shift_ref[...]
+
+    for first in range(0, slots, ROWS):
+        rows = pl.ds(first, ROWS)
+        pre_act = rows_nt(low_ref[rows, :], in_ref[...]) + bias_ref[...]
+        made, slope = gelu_and_slope(pre_act)
+        hidden = low(made)
+        hidden_ref[rows, :] = hidden
+        slope_ref[rows, :] = low(slope)
+        acc[rows, :] += rows_nn(hidden, down_ref[...])
+
+    @pl.when(step == pl.num_programs(0) - 1)
+    def _():
+        for first in range(0, slots, ROWS):
+            rows = pl.ds(first, ROWS)
+            made, normed, factor = layer_norm(acc[rows, :], gain_ref[...], shift_ref[...])
+            made_ref[rows, :] = low(made)
+            norm_ref[rows, :] = normed
+            factor_ref[rows, :] = factor
+
+
+def whole_spec(shape):
+    return pl.BlockSpec(shape, lambda *_: (0,) * len(shape))
+
+
+def feed_call(alpha, rows_low, rows_wide, in_rows, in_shift, down_rows, down_shift, gain, shift):
+    slots, width = rows_low.shape
+    hidden = in_rows.shape[0]
+    block = min(BLOCK, hidden)
+    square, row = (whole_spec((slots, width)), whole_spec((1, width)))
+    weight = pl.BlockSpec((block, width), lambda step: (step, 0))
+    column = pl.BlockSpec((slots, block), lambda step: (0, step))
+    return pl.pallas_call(
+        feed_kernel,
+        grid=(hidden // block,),
+        in_specs=[
+            pl.BlockSpec(memory_space=pltpu.SMEM),
+            square,
+            square,
+            weight,
+            pl.BlockSpec((1, block), lambda step: (0, step)),
+            weight,
+            row,
+            row,
+            row,
+        ],
+        out_specs=[column, column, square, square, whole_spec((slots, 1))],
+        out_shape=[
+            jax.ShapeDtypeStruct((slots, hidden), BF16),
+            jax.ShapeDtypeStruct((slots, hidden), BF16),
+            jax.ShapeDtypeStruct((slots, width), BF16),
+            jax.ShapeDtypeStruct((slots, width), F32),
+            jax.ShapeDtypeStruct((slots, 1), F32),
+        ],
+        scratch_shapes=[pltpu.VMEM((slots, width), F32)],
+        compiler_params=pltpu.CompilerParams(
+            dimension_semantics=("arbitrary",), vmem_limit_bytes=56 * 1024 * 1024
+        ),
+        cost_estimate=pl.CostEstimate(
+            flops=4 * slots * width * hidden,
+            bytes_accessed=4 * hidden * (width + slots),
+            transcendentals=slots * hidden,
+        ),
+    )(alpha, rows_low, rows_wide, in_rows, in_shift, down_rows, down_shift, gain, shift)
+
+
+def feed_back_kernel(
+    alpha_ref, low_ref, wide_ref, in_ref, down_ref, slope_ref, pre_ref, bias_ref, total_ref, acc
+):
+    step = pl.program_id(0)
+    slots = low_ref.shape[0]
+
+    @pl.when(step == 0)
+    def _():
+        acc[...] = alpha_ref[0] * wide_ref[...]
+
+    sums = None
+    for first in range(0, slots, ROWS):
+        rows = pl.ds(first, ROWS)
+        made = rows_nt(low_ref[rows, :], down_ref[...]) * wide(slope_ref[rows, :])
+        grad_pre = low(made)
+        pre_ref[rows, :] = grad_pre
+        part = jnp.sum(wide(grad_pre), axis=0, keepdims=True)
+        sums = part if sums is None else sums + part
+        acc[rows, :] += rows_nn(grad_pre, in_ref[...])
+    bias_ref[...] = sums
+
+    @pl.when(step == pl.num_programs(0) - 1)
+    def _():
+        total_ref[...] = acc[...]
+
+
+def feed_back_call(alpha, grad_low, grad_wide, in_rows, down_rows, slopes):
+    slots, width = grad_low.shape
+    hidden = in_rows.shape[0]
+    block = min(BLOCK, hidden)
+    square = whole_spec((slots, width))
+    weight = pl.BlockSpec((block, width), lambda step: (step, 0))
+    column = pl.BlockSpec((slots, block), lambda step: (0, step))
+    return pl.pallas_call(
+        feed_back_kernel,
+        grid=(hidden // block,),
+        in_specs=[pl.BlockSpec(memory_space=pltpu.SMEM), square, square, weight, weight, column],
+        out_specs=[column, pl.BlockSpec((1, block), lambda step: (0, step)), square],
+        out_shape=[
+            jax.ShapeDtypeStruct((slots, hidden), BF16),
+            jax.ShapeDtypeStruct((1, hidden), F32),
+            jax.ShapeDtypeStruct((slots, width), F32),
+        ],
+        scratch_shapes=[pltpu.VMEM((slots, width), F32)],
+        compiler_params=pltpu.CompilerParams(
+            dimension_semantics=("arbitrary",), vmem_limit_bytes=56 * 1024 * 1024
+        ),
+        cost_estimate=pl.CostEstimate(
+            flops=4 * slots * width * hidden,
+            bytes_accessed=4 * hidden * (width + slots),
+            transcendentals=0,
+        ),
+    )(alpha, grad_low, grad_wide, in_rows, down_rows, slopes)
+
+
+def norm_back_kernel(limit_ref, grad_ref, norm_ref, factor_ref, gain_ref, made_ref, low_ref, sums_ref):
+    step = pl.program_id(0)
+    rows = grad_ref.shape[0]
+    position = step * rows + lax.broadcasted_iota(jnp.int32, (rows, 1), 0)
+    gradient = jnp.where(position < limit_ref[0], wide(grad_ref[...]), 0.0)
+    normed = norm_ref[...]
+    made, gain_sum, shift_sum = norm_back(gradient, normed, factor_ref[...], gain_ref[...])
+    made_ref[...] = made
+    low_ref[...] = low(made)
+    rows_made = jnp.concatenate(
+        [
+            gain_sum[None],
+            shift_sum[None],
+            jnp.sum(made, axis=0, keepdims=True),
+            jnp.zeros((5, made.shape[1]), jnp.float32),
+        ]
+    )
+
+    @pl.when(step == 0)
+    def _():
+        sums_ref[...] = rows_made
+
+    @pl.when(step != 0)
+    def _():
+        sums_ref[...] += rows_made
+
+
+def norm_back_call(limit, gradient, normed, factor, gain):
+    slots, width = gradient.shape
+    block = pl.BlockSpec((ROWS, width), lambda step, *_: (step, 0))
+    return pl.pallas_call(
+        norm_back_kernel,
+        grid_spec=pltpu.PrefetchScalarGridSpec(
+            num_scalar_prefetch=1,
+            grid=(slots // ROWS,),
+            in_specs=[
+                block,
+                block,
+                pl.BlockSpec((ROWS, 1), lambda step, *_: (step, 0)),
+                whole_spec((1, width)),
+            ],
+            out_specs=[block, block, whole_spec((8, width))],
+        ),
+        out_shape=[
+            jax.ShapeDtypeStruct((slots, width), F32),
+            jax.ShapeDtypeStruct((slots, width), BF16),
+            jax.ShapeDtypeStruct((8, width), F32),
+        ],
+        compiler_params=pltpu.CompilerParams(
+            dimension_semantics=("arbitrary",), vmem_limit_bytes=32 * 1024 * 1024
+        ),
+    )(limit, gradient, normed, factor, gain)
 
 
 def mesh_place():
@@ -957,17 +1201,19 @@
     )
 
 
-def at_slot(ref, axis, slot):
-    return ref.at[slot] if axis == 0 else ref.at[:, slot]
+def at_slot(ref, paired, half, slot):
+    outer, inner = divmod(slot, 2)
+    return ref.at[half, outer, :, inner] if paired else ref.at[half, outer, inner]
 
 
 def gather_kernel(axes, *refs):
     groups = len(axes)
     blocks, own, across = (refs[0], refs[1 : 1 + groups], refs[1 + groups : 1 + 2 * groups])
     rest = refs[1 + 2 * groups :]
-    rows, near, far = (rest[0], rest[1 : 1 + groups], rest[1 + groups : 1 + 2 * groups])
-    local_sem, block_send, block_recv, ring_send, ring_recv = rest[1 + 2 * groups : 6 + 2 * groups]
-    side_send, side_recv, core_send, core_recv = rest[6 + 2 * groups :]
+    rows, filled = (rest[0], rest[1 : 1 + groups])
+    near, far = (0, 1)
+    local_sem, block_send, block_recv, ring_send, ring_recv = rest[1 + groups : 6 + groups]
+    side_send, side_recv, core_send, core_recv = rest[6 + groups :]
     unit, place, count = mesh_place()
     partners = greet(unit, place, count)
     right, side, core = (partners[0], partners[-2], partners[-1])
@@ -985,8 +1231,8 @@
         copy.start()
         local.append(copy)
 
-    def slot(refs_of, group, index):
-        return at_slot(refs_of[group], axes[group], index)
+    def slot(half, group, index):
+        return at_slot(filled[group], axes[group], half, index)
 
     def hop(group, step):
         source = own[group] if step == 1 else slot(near, group, step - 1)
@@ -1070,23 +1316,23 @@
         copy.wait_send()
 
 
-def gather_all(blocks, own, across, axes):
+def gather_all(blocks, own, across, paired):
     count = lax.axis_size("tensor")
-    groups = len(axes)
+    groups = len(paired)
     anywhere = pl.BlockSpec(memory_space=pl.ANY)
-
-    def spread_shape(array, axis):
-        shape = list(array.shape)
-        shape.insert(axis, 2 * count)
-        return jax.ShapeDtypeStruct(tuple(shape), array.dtype)
-
-    halves = [spread_shape(array, axis) for array, axis in zip(own, axes)]
+    filled = []
+    for array, in_pairs in zip(own, paired):
+        if in_pairs:
+            shape = (2, count, array.shape[0], 2) + array.shape[1:]
+        else:
+            shape = (2, count, 2) + array.shape
+        filled.append(jax.ShapeDtypeStruct(shape, array.dtype))
     dma = pltpu.SemaphoreType.DMA
     made = pl.pallas_call(
-        functools.partial(gather_kernel, axes),
+        functools.partial(gather_kernel, paired),
         in_specs=[anywhere] * (1 + 2 * groups),
-        out_specs=[anywhere] * (1 + 2 * groups),
-        out_shape=[jax.ShapeDtypeStruct(blocks.shape, blocks.dtype)] + halves + halves,
+        out_specs=[anywhere] * (1 + groups),
+        out_shape=[jax.ShapeDtypeStruct(blocks.shape, blocks.dtype)] + filled,
         scratch_shapes=[
             dma((1 + 2 * groups,)),
             dma((count - 1,)),
@@ -1100,14 +1346,58 @@
         ],
         compiler_params=pltpu.CompilerParams(collective_id=0, has_side_effects=True),
     )(blocks, *own, *across)
-    return (made[0], made[1 : 1 + groups], made[1 + groups :])
-
-
-def reduce_kernel(axes, depths, *refs):
-    groups = len(axes)
+    return (made[0], made[1:])
+
+
+def exchange_kernel(active, blocks, rows, local_sem, send_sem, recv_sem):
+    @pl.when(lax.axis_index("section") == active)
+    def _():
+        place, count = (lax.axis_index("tensor"), lax.axis_size("tensor"))
+        partners = [{"tensor": lax.rem(place + d, count)} for d in range(1, count)]
+        barrier = pltpu.get_barrier_semaphore()
+        for partner_id in partners:
+            pl.semaphore_signal(barrier, inc=1, device_id=partner_id, device_id_type=MESH)
+        pl.semaphore_wait(barrier, count - 1)
+        own = pltpu.make_async_copy(blocks.at[place], rows.at[place], local_sem.at[0])
+        own.start()
+        copies = []
+        for distance in range(1, count):
+            copy = remote(
+                blocks.at[lax.rem(place + distance, count)],
+                rows.at[place],
+                send_sem.at[distance - 1],
+                recv_sem.at[distance - 1],
+                partners[distance - 1],
+            )
+            copy.start()
+            copies.append(copy)
+        own.wait()
+        for copy in copies:
+            copy.wait()
+
+
+def exchange_in(active, number, blocks):
+    count = lax.axis_size("tensor")
+    anywhere = pl.BlockSpec(memory_space=pl.ANY)
+    return pl.pallas_call(
+        functools.partial(exchange_kernel, active),
+        in_specs=[anywhere],
+        out_specs=anywhere,
+        out_shape=jax.ShapeDtypeStruct(blocks.shape, blocks.dtype),
+        scratch_shapes=[
+            pltpu.SemaphoreType.DMA((1,)),
+            pltpu.SemaphoreType.DMA((count - 1,)),
+            pltpu.SemaphoreType.DMA((count - 1,)),
+        ],
+        compiler_params=pltpu.CompilerParams(collective_id=number, has_side_effects=True),
+    )(blocks)
+
+
+def reduce_kernel(paired, depths, *refs):
+    groups = len(paired)
     blocks, small = refs[:2]
-    near, far = (refs[2 : 2 + groups], refs[2 + groups : 2 + 2 * groups])
-    rest = refs[2 + 2 * groups :]
+    made = refs[2 : 2 + groups]
+    rest = refs[2 + groups :]
     rows, small_out, out = (rest[0], rest[1], rest[2 : 2 + groups])
     (
         near_buf,
@@ -1155,7 +1445,7 @@
 
     chunks = []
     for group in range(groups):
-        if axes[group] == 0:
+        if not paired[group]:
             for first in range(0, depths[group], CHUNK):
                 chunks.append((group, (pl.ds(first, CHUNK),)))
         else:
@@ -1163,13 +1453,19 @@
                 for first in range(0, depths[group], CHUNK):
                     chunks.append((group, (part, pl.ds(first, CHUNK))))
 
-    def rows_of(ref, chunk, slots):
+    def rows_of(chunk, half):
         group, place_in = chunk
-        if axes[group] == 0:
-            return ref[group].at[slots, place_in[0]]
-        return ref[group].at[place_in[0], slots, place_in[1]]
-
-    everything = slice(None)
+        ref = made[group]
+        if paired[group]:
+            return ref.at[half, :, place_in[0], :, place_in[1]]
+        return ref.at[half, :, :, place_in[0]]
+
+    def result_of(chunk, owner):
+        group, place_in = chunk
+        if paired[group]:
+            return out[group].at[owner, place_in[0], place_in[1]]
+        return out[group].at[owner, place_in[0]]
+
     block_copies = []
     for distance in range(1, count):
         block_copies.append(
@@ -1189,19 +1485,16 @@
     state = {}
     outs = []
 
-    def wide(value):
-        return value.astype(jnp.float32)
-
     def enter(index):
         chunk = chunks[index]
         copy = pltpu.make_async_copy(
-            rows_of(near, chunk, everything), near_buf.at[index % 3], near_sem.at[index]
+            rows_of(chunk, 0), near_buf.at[index % 3], near_sem.at[index]
         )
         copy.start()
         state["near", index] = copy
         state["core", index] = begin(
             remote(
-                rows_of(far, chunk, everything),
+                rows_of(chunk, 1),
                 sums.at[index],
                 core_send.at[index],
                 core_recv.at[index],
@@ -1212,7 +1505,7 @@
     def first_sum(index):
         state["near", index].wait()
         state["core", index].wait_recv()
-        upper = pl.ds(count, count)
+        upper = pl.ds(count // 2, count // 2)
         total = wide(near_buf[index % 3, upper]) + wide(sums[index, upper])
         sums[index, upper] = total.astype(jnp.bfloat16)
         state["side", index] = begin(
@@ -1227,13 +1520,13 @@
 
     def second_sum(index):
         state["side", index].wait_recv()
-        lower = pl.ds(0, count)
+        lower = pl.ds(0, count // 2)
         total = wide(near_buf[index % 3, lower]) + wide(sums[index, lower]) + wide(side_in[index])
         sums[index, lower] = total.astype(jnp.bfloat16)
         for distance in range(1, count):
             state["ring", index, distance] = begin(
                 remote(
-                    sums.at[index, distance],
+                    sums.at[index, distance // 2, distance % 2],
                     ring_in.at[index, distance - 1],
                     ring_send.at[index, distance - 1],
                     ring_recv.at[index, distance - 1],
@@ -1242,7 +1535,7 @@
             )
 
     def third_sum(index):
-        total = wide(sums[index, 0])
+        total = wide(sums[index, 0, 0])
         for distance in range(1, count):
             state["ring", index, distance].wait_recv()
             total = total + wide(ring_in[index, distance - 1])
@@ -1269,7 +1562,7 @@
         found = (pair.at[index, 0], pair.at[index, 1], other.at[index, 0], other.at[index, 1])
         for bits in range(4):
             copy = pltpu.make_async_copy(
-                found[bits], rows_of(out, chunk, units[bits]), out_sem.at[index, bits]
+                found[bits], result_of(chunk, units[bits]), out_sem.at[index, bits]
             )
             copy.start()
             outs.append(copy)
@@ -1313,36 +1606,34 @@
         copy.wait_send()
 
 
-def reduce_all(blocks, small, near, far, axes):
+def reduce_all(blocks, small, made, paired):
     count = lax.axis_size("tensor")
     units = lax.axis_size("dp")
-    groups = len(axes)
+    groups = len(paired)
     anywhere = pl.BlockSpec(memory_space=pl.ANY)
     vmem = pl.BlockSpec(memory_space=pltpu.VMEM)
     width = blocks.shape[-1]
-    depths = [array.shape[axis + 1] for array, axis in zip(near, axes)]
-    total = sum(depth * (1 + axis) for depth, axis in zip(depths, axes)) // CHUNK
-
-    def own_shape(array, axis):
-        shape = list(array.shape)
-        shape[axis] = units
-        return jax.ShapeDtypeStruct(tuple(shape), array.dtype)
-
+    depths = [array.shape[-2] for array in made]
+    total = sum(depth * (2 if double else 1) for depth, double in zip(depths, paired)) // CHUNK
+    results = []
+    for array, double in zip(made, paired):
+        shape = (units,) + ((2,) if double else ()) + array.shape[-2:]
+        results.append(jax.ShapeDtypeStruct(shape, array.dtype))
     dma = pltpu.SemaphoreType.DMA
     bf16 = jnp.bfloat16
-    made = pl.pallas_call(
-        functools.partial(reduce_kernel, axes, depths),
-        in_specs=[anywhere, vmem] + [anywhere] * (2 * groups),
+    found = pl.pallas_call(
+        functools.partial(reduce_kernel, paired, depths),
+        in_specs=[anywhere, vmem] + [anywhere] * groups,
         out_specs=[anywhere, vmem] + [anywhere] * groups,
         out_shape=[
             jax.ShapeDtypeStruct(blocks.shape, blocks.dtype),
             jax.ShapeDtypeStruct(small.shape, small.dtype),
         ]
-        + [own_shape(array, axis) for array, axis in zip(near, axes)],
+        + results,
         scratch_shapes=[
-            pltpu.VMEM((3, 2 * count, CHUNK, width), bf16),
-            pltpu.VMEM((total, 2 * count, CHUNK, width), bf16),
-            pltpu.VMEM((total, count, CHUNK, width), bf16),
+            pltpu.VMEM((3, count, 2, CHUNK, width), bf16),
+            pltpu.VMEM((total, count, 2, CHUNK, width), bf16),
+            pltpu.VMEM((total, count // 2, 2, CHUNK, width), bf16),
             pltpu.VMEM((total, count - 1, CHUNK, width), bf16),
             pltpu.VMEM((total, 2, CHUNK, width), bf16),
             pltpu.VMEM((total, 2, CHUNK, width), bf16),
@@ -1370,8 +1661,12 @@
         compiler_params=pltpu.CompilerParams(
             collective_id=1, has_side_effects=True, vmem_limit_bytes=56 * 1024 * 1024
         ),
-    )(blocks, small, *near, *far)
-    return (made[0], made[1], made[2:])
+    )(blocks, small, *made)
+    return (found[0], found[1], found[2:])
+
+
+def after(value, *earlier):
+    return lax.optimization_barrier((value, earlier))[0]
 
 
 def sequence_body(
@@ -1395,16 +1690,19 @@
     units = lax.axis_size("dp")
     decoder = section == 1
     alpha = jnp.where(decoder, ALPHA_DEC, ALPHA_ENC).astype(jnp.float32)
+    alpha_row = alpha.reshape(1)
     batches, shard_rows, width = (inputs.shape[1], inputs.shape[2], inputs.shape[3])
     slots = batches * shard_rows
     gains = norm_gain[0].astype(jnp.float32)
     shifts = norm_bias[0].astype(jnp.float32)
-    down_shift = ffn_out_bias[0].astype(jnp.float32)
+    down_shift = ffn_out_bias.astype(jnp.float32)
 
     def unit_of(array, axis, bits):
         size = array.shape[axis] // units
         piece = lax.dynamic_slice_in_dim(array, (unit ^ bits) * size, size, axis)
         return piece.T if axis == 1 else piece
+
+    bias_size = ffn_in_bias.shape[1] // units
 
     def units_of(bits):
         return (
@@ -1416,72 +1714,64 @@
             jnp.broadcast_to(unit_of(ffn_in_bias[0], 0, bits)[None], (16, bias_size)),
         )
 
-    bias_size = ffn_in_bias.shape[1] // units
-    x, near, far = gather_all(inputs[0], units_of(0), units_of(2), (0, 0, 0, 0, 1, 0))
+    x, filled = gather_all(
+        inputs[0], units_of(0), units_of(2), (False, False, False, False, True, False)
+    )
     x = x.reshape(slots, width)
-    qkv_rows, out_rows, in_rows, down_rows = [
-        tuple(array.reshape(-1, width) for array in halves)
-        for halves in zip(near[:4], far[:4])
+    qkv_rows, out_rows, in_rows, down_rows, cross_rows = [
+        array.reshape(-1, width) for array in filled[:5]
     ]
-    cross_rows = tuple(array.reshape(2, -1, width) for array in (near[4], far[4]))
-    in_shift = tuple(
-        array[:, 0].reshape(-1).astype(jnp.float32) for array in (near[5], far[5])
-    )
+    in_shift = filled[5][:, :, :, 0].reshape(1, -1).astype(jnp.float32)
+    cross_parts = cross_rows.reshape(-1, 2, LANES, width)
+    half = width // 2
 
     source_len = lax.dynamic_index_in_dim(lengths[0, :, 0], tensor_index, 0, keepdims=False)
     target_len = lax.dynamic_index_in_dim(lengths[1, :, 0], tensor_index, 0, keepdims=False)
     own_len = jnp.where(decoder, target_len, source_len)
     self_scalars = jnp.stack([own_len, decoder.astype(jnp.int32)])
     cross_scalars = jnp.stack([source_len, jnp.zeros_like(source_len)])
+    no_limit = jnp.full((1,), 1 << 20, jnp.int32)
+    pairs = width // LANES
     sides = (0, 1)
 
-    qkv = [low(rows_nt(x, qkv_rows[side])) for side in sides]
-    mixed, lse_self = zip(*[self_attention(self_scalars, qkv[side]) for side in sides])
-    attn_sum = rows_nn(mixed[0], out_rows[0]) + rows_nn(mixed[1], out_rows[1])
+    qkv = low(rows_nt(x, qkv_rows))
+    mixed, lse_self = self_attention(self_scalars, qkv, 0, pairs)
     resid_a, norm_a, factor_a = layer_norm(
-        alpha * x.astype(jnp.float32) + attn_sum, gains[0], shifts[0]
+        alpha * x.astype(jnp.float32) + rows_nn(mixed, out_rows), gains[0], shifts[0]
     )
     a_low = low(resid_a)
-    half_width = width // 2
-    half_zero = jnp.zeros((slots, half_width), jnp.bfloat16)
 
     def zeros_like_of(branch):
         shapes = jax.eval_shape(branch)
         return lambda: jax.tree.map(lambda leaf: jnp.zeros(leaf.shape, leaf.dtype), shapes)
 
     def dec_query():
-        return tuple(low(rows_nt(a_low, cross_rows[side][0])) for side in sides)
-
-    query_sent = lax.cond(decoder, dec_query, zeros_like_of(dec_query))
-    query_held = [lax.ppermute(piece, "section", [(1, 0)]) for piece in query_sent]
-
-    def feed(rows_low, rows_wide, gain_row, shift_row):
-        hidden, slopes, total = ([], [], alpha * rows_wide + down_shift)
-        for side in sides:
-            made, slope = gelu_and_slope(rows_nt(rows_low, in_rows[side]) + in_shift[side])
-            hidden.append(low(made))
-            slopes.append(low(slope))
-        for side in sides:
-            total = total + rows_nn(hidden[side], down_rows[side])
-        return (tuple(hidden), tuple(slopes)) + layer_norm(total, gain_row, shift_row)
-
-    def feed_back(grad_sum, slopes):
-        grad_low = low(grad_sum)
-        grad_pre = tuple(
-            low(rows_nt(grad_low, down_rows[side]) * slopes[side].astype(jnp.float32))
-            for side in sides
-        )
-        total = alpha * grad_sum
-        for side in sides:
-            total = total + rows_nn(grad_pre[side], in_rows[side])
-        return (grad_low, grad_pre, total)
+        first = cross_parts[:, 0].reshape(-1, width)
+        made = low(rows_nt(a_low, first))
+        return (made[:, :half], made[:, half:], first, cross_parts[:, 1].reshape(-1, width))
+
+    query_left, query_right, cross_first, cross_second = lax.cond(
+        decoder, dec_query, zeros_like_of(dec_query)
+    )
+    query_held = [lax.ppermute(piece, "section", [(1, 0)]) for piece in (query_left, query_right)]
+    cotangent_rows = exchange_in(1, 2, after(cotangent, query_held)).reshape(slots, width)
+
+    def feed(rows_low, rows_wide):
+        return feed_call(
+            alpha_row,
+            rows_low,
+            rows_wide,
+            in_rows,
+            in_shift,
+            down_rows,
+            down_shift,
+            gains[2:3],
+            shifts[2:3],
+        )
 
     def enc_feed():
-        hidden, slopes, memory, norm_y, factor_y = feed(a_low, resid_a, gains[2], shifts[2])
-        memory_low = low(memory)
-        key_values = tuple(
-            low(rows_nt(memory_low, cross_rows[side].reshape(-1, width))) for side in sides
-        )
+        hidden, slopes, memory_low, norm_y, factor_y = feed(a_low, resid_a)
+        key_values = low(rows_nt(memory_low, cross_rows))
         return (hidden, slopes, memory_low, norm_y, factor_y, key_values)
 
     hidden_e, slopes_e, memory_low, norm_e, factor_e, key_values = lax.cond(
@@ -1492,39 +1782,55 @@
     for side in sides:
 
         def enc_mix():
-            return tuple(cross_attention(cross_scalars, query_held[side], key_values[side]))
+            return tuple(
+                cross_attention(
+                    cross_scalars, query_held[side], key_values, side * pairs // 2, pairs // 2
+                )
+            )
 
         mix_made, lse_made = lax.cond(decoder, zeros_like_of(enc_mix), enc_mix)
         mixed_c.append(mix_made)
         lse_c.append(lse_made)
         mixed_held.append(lax.ppermute(mix_made, "section", [(0, 1)]))
 
-    own_pos = lax.broadcasted_iota(jnp.int32, (slots, 1), 0)
-    cotangent_rows = exchange(after(cotangent, qkv[0]), jnp.bfloat16).reshape(slots, width)
+    def sharded(rows):
+        return rows.reshape(batches, shard_rows, width)
+
+    outputs_e = exchange_in(0, 3, after(sharded(memory_low), mixed_held))
+    mixed_held = after(mixed_held, outputs_e)
 
     def dec_middle():
-        crossed = rows_nn(mixed_held[0], cross_rows[0][1]) + rows_nn(
-            mixed_held[1], cross_rows[1][1]
+        crossed = rows_nn(mixed_held[0], cross_second[:half]) + rows_nn(
+            mixed_held[1], cross_second[half:]
         )
         resid_c, norm_c, factor_c = layer_norm(alpha * resid_a + crossed, gains[1], shifts[1])
         c_low = low(resid_c)
-        hidden, slopes, decoded, norm_y, factor_y = feed(c_low, resid_c, gains[2], shifts[2])
-        grad_top = jnp.where(own_pos < target_len, cotangent_rows.astype(jnp.float32), 0.0)
-        grad_y, gain_y, shift_y = norm_back(grad_top, norm_y, factor_y, gains[2])
-        grad_low, grad_pre, grad_c = feed_back(grad_y, slopes)
-        grad_mid, gain_c, shift_c = norm_back(grad_c, norm_c, factor_c, gains[1])
-        mid_low = low(grad_mid)
-        grad_mixed_c = tuple(low(rows_nt(mid_low, cross_rows[side][1])) for side in sides)
+        hidden, slopes, decoded_low, norm_y, factor_y = feed(c_low, resid_c)
+        grad_y, grad_low, sums_y = norm_back_call(
+            target_len.reshape(1), cotangent_rows, norm_y, factor_y, gains[2:3]
+        )
+        grad_pre, bias_sum, grad_c = feed_back_call(
+            alpha_row, grad_low, grad_y, in_rows, down_rows, slopes
+        )
+        grad_mid, mid_low, sums_c = norm_back_call(
+            no_limit, grad_c, norm_c, factor_c, gains[1:2]
+        )
+        grad_mixed_c = tuple(
+            low(rows_nt(mid_low, cross_second[side * half : side * half + half]))
+            for side in sides
+        )
         return (
-            low(decoded),
+            decoded_low,
             hidden,
             c_low,
             grad_low,
             grad_pre,
+            bias_sum,
             grad_mid,
             mid_low,
             grad_mixed_c,
-            jnp.stack([gain_c, gain_y, shift_c, shift_y, jnp.sum(grad_y, axis=0)]),
+            sums_y,
+            sums_c,
         )
 
     (
@@ -1533,12 +1839,15 @@
         c_low,
         grad_low_d,
         grad_pre_d,
+        bias_sum_d,
         grad_mid,
         mid_low,
         grad_mixed_c,
-        vectors_d,
+        sums_yd,
+        sums_cd,
     ) = lax.cond(decoder, dec_middle, zeros_like_of(dec_middle))
     grad_mixed_held = [lax.ppermute(piece, "section", [(1, 0)]) for piece in grad_mixed_c]
+
     grad_query_held, grad_kv = ([], [])
     for side in sides:
 
@@ -1547,10 +1856,12 @@
                 cross_attention_back(
                     cross_scalars,
                     query_held[side],
-                    key_values[side],
+                    key_values,
                     mixed_c[side],
                     grad_mixed_held[side],
                     lse_c[side],
+                    side * pairs // 2,
+                    pairs // 2,
                 )
             )
 
@@ -1558,83 +1869,54 @@
         grad_kv.append(kv_made)
         grad_query_held.append(lax.ppermute(query_made, "section", [(0, 1)]))
 
+    outputs_d = exchange_in(1, 4, after(sharded(decoded_low), grad_mixed_held))
+    grad_query_held = after(grad_query_held, outputs_d)
+    outputs = jnp.where(decoder, outputs_d, outputs_e)
+
     def enc_back():
-        grad_memory = None
-        for side in sides:
-            for part in range(2):
-                term = rows_nn(grad_kv[side][part], cross_rows[side][part])
-                grad_memory = term if grad_memory is None else grad_memory + term
-        grad_y, gain_y, shift_y = norm_back(grad_memory, norm_e, factor_e, gains[2])
-        grad_low, grad_pre, grad_a = feed_back(grad_y, slopes_e)
-        zero_row = jnp.zeros_like(gain_y)
-        rows = jnp.stack([zero_row, gain_y, zero_row, shift_y, jnp.sum(grad_y, axis=0)])
-        return (grad_low, grad_pre, grad_a, rows)
+        grad_memory = rows_nn(grad_kv[0], cross_rows[:width]) + rows_nn(
+            grad_kv[1], cross_rows[width:]
+        )
+        grad_y, grad_low, sums_y = norm_back_call(
+            no_limit, grad_memory, norm_e, factor_e, gains[2:3]
+        )
+        grad_pre, bias_sum, grad_a = feed_back_call(
+            alpha_row, grad_low, grad_y, in_rows, down_rows, slopes_e
+        )
+        made = [rows_tn(piece, memory_low) for piece in grad_kv]
+        return (grad_low, grad_pre, bias_sum, grad_a, sums_y, low(jnp.concatenate(made)))
 
     def dec_back():
-        grad_a = alpha * grad_mid
-        for side in sides:
-            grad_a = grad_a + rows_nn(grad_query_held[side], cross_rows[side][0])
-        return (grad_low_d, grad_pre_d, grad_a, vectors_d)
-
-    grad_low, grad_pre, grad_a, vectors = lax.cond(decoder, dec_back, enc_back)
-
-    outputs = exchange(
-        after(jnp.where(decoder, decoded_low, memory_low), grad_a).reshape(
-            batches, shard_rows, width
-        ),
-        jnp.bfloat16,
-    )
-
-    def cross_grads(side):
-        def enc():
-            return jnp.stack([low(rows_tn(grad_kv[side][part], memory_low)) for part in range(2)])
-
-        def dec():
-            return jnp.stack(
-                [
-                    low(rows_tn(grad_query_held[side], a_low)),
-                    low(rows_tn(mixed_held[side], mid_low)),
-                ]
-            )
-
-        return lax.cond(decoder, dec, enc)
-
-    def down_grads(side):
+        grad_query = jnp.concatenate(grad_query_held, axis=1)
+        grad_a = alpha * grad_mid + rows_nn(grad_query, cross_first)
+        mixed_all = jnp.concatenate(mixed_held, axis=1)
+        made = [rows_tn(grad_query, a_low), rows_tn(mixed_all, mid_low)]
+        made = [piece.reshape(-1, 1, LANES, width) for piece in made]
+        cross_made = low(jnp.concatenate(made, axis=1)).reshape(-1, width)
+        return (grad_low_d, grad_pre_d, bias_sum_d, grad_a, sums_yd, cross_made)
+
+    grad_low, grad_pre, bias_sum, grad_a, sums_y, cross_made = lax.cond(
+        decoder, dec_back, enc_back
+    )
+
+    def down_grads():
         return lax.cond(
             decoder,
-            lambda: low(rows_tn(hidden_d[side], grad_low)),
-            lambda: low(rows_tn(hidden_e[side], grad_low)),
-        )
-
-    def in_grads(side):
+            lambda: low(rows_tn(hidden_d, grad_low)),
+            lambda: low(rows_tn(hidden_e, grad_low)),
+        )
+
+    def in_grads():
         return lax.cond(
             decoder,
-            lambda: low(rows_tn(grad_pre[side], c_low)),
-            lambda: low(rows_tn(grad_pre[side], a_low)),
-        )
-
-    def total_of(made):
-        far = made(1)
-        return (made(0), far)
-
-    down_made, in_made, cross_made = (
-        total_of(down_grads),
-        total_of(in_grads),
-        total_of(cross_grads),
-    )
-
-    grad_r, gain_a, shift_a = norm_back(grad_a, norm_a, factor_a, gains[0])
-    r_low = low(grad_r)
-    grad_mixed = [low(rows_nt(r_low, out_rows[side])) for side in sides]
-    out_made = total_of(lambda side: low(rows_tn(mixed[side], r_low)))
-    grad_qkv = [
-        self_attention_back(self_scalars, qkv[side], mixed[side], grad_mixed[side], lse_self[side])
-        for side in sides
-    ]
-    grad_x = alpha * grad_r
-    for side in sides:
-        grad_x = grad_x + rows_nn(grad_qkv[side], qkv_rows[side])
-    qkv_made = total_of(lambda side: low(rows_tn(grad_qkv[side], x)))
+            lambda: low(rows_tn(grad_pre, c_low)),
+            lambda: low(rows_tn(grad_pre, a_low)),
+        )
+
+    grad_r, r_low, sums_a = norm_back_call(no_limit, grad_a, norm_a, factor_a, gains[0:1])
+    grad_mixed = low(rows_nt(r_low, out_rows))
+    grad_qkv = self_attention_back(self_scalars, qkv, mixed, grad_mixed, lse_self, 0, pairs)
+    grad_x = low(alpha * grad_r + rows_nn(grad_qkv, qkv_rows))
 
     slot_bits = jnp.asarray([0, 2, 1, 3], jnp.int32)[:, None]
     slot_unit = unit ^ slot_bits
@@ -1643,32 +1925,28 @@
     hot = (slot_index[None, :] == lax.iota(jnp.int32, slot_index.shape[0])[:, None]).astype(
         jnp.float32
     )
-    shift_rel = jnp.concatenate(
-        [jnp.sum(grad_pre[side].astype(jnp.float32), axis=0) for side in sides]
-    ).reshape(-1, bias_size)
-    shift_abs = jnp.dot(hot, shift_rel, precision=lax.Precision.HIGHEST).reshape(-1, width)
-    small = jnp.concatenate([jnp.stack([gain_a, shift_a]), vectors, shift_abs])
+    shift_abs = jnp.dot(
+        hot, bias_sum.reshape(-1, bias_size), precision=lax.Precision.HIGHEST
+    ).reshape(-1, width)
+    small = jnp.concatenate([sums_a[:2], sums_cd[:2], sums_y[:3], shift_abs])
     small = jnp.pad(small, ((0, -small.shape[0] % 8), (0, 0)))
-    made = (qkv_made, out_made, in_made, down_made, cross_made)
-    axes = (0, 0, 0, 0, 1)
-
-    def by_slot(array, axis):
-        shape = list(array.shape)
-        shape[axis : axis + 1] = [2 * tensor_count, shape[axis] // (2 * tensor_count)]
-        return array.reshape(shape)
-
+    made = (
+        low(rows_tn(grad_qkv, x)),
+        low(rows_tn(mixed, r_low)),
+        in_grads(),
+        down_grads(),
+        cross_made,
+    )
     input_rows, small, grads = reduce_all(
-        low(grad_x).reshape(batches, shard_rows, width),
+        sharded(grad_x),
         small,
-        [by_slot(halves[0], axis) for halves, axis in zip(made, axes)],
-        [by_slot(halves[1], axis) for halves, axis in zip(made, axes)],
-        axes,
+        [array.reshape(like.shape) for array, like in zip(made, filled)],
+        (False, False, False, False, True),
     )
     input_grad = input_rows.astype(jnp.float32)
     qkv_grad, out_grad, in_grad, down_grad, cross_grad = [
         array.astype(jnp.float32) for array in grads
     ]
-    cross_grad = jnp.swapaxes(cross_grad, 0, 1)
     in_shift_grad = lax.dynamic_index_in_dim(
         small[7:11].reshape(tensor_count, -1), tensor_index, 0, keepdims=False
     )
@@ -1686,8 +1964,8 @@
         in_shift_grad[None],
         down_grad.reshape(1, -1, width),
         small[6][None],
-        small[jnp.asarray([0, 2, 3])][None],
-        small[jnp.asarray([1, 4, 5])][None],
+        small[jnp.asarray([0, 2, 4])][None],
+        small[jnp.asarray([1, 3, 5])][None],
     )
 
 

time: 1310 us -> 1090 us (0.83)
  waiting for transfers between devices: 253 us -> 89.2 us
  Pallas kernels: 661 us -> 790 us
  matrix products: 205 us -> 98 us
  other arithmetic: 61 us -> 26 us
  local copies, waits for them, and re-layouts: 85.4 us -> 65.9 us
  starting transfers between devices: 27.5 us -> 14.3 us
    pallas_call x2 -> x9, Pallas kernels: 441 us -> 574 us  [the longest x1 267 us: reduce_all(): pl.pallas_call(functools.partial(reduce_kernel, paired, depths), in_specs...]
    ppermute x4, waiting for transfers between devices: 174 us -> 52.9 us  [sequence_body(): lax.ppermute(piece, 'section', [(1, 0)])]
    ppermute x6 -> x0, waiting for transfers between devices: 63.7 us -> none  [around(): lax.ppermute(value, 'tensor', [(i, (i + distance) % count) for i in range...]
    dot_general x12 -> x4, matrix products: 73.6 us -> 22.3 us  [rows_nn(): return jnp.dot(rows, weight_rows, preferred_element_type=jnp.float32)]
    dot_general x10 -> x3, matrix products: 66.9 us -> 21.6 us  [rows_nt(): lax.dot_general(rows, weight_rows, COL_DIMS, preferred_element_type=jnp.f...]
    ppermute x2, waiting for transfers between devices: 0.01 us -> 22.1 us  [sequence_body(): mixed_held.append(lax.ppermute(mix_made, 'section', [(0, 1)]))]
    reduce_sum x4 -> x0, other arithmetic: 21.9 us -> none  [the longest x1 13.7 us: norm_back(): jnp.sum(gradient * normed, axis=0)]
    ppermute x6 -> x0, starting transfers between devices: 14.9 us -> none  [around(): lax.ppermute(value, 'tensor', [(i, (i + distance) % count) for i in range...]
  transfers between devices with their start and end apart: 14 -> 8, of which waited for: 5 -> 3; matrix products, arithmetic and copies ran while one was open for 7% -> 1% of each run, Pallas kernels for 9% -> 13%
where the time goes in v3:
time: 1090 us
  Pallas kernels  790 us (72%)
  matrix products  98 us (9%)
  waiting for transfers between devices  89.2 us (8%)
  local copies, waits for them, and re-layouts  65.9 us (6%)
  other arithmetic  26 us (2%)
  starting transfers between devices  14.3 us (1%)
    pallas_call x1, Pallas kernels, reduce_all(): pl.pallas_call(functools.partial(reduce_kernel, paired, depths), in_specs...  267 us
    pallas_call x6, Pallas kernels, head_call(): pl.pallas_call(kernel, grid_spec=pltpu.PrefetchScalarGridSpec(num_scalar_...  216 us
    pallas_call x1, Pallas kernels, gather_all(): pl.pallas_call(functools.partial(gather_kernel, paired), in_specs=[anywhe...  174 us
    pallas_call x3, Pallas kernels, exchange_in(): pl.pallas_call(functools.partial(exchange_kernel, active), in_specs=[anyw...  57.5 us
    dot_general x6, matrix products, rows_tn(): lax.dot_general(left_rows, right_rows, ROW_DIMS, preferred_element_type=j...  54 us
    ppermute x4, waiting for transfers between devices, sequence_body(): lax.ppermute(piece, 'section', [(1, 0)])  52.9 us
    pallas_call x1, Pallas kernels, feed_call(): pl.pallas_call(feed_kernel, grid=(hidden // block,), in_specs=[pl.BlockSp...  37.2 us
    pallas_call x1, Pallas kernels, feed_back_call(): pl.pallas_call(feed_back_kernel, grid=(hidden // block,), in_specs=[pl.Bl...  27.8 us
  transfers between devices with their start and end apart: 8, of which 3 were waited for; matrix products, arithmetic and copies ran while one was open for 1% of the time, Pallas kernels for 13%

profile of v3, /device:TPU:9, one launch (start us, length us, event | category | flops | bytes accessed | tf_op | source)
XLA Modules:
  0.0 1088.2 jit_solution(13039193215179489501)
XLA Ops:
  13.3 173.7 %shard_map.230 = (bf16[4,256,1024]{2,1,0:T(8,128)(2,1)}, bf16[2,4,2,192,1024]{4,3,2,1,0:T(8,128)(2,1)}, bf16[2,4,2,64,1024]{4,3,2,1,0:T(8,128)(2,1)}, bf16[2,4,2...) custom-call(bf16[4,256,1024]{2,1,0:T(8,128)(2,1)} %bitcast.170, ...), custom_call_target="tpu_custom_call" | custom-call | tf_op jit(solution)/shard_map/pallas_call | solution.py:1331
  187.1 11.5 %convolution_convert_fusion.9.packed_ref = bf16[1024,3072]{1,0:T(8,128)(2,1)} fusion(bf16[1024,1024]{1,0:T(8,128)(2,1)} %bitcast.198, bf16[3072,1024]{1,0:T(8,128)(2,1)} %bitcast.196), kind=kOutput, calls=%fused_computation.37 | convolution fusion | flops 6445596672 | bytes 14680064 | tf_op jit(solution)/shard_map/dot_general | solution.py:958
  200.6 44.8 %shard_map.231 = (bf16[1024,1024]{1,0:T(8,128)(2,1)S(1)}, f32[1024,1024]{1,0:T(8,128)}) custom-call(s32[2]{0:T(128)S(1)} %pad_add_fusion.scalars, bf16[1024,3072]{1,0:T(8,128)(2,1)} %convolution_convert_fusion.9.packed_ref), custom_call_target="tpu_custom_call" | custom-call | flops 34359738368 | bytes 6291456 | tf_op jit(solution)/shard_map/pallas_call | solution.py:868
  245.9 5.4 fusion.32
  252.1 4.3 fusion.24
  256.4 4.9 conditional.21
  265.4 46.1 %conditional.22 = (bf16[1024,4096]{1,0:T(8,128)(2,1)}, bf16[1024,4096]{1,0:T(8,128)(2,1)}, bf16[1024,1024]{1,0:T(8,128)(2,1)}, f32[1024,1024]{1,0:T(8,128)}, f32...) conditional(s32[]{:T(128)} %convert_element_type.110, (f32[3,1024]{1,0:T(4,128)S(1)}, f32[3,1024]{1,0:T(4,128)S(1)}, ...), branch_computations={%region_4.5_spmd, %region_5.6_spmd} | conditional | flops 21476933632 | bytes 60833868 | solution.py:1777
  266.6 37.2 %branch_0_fun.7 = (bf16[1024,4096]{1,0:T(8,128)(2,1)}, bf16[1024,4096]{1,0:T(8,128)(2,1)}, bf16[1024,1024]{1,0:T(8,128)(2,1)}, f32[1024,1024]{1,0:T(8,128)}, f32[1024,1]{1,0:T(8,128)}) custom-call(f32[1]{0:T(128)} %get-tuple-element.182.alpha_ref, bf16[1024,1024]{1,0:T(8,128)(2,1)S(1)} %get-tuple-element.183.low_ref, ...), custom_call_target="tpu_custom_call" | custom-call | flops 17179869184 | bytes 33554432 | tf_op jit(solution)/shard_map/cond/branch_0_fun/pallas_call | solution.py:1031
  303.8 7.7 convolution_convert_fusion.1
  312.3 23.4 %conditional.24 = ((bf16[1024,512]{1,0:T(8,128)(2,1)}, f32[1024,512]{1,0:T(8,128)S(1)})) conditional(s32[]{:T(128)} %convert_element_type.110, (s32[2]{0:T(128)S(1)}, bf16[1024,512]{1,0:T(8,128)(2,1)}, bf16[1024,2048]{1,0:T(8,128)(2,1)}) %tuple.110, () %tuple.111), branch_computations={%region_8.9_spmd, %region_9.10_spmd} | conditional | flops 17179869184 | bytes 3145758 | solution.py:1791
  312.3 23.4 %branch_0_fun.9 = (bf16[1024,512]{1,0:T(8,128)(2,1)}, f32[1024,512]{1,0:T(8,128)S(1)}) custom-call(s32[2]{0:T(128)S(1)} %get-tuple-element.200.scalars, bf16[1024,512]{1,0:T(8,128)(2,1)} %get-tuple-element.201.query_ref, bf16[1024,2048]{1,0:T(8,128)(2,1)} %get-tuple-element.202.key_ref.value_ref, bf16[1024,2048]{1,0:T(8,128)(2,1)} %get-tuple-element.202.key_ref.value_ref), custom_call_target="tpu_custom_call" | custom-call | flops 17179869184 | bytes 3145728 | tf_op jit(solution)/shard_map/cond/branch_0_fun/pallas_call | solution.py:868
  338.0 23.6 %conditional.23 = ((bf16[1024,512]{1,0:T(8,128)(2,1)}, f32[1024,512]{1,0:T(8,128)})) conditional(s32[]{:T(128)} %convert_element_type.110, (s32[2]{0:T(128)S(1)}, bf16[1024,512]{1,0:T(8,128)(2,1)}, bf16[1024,2048]{1,0:T(8,128)(2,1)}) %tuple.108, () %tuple.109), branch_computations={%region_6.7_spmd, %region_7.8_spmd} | conditional | flops 17179869184 | bytes 3145758 | solution.py:1791
  338.1 23.4 %branch_0_fun.8 = (bf16[1024,512]{1,0:T(8,128)(2,1)}, f32[1024,512]{1,0:T(8,128)}) custom-call(s32[2]{0:T(128)S(1)} %get-tuple-element.197.scalars, bf16[1024,512]{1,0:T(8,128)(2,1)} %get-tuple-element.198.query_ref, bf16[1024,2048]{1,0:T(8,128)(2,1)} %get-tuple-element.199.key_ref.value_ref, bf16[1024,2048]{1,0:T(8,128)(2,1)} %get-tuple-element.199.key_ref.value_ref), custom_call_target="tpu_custom_call" | custom-call | flops 17179869184 | bytes 3145728 | tf_op jit(solution)/shard_map/cond/branch_0_fun/pallas_call | solution.py:868
  363.9 22.0 %collective-permute-done.1 = bf16[1024,512]{1,0:T(8,128)(2,1)} collective-permute-done((bf16[1024,512]{1,0:T(8,128)(2,1)}, bf16[1024,512]{1,0:T(8,128)(2,1)}, u32[]{:S(2)}, u32[]{:S(2)}) %collective-permute-start.1) | collective-permute-done | bytes 1048608 | tf_op jit(solution)/shard_map/ppermute | solution.py:1794
  385.9 57.4 %shard_map.232 = bf16[4,256,1024]{2,1,0:T(8,128)(2,1)} custom-call(bf16[4,256,1024]{2,1,0:T(8,128)(2,1)} %bitcast.54.blocks), custom_call_target="tpu_custom_call" | custom-call | tf_op jit(solution)/shard_map/pallas_call | solution.py:1382
  443.4 20.3 %conditional.25 = (bf16[1024,4096]{1,0:T(8,128)(2,1)}, bf16[1024,1024]{1,0:T(8,128)(2,1)}, bf16[1024,1024]{1,0:T(8,128)(2,1)}, bf16[1024,4096]{1,0:T(8,128)(2,1)...) conditional(s32[]{:T(128)} %convert_element_type.110, ...), branch_computations={%region_10.11_spmd, %region_11.14_spmd} | conditional | flops 38668337152 | bytes 199365440 | solution.py:1848
  443.4 4.3 broadcast.173
  447.7 4.4 broadcast.173.clone
  452.1 2.6 broadcast.176
  466.3 52.9 %collective-permute-done.5 = bf16[1024,512]{1,0:T(8,128)(2,1)S(1)} collective-permute-done((bf16[1024,512]{1,0:T(8,128)(2,1)}, bf16[1024,512]{1,0:T(8,128)(2,1)S(1)}, u32[]{:S(2)}, u32[]{:S(2)}) %collective-permute-start.5) | collective-permute-done | bytes 1048608 | tf_op jit(solution)/shard_map/ppermute | solution.py:1849
  519.2 31.3 %conditional.27 = ((bf16[1024,512]{1,0:T(8,128)(2,1)}, bf16[1024,1024]{1,0:T(8,128)(2,1)})) conditional(s32[]{:T(128)} %convert_element_type.110, (s32[2]{0:T(128)S(1)}, bf16[1024,512]{1,0:T(8,128)(2,1)}, bf16[1024,2048]{1,0:T(8,128)(2,1)}, bf16[1024,512]{1,0:T(8,128)(2,1)}, bf16[1024,512]{1,0:T(8,128)(2,1)S(1)}, ...), branch_computations={%region_16.17_spmd, %region_17.18_spmd} | conditional | flops 42949672960 | bytes 6291464 | solution.py:1868
  519.2 31.3 %branch_0_fun.11 = (bf16[1024,512]{1,0:T(8,128)(2,1)}, bf16[1024,1024]{1,0:T(8,128)(2,1)}) custom-call(s32[2]{0:T(128)S(1)} %get-tuple-element.237.scalars, bf16[1024,512]{1,0:T(8,128)(2,1)} %get-tuple-element.238.query_ref, bf16[1024,2048]{1,0:T(8,128)(2,1)} %get-tuple-element.239.key_ref.value_ref, ...), custom_call_target="tpu_custom_call" | custom-call | flops 42949672960 | bytes 6291456 | tf_op jit(solution)/shard_map/cond/branch_0_fun/pallas_call | solution.py:868
  552.8 31.4 %conditional.26 = ((bf16[1024,512]{1,0:T(8,128)(2,1)}, bf16[1024,1024]{1,0:T(8,128)(2,1)})) conditional(s32[]{:T(128)} %convert_element_type.110, (s32[2]{0:T(128)S(1)}, bf16[1024,512]{1,0:T(8,128)(2,1)}, bf16[1024,2048]{1,0:T(8,128)(2,1)}, bf16[1024,512]{1,0:T(8,128)(2,1)}, bf16[1024,512]{1,0:T(8,128)(2,1)S(1)}, ...), branch_computations={%region_14.15_spmd, %region_15.16_spmd} | conditional | flops 42949672960 | bytes 6291464 | solution.py:1868
  552.8 31.4 %branch_0_fun.10 = (bf16[1024,512]{1,0:T(8,128)(2,1)}, bf16[1024,1024]{1,0:T(8,128)(2,1)}) custom-call(s32[2]{0:T(128)S(1)} %get-tuple-element.231.scalars, bf16[1024,512]{1,0:T(8,128)(2,1)} %get-tuple-element.232.query_ref, bf16[1024,2048]{1,0:T(8,128)(2,1)} %get-tuple-element.233.key_ref.value_ref, ...), custom_call_target="tpu_custom_call" | custom-call | flops 42949672960 | bytes 6291456 | tf_op jit(solution)/shard_map/cond/branch_0_fun/pallas_call | solution.py:868
  592.4 14.2 %collective-permute-done.6 = bf16[1024,512]{1,0:T(8,128)(2,1)} collective-permute-done((bf16[1024,512]{1,0:T(8,128)(2,1)}, bf16[1024,512]{1,0:T(8,128)(2,1)}, u32[]{:S(2)}, u32[]{:S(2)}) %collective-permute-start.6) | collective-permute-done | bytes 1048608 | tf_op jit(solution)/shard_map/ppermute | solution.py:1870
  606.6 49.9 %conditional.28 = (bf16[1024,1024]{1,0:T(8,128)(2,1)}, bf16[1024,4096]{1,0:T(8,128)(2,1)}, f32[1,4096]{1,0:T(1,128)S(1)}, f32[1024,1024]{1,0:T(8,128)S(1)}, f32[...) conditional(s32[]{:T(128)} %convert_element_type.110, (bf16[2048,1024]{1,0:T(8,128)(2,1)S(1)}, ...), branch_computations={%region_18.19_spmd, %region_19.20_spmd} | conditional | flops 25779240960 | bytes 117448872 | solution.py:2008
  609.2 2.4 fusion.9.grad_ref
  611.6 5.5 branch_0_fun.12
  619.0 27.8 %branch_0_fun.13 = (bf16[1024,4096]{1,0:T(8,128)(2,1)}, f32[1,4096]{1,0:T(1,128)S(1)}, f32[1024,1024]{1,0:T(8,128)S(1)}) custom-call(f32[1]{0:T(128)} %get-tuple-element.250.alpha_ref, bf16[1024,1024]{1,0:T(8,128)(2,1)} %get-tuple-element.539.low_ref, f32[1024,1024]{1,0:T(8,128)} %copy-done.7, bf16[4096,1024]{1,0:T(8,128)(2,1)} %get-tuple-element.252.in_ref, ...), custom_call_target="tpu_custom_call" | custom-call | flops 17179869184 | bytes 33554432 | tf_op jit(solution)/shard_map/cond/branch_0_fun/pallas_call | solution.py:1098
  646.8 4.8 fusion.33
  651.6 4.0 fusion.34
  658.5 2.9 copy-done
  661.4 4.6 shard_map.235
  666.1 3.8 convolution_convert_fusion.10
  669.9 2.4 convolution_convert_fusion.11.grad_ref
  672.3 62.0 %shard_map.236 = bf16[1024,3072]{1,0:T(8,128)(2,1)} custom-call(s32[2]{0:T(128)S(1)} %copy-done.10, bf16[1024,3072]{1,0:T(8,128)(2,1)} %convolution_convert_fusion.9.packed_ref, bf16[1024,1024]{1,0:T(8,128)(2,1)S(1)} %copy-done.12, bf16[1024,1024]{1,0:T(8,128)(2,1)S(1)} %convolution_convert_fusion.11.grad_ref, f32[1024,1024]{1,0:T(8,128)} %get-tuple-element.398.lse_ref), custom_call_target="tpu_custom_call" | custom-call | flops 85899345920 | bytes 12582912 | tf_op jit(solution)/shard_map/pallas_call | solution.py:868
  734.3 11.7 %convolution_convert_fusion.8 = bf16[3072,1024]{1,0:T(8,128)(2,1)} fusion(bf16[1024,3072]{1,0:T(8,128)(2,1)} %shard_map.236, bf16[1024,1024]{1,0:T(8,128)(2,1)S(1)} %bitcast.200), kind=kOutput, calls=%fused_computation.36 | convolution fusion | flops 6445596672 | bytes 14680064 | tf_op jit(solution)/shard_map/dot_general | solution.py:966
  747.4 12.2 %add_convert_fusion = bf16[1024,1024]{1,0:T(8,128)(2,1)} fusion(f32[1024,1024]{1,0:T(8,128)} %copy-done.6, f32[]{:T(128)} %select_n.69, bf16[1024,3072]{1,0:T(8,128)(2,1)} %shard_map.236, bf16[3072,1024]{1,0:T(8,128)(2,1)} %bitcast.197), kind=kOutput, calls=%fused_computation.38 | convolution fusion | flops 6445596672 | bytes 18874372 | tf_op jit(solution)/shard_map/dot_general | solution.py:962
  759.6 15.2 %conditional.30 = (bf16[2,4,2,256,1024]{4,3,2,1,0:T(8,128)(2,1)}) conditional(s32[]{:T(128)} %convert_element_type.110, (bf16[1024,4096]{1,0:T(8,128)(2,1)}, bf16[1024,1024]{1,0:T(8,128)(2,1)}) %tuple.126, (bf16[1024,4096]{1,0:T(8,128)(2,1)}, bf16[1024,1024]{1,0:T(8,128)(2,1)}) %tuple.127), branch_computations={%region_22.23_spmd, %region_23.24_spmd} | conditional | flops 8594128896 | bytes 18874376 | solution.py:1903
  759.6 15.0 %convolution_convert_fusion.6 = bf16[4096,1024]{1,0:T(8,128)(2,1)} fusion(bf16[1024,4096]{1,0:T(8,128)(2,1)} %get-tuple-element.277, bf16[1024,1024]{1,0:T(8,128)(2,1)} %get-tuple-element.278), kind=kOutput, calls=%fused_computation.34 | convolution fusion | flops 8594128896 | bytes 18874368 | tf_op jit(solution)/shard_map/cond/branch_0_fun/dot_general | solution.py:966
  774.8 15.0 %conditional.29 = (bf16[2,4,2,256,1024]{4,3,2,1,0:T(8,128)(2,1)}) conditional(s32[]{:T(128)} %convert_element_type.110, (bf16[1024,4096]{1,0:T(8,128)(2,1)}, bf16[1024,1024]{1,0:T(8,128)(2,1)S(1)}) %tuple.187, (bf16[1024,4096]{1,0:T(8,128)(2,1)}, bf16[1024,1024]{1,0:T(8,128)(2,1)}) %tuple.125), branch_computations={%region_20.21_spmd, %region_21.22_spmd} | conditional | flops 8594128896 | bytes 18874376 | solution.py:1910
  774.8 14.7 %convolution_convert_fusion.4 = bf16[4096,1024]{1,0:T(8,128)(2,1)} fusion(bf16[1024,4096]{1,0:T(8,128)(2,1)} %get-tuple-element.273, bf16[1024,1024]{1,0:T(8,128)(2,1)S(1)} %get-tuple-element.274), kind=kOutput, calls=%fused_computation.32 | convolution fusion | flops 8594128896 | bytes 18874368 | tf_op jit(solution)/shard_map/cond/branch_0_fun/dot_general | solution.py:966
  790.4 267.2 %shard_map.237 = (bf16[4,256,1024]{2,1,0:T(8,128)(2,1)}, f32[16,1024]{1,0:T(8,128)}, bf16[4,192,1024]{2,1,0:T(8,128)(2,1)}, bf16[4,64,1024]{2,1,0:T(8,128)(2,1)}...) custom-call(bf16[4,256,1024]{2,1,0:T(8,128)(2,1)} %bitcast.176, ...), custom_call_target="tpu_custom_call" | custom-call | tf_op jit(solution)/shard_map/pallas_call | solution.py:1624
  1059.9 4.1 bitcast_convert_fusion.1
  1064.0 5.3 copy.59
  1071.1 2.4 copy.57
  1076.7 4.2 bitcast_convert_fusion
  1081.0 2.5 bitcast_convert_fusion.2
  (166 shorter events, 71.9 us)
Async XLA Ops:
  2.0 4.3 copy-start.36
  2.0 4.3 copy-start.25
  6.7 4.7 copy-start.37
  6.7 4.7 copy-start.27
  245.3 0.6 copy-start.9
  245.9 5.4 copy-start.11
  251.3 0.7 copy-start.32
  251.4 0.7 copy-start.33
  252.0 4.3 copy-start.28
  252.1 4.3 copy-start.16
  256.3 9.0 copy-start.21
  256.3 8.4 copy-start.34
  261.3 51.0 %collective-permute-start.2 = (bf16[1024,512]{1,0:T(8,128)(2,1)}, bf16[1024,512]{1,0:T(8,128)(2,1)}, u32[]{:S(2)}, u32[]{:S(2)}) collective-permute-start(bf16[1024,512]{1,0:T(8,128)(2,1)} %get-tuple-element.366), channel_id=1, source_target_pairs={{16,0},{17,1},{18,2},{19,3},{20,4},{21,5},{22,6},{23,7},{24,8},{25... | collective-permute-start | bytes 3145736 | tf_op jit(solution)/shard_map/ppermute | solution.py:1756
  262.6 75.4 %collective-permute-start = (bf16[1024,512]{1,0:T(8,128)(2,1)S(1)}, bf16[1024,512]{1,0:T(8,128)(2,1)}, u32[]{:S(2)}, u32[]{:S(2)}) collective-permute-start(bf16[1024,512]{1,0:T(8,128)(2,1)S(1)} %get-tuple-element.360), channel_id=1, source_target_pairs={{16,0},{17,1},{18,2},{19,3},{20,4},{21,5},{22,6},{23,7},{24,8},{25... | collective-permute-start | bytes 3145736 | tf_op jit(solution)/shard_map/ppermute | solution.py:1756
  266.6 37.2 %copy-start.18 = (bf16[2048,1024]{1,0:T(8,128)(2,1)S(1)}, bf16[2048,1024]{1,0:T(8,128)(2,1)}, u32[]{:S(2)}) copy-start(bf16[2048,1024]{1,0:T(8,128)(2,1)} %get-tuple-element.196) | copy-start | bytes 12582916 | tf_op jit(solution)/shard_map/cond
  335.7 2.3 copy-start.42
  335.7 28.2 %collective-permute-start.3 = (bf16[1024,512]{1,0:T(8,128)(2,1)}, bf16[1024,512]{1,0:T(8,128)(2,1)}, u32[]{:S(2)}, u32[]{:S(2)}) collective-permute-start(bf16[1024,512]{1,0:T(8,128)(2,1)} %get-tuple-element.367), channel_id=1, source_target_pairs={{0,16},{1,17},{2,18},{3,19},{4,20},{5,21},{6,22},{7,23},{8,24},{9,... | collective-permute-start | bytes 3145736 | tf_op jit(solution)/shard_map/ppermute | solution.py:1794
  361.5 24.4 %collective-permute-start.1 = (bf16[1024,512]{1,0:T(8,128)(2,1)}, bf16[1024,512]{1,0:T(8,128)(2,1)}, u32[]{:S(2)}, u32[]{:S(2)}) collective-permute-start(bf16[1024,512]{1,0:T(8,128)(2,1)} %get-tuple-element.365), channel_id=1, source_target_pairs={{0,16},{1,17},{2,18},{3,19},{4,20},{5,21},{6,22},{7,23},{8,24},{9,... | collective-permute-start | bytes 3145736 | tf_op jit(solution)/shard_map/ppermute | solution.py:1794
  443.3 23.0 %copy-start.39 = (s32[4]{0:T(128)S(1)}, s32[4]{0:T(128)}, u32[]{:S(2)}) copy-start(s32[4]{0:T(128)} %constant.143.clone) | copy-start | bytes 52
  463.7 55.5 %copy-start.30 = (f32[2,1024]{1,0:T(2,128)}, f32[2,1024]{1,0:T(2,128)S(1)}, u32[]{:S(2)}) copy-start(f32[2,1024]{1,0:T(2,128)S(1)} %get-tuple-element.400) | copy-start | bytes 24580
  463.7 55.5 %collective-permute-start.5 = (bf16[1024,512]{1,0:T(8,128)(2,1)}, bf16[1024,512]{1,0:T(8,128)(2,1)S(1)}, u32[]{:S(2)}, u32[]{:S(2)}) collective-permute-start(bf16[1024,512]{1,0:T(8,128)(2,1)} %get-tuple-element.375), channel_id=1, source_target_pairs={{16,0},{17,1},{18,2},{19,3},{20,4},{21,5},{22,6},{23,7},{24,8},{25... | collective-permute-start | bytes 3145736 | tf_op jit(solution)/shard_map/ppermute | solution.py:1849
  465.0 87.8 %collective-permute-start.4 = (bf16[1024,512]{1,0:T(8,128)(2,1)}, bf16[1024,512]{1,0:T(8,128)(2,1)S(1)}, u32[]{:S(2)}, u32[]{:S(2)}) collective-permute-start(bf16[1024,512]{1,0:T(8,128)(2,1)} %get-tuple-element.374), channel_id=1, source_target_pairs={{16,0},{17,1},{18,2},{19,3},{20,4},{21,5},{22,6},{23,7},{24,8},{25... | collective-permute-start | bytes 3145736 | tf_op jit(solution)/shard_map/ppermute | solution.py:1849
  550.5 41.9 %collective-permute-start.7 = (bf16[1024,512]{1,0:T(8,128)(2,1)}, bf16[1024,512]{1,0:T(8,128)(2,1)}, u32[]{:S(2)}, u32[]{:S(2)}) collective-permute-start(bf16[1024,512]{1,0:T(8,128)(2,1)} %get-tuple-element.386), channel_id=1, source_target_pairs={{0,16},{1,17},{2,18},{3,19},{4,20},{5,21},{6,22},{7,23},{8,24},{9,... | collective-permute-start | bytes 3145736 | tf_op jit(solution)/shard_map/ppermute | solution.py:1870
  552.7 33.7 %copy-start.29 = (f32[1024]{0:T(1024)S(1)}, f32[1024]{0:T(1024)}, u32[]{:S(2)}) copy-start(f32[1024]{0:T(1024)} %copy-done.28) | copy-start | bytes 12292
  552.8 35.2 %copy-start.38 = (s32[3]{0:T(128)S(1)}, s32[3]{0:T(128)}, u32[]{:S(2)}) copy-start(s32[3]{0:T(128)} %constant.163) | copy-start | bytes 40
  584.1 22.5 %collective-permute-start.6 = (bf16[1024,512]{1,0:T(8,128)(2,1)}, bf16[1024,512]{1,0:T(8,128)(2,1)}, u32[]{:S(2)}, u32[]{:S(2)}) collective-permute-start(bf16[1024,512]{1,0:T(8,128)(2,1)} %get-tuple-element.385), channel_id=1, source_target_pairs={{0,16},{1,17},{2,18},{3,19},{4,20},{5,21},{6,22},{7,23},{8,24},{9,... | collective-permute-start | bytes 3145736 | tf_op jit(solution)/shard_map/ppermute | solution.py:1870
  589.2 1.6 copy-start.15
  590.8 15.8 %copy-start.17 = (bf16[2,4,2,2,64,1024]{5,4,3,2,1,0:T(8,128)(2,1)S(1)}, bf16[2,4,2,2,64,1024]{5,4,3,2,1,0:T(8,128)(2,1)}, u32[]{:S(2)}) copy-start(bf16[2,4,2,2,64,1024]{5,4,3,2,1,0:T(8,128)(2,1)} %get-tuple-element.358) | copy-start | bytes 12582916
  590.8 15.8 %copy-start.43 = (bf16[1024,1024]{1,0:T(8,128)(2,1)S(1)}, bf16[1024,1024]{1,0:T(8,128)(2,1)}, u32[]{:S(2)}) copy-start(bf16[1024,1024]{1,0:T(8,128)(2,1)} %get-tuple-element.380) | copy-start | bytes 6291460
  606.8 2.4 copy-start.44
  606.8 2.4 copy-start.46
  617.0 2.0 copy-start.7
  646.8 4.8 copy-start.45
  656.5 2.0 copy-start.19
  656.5 9.6 copy-start.13
  658.5 2.9 copy-start
  661.4 4.7 copy-start.12
  666.1 3.8 copy-start.6
  666.1 3.8 copy-start.41
  669.9 2.4 copy-start.10
  672.3 62.0 %copy-start.40 = (bf16[4,256,1024]{2,1,0:T(8,128)(2,1)S(1)}, bf16[4,256,1024]{2,1,0:T(8,128)(2,1)}, u32[]{:S(2)}) copy-start(bf16[4,256,1024]{2,1,0:T(8,128)(2,1)} %get-tuple-element.354) | copy-start | bytes 6291460
  734.3 12.9 %copy-start.35 = (s32[16]{0:T(128)S(1)}, s32[16]{0:T(128)}, u32[]{:S(2)}) copy-start(s32[16]{0:T(128)} %add.157) | copy-start | bytes 196
  759.6 15.2 %copy-start.22 = (bf16[1024,1024]{1,0:T(8,128)(2,1)S(1)}, bf16[1024,1024]{1,0:T(8,128)(2,1)}, u32[]{:S(2)}) copy-start(bf16[1024,1024]{1,0:T(8,128)(2,1)} %copy-done.21) | copy-start | bytes 6291460
  774.8 15.0 %copy-start.31 = (f32[2,1024]{1,0:T(2,128)S(1)}, f32[2,1024]{1,0:T(2,128)}, u32[]{:S(2)}) copy-start(f32[2,1024]{1,0:T(2,128)} %copy-done.30) | copy-start | bytes 24580
  1076.7 4.2 copy-start.20
  1081.0 2.5 copy-start.26
  1081.0 3.6 copy-start.24

commit v4 on v3

--- a/solution.py
+++ b/solution.py
@@ -20,7 +20,9 @@
 LANES = 2 * HS
 ROWS = 256
 CHUNK = 32
-BLOCK = 512
+AHEAD = 1
+FEED_ROWS = 512
+BLOCK = 1024
 MESH = pl.DeviceIdType.MESH
 SCALE = HS ** (-0.5)
 GELU_C = (2.0 / 3.141592653589793) ** 0.5
@@ -610,49 +612,60 @@
     lane = lanes_of(ROWS)
     left = lane < HS
 
-    def block(first_row, key_count, triangle):
+    def score(first_row, key_count, triangle, half):
         queries = wide(queries_ref[pl.ds(first_row, ROWS), :]) * SCALE
-        query_halves = half_tiles(
-            queries, jnp.where(lane == HS, 1.0, 0.0), jnp.where(lane == 0, 1.0, 0.0), left
-        )
+        start = HS if half == 0 else 0
+        mine = left if half == 0 else jnp.logical_not(left)
+        augmented = low(jnp.where(mine, queries, jnp.where(lane == start, 1.0, 0.0)))
+        scores = lax.dot_general(
+            augmented,
+            key_refs[half][pl.ds(0, key_count), :],
+            COL_DIMS,
+            preferred_element_type=jnp.float32,
+        )
+        if triangle:
+            column = lax.broadcasted_iota(jnp.int32, (ROWS, key_count), 1)
+            row = first_row + lax.broadcasted_iota(jnp.int32, (ROWS, key_count), 0)
+            scores = jnp.where(column <= row, scores, NEG)
+        return scores
+
+    def finish(first_row, totals, tops):
+        norm = swap_halves(jnp.where(left, totals[1], totals[0]))
+        mixed_ref[pl.ds(first_row, ROWS), :] = low(jnp.where(left, totals[0], totals[1]) / norm)
+        logs = jnp.where(left, tops[0], tops[1]) + jnp.log(norm)
+        lse_ref[pl.ds(first_row, ROWS), :] = swap_halves(logs)
+
+    def run(triangle):
+        items = []
+        for first_row in range(0, slots, ROWS):
+            for half in range(2):
+                items.append((first_row, first_row + ROWS if triangle else slots, triangle, half))
+        waiting = [score(*item) for item in items[:AHEAD]]
         totals, tops = ([], [])
-        for half in range(2):
-            scores = lax.dot_general(
-                low(query_halves[half]),
-                key_refs[half][pl.ds(0, key_count), :],
-                COL_DIMS,
-                preferred_element_type=jnp.float32,
-            )
-            if triangle:
-                column = lax.broadcasted_iota(jnp.int32, (ROWS, key_count), 1)
-                row = first_row + lax.broadcasted_iota(jnp.int32, (ROWS, key_count), 0)
-                scores = jnp.where(column <= row, scores, NEG)
+        for number, item in enumerate(items):
+            if number + AHEAD < len(items):
+                waiting.append(score(*items[number + AHEAD]))
+            scores = waiting.pop(0)
             top = jnp.max(scores, axis=1, keepdims=True)
             tops.append(top)
             totals.append(
                 jnp.dot(
                     low(jnp.exp(scores - top)),
-                    value_refs[half][pl.ds(0, key_count), :],
+                    value_refs[item[3]][pl.ds(0, item[1]), :],
                     preferred_element_type=jnp.float32,
                 )
             )
-        norm = swap_halves(jnp.where(left, totals[1], totals[0]))
-        mixed_ref[pl.ds(first_row, ROWS), :] = low(jnp.where(left, totals[0], totals[1]) / norm)
-        logs = jnp.where(left, tops[0], tops[1]) + jnp.log(norm)
-        lse_ref[pl.ds(first_row, ROWS), :] = swap_halves(logs)
+            if item[3] == 1:
+                finish(item[0], totals, tops)
+                totals, tops = ([], [])
 
     @pl.when(causal == 0)
     def _():
-        def step(index, carry):
-            block(pl.multiple_of(index * ROWS, ROWS), slots, False)
-            return carry
-
-        lax.fori_loop(0, slots // ROWS, step, 0)
+        run(False)
 
     @pl.when(causal != 0)
     def _():
-        for first_row in range(0, slots, ROWS):
-            block(first_row, first_row + ROWS, True)
+        run(True)
 
 
 def fill_forward(length, keys_in, values, key_refs, value_refs):
@@ -702,63 +715,68 @@
             value = value - found[-1]
         return found
 
-    def block(first_row, key_count, triangle):
+    def prepare(first_row, key_count, triangle, half):
         rows = pl.ds(first_row, ROWS)
         keys = pl.ds(0, key_count)
+        mine = left if half == 0 else jnp.logical_not(left)
+        start = HS if half == 0 else 0
         queries = wide(queries_ref[rows, :]) * SCALE
         grads = wide(grad_ref[rows, :])
         product = grads * wide(mixed_ref[rows, :])
+        delta = jnp.sum(jnp.where(mine, product, 0.0), axis=1, keepdims=True)
         log_parts = parts(lse_ref[rows, :], 3)
+        query_aug = low(jnp.where(mine, queries, extra(start, log_parts, 1.0)))
+        grad_aug = low(jnp.where(mine, grads, extra(start, parts(delta, 2), 0.0)))
+        scores = lax.dot_general(
+            key_refs[half][keys, :], query_aug, COL_DIMS, preferred_element_type=jnp.float32
+        )
+        grad_probs = lax.dot_general(
+            value_refs[half][keys, :], grad_aug, COL_DIMS, preferred_element_type=jnp.float32
+        )
+        return (
+            scores,
+            grad_probs,
+            low(jnp.where(mine, queries, 0.0)),
+            low(jnp.where(mine, grads, 0.0)),
+        )
+
+    def run(triangle):
+        items = []
+        for first_row in range(0, slots, ROWS):
+            for half in range(2):
+                items.append((first_row, first_row + ROWS if triangle else slots, triangle, half))
+        waiting = [prepare(*item) for item in items[:AHEAD]]
         query_total, key_total, value_total = (None, None, None)
-        for half in range(2):
-            mine = left if half == 0 else jnp.logical_not(left)
-            start = HS if half == 0 else 0
-            delta = jnp.sum(jnp.where(mine, product, 0.0), axis=1, keepdims=True)
-            query_aug = low(jnp.where(mine, queries, extra(start, log_parts, 1.0)))
-            grad_aug = low(jnp.where(mine, grads, extra(start, parts(delta, 2), 0.0)))
-            scores = lax.dot_general(
-                key_refs[half][keys, :], query_aug, COL_DIMS, preferred_element_type=jnp.float32
-            )
+        for number, (first_row, key_count, _, half) in enumerate(items):
+            if number + AHEAD < len(items):
+                waiting.append(prepare(*items[number + AHEAD]))
+            scores, grad_probs, query_half, grad_half = waiting.pop(0)
+            keys = pl.ds(0, key_count)
             probs = jnp.exp(scores)
             if triangle:
                 key_pos = lax.broadcasted_iota(jnp.int32, (key_count, ROWS), 0)
                 position = first_row + lax.broadcasted_iota(jnp.int32, (key_count, ROWS), 1)
                 probs = jnp.where(key_pos <= position, probs, 0.0)
-            grad_probs = lax.dot_general(
-                value_refs[half][keys, :], grad_aug, COL_DIMS, preferred_element_type=jnp.float32
-            )
             grad_raw = low(probs * grad_probs)
-            value_part = jnp.dot(
-                low(probs), low(jnp.where(mine, grads, 0.0)), preferred_element_type=jnp.float32
-            )
-            key_part = jnp.dot(
-                grad_raw, low(jnp.where(mine, queries, 0.0)), preferred_element_type=jnp.float32
-            )
+            value_part = jnp.dot(low(probs), grad_half, preferred_element_type=jnp.float32)
+            key_part = jnp.dot(grad_raw, query_half, preferred_element_type=jnp.float32)
             query_part = lax.dot_general(
-                grad_raw, plain_refs[half][keys, :], ROW_DIMS, preferred_element_type=jnp.float32
+                plain_refs[half][keys, :], grad_raw, ROW_DIMS, preferred_element_type=jnp.float32
             )
             if half == 0:
                 query_total, key_total, value_total = (query_part, key_part, value_part)
-            else:
-                query_total = query_total + query_part
-                key_total = key_total + key_part
-                value_total = value_total + value_part
-        value_acc[keys, :] += value_total
-        key_acc[keys, :] += key_total
-        dq_ref[rows, :] = low(query_total)
+                continue
+            value_acc[keys, :] += value_total + value_part
+            key_acc[keys, :] += key_total + key_part
+            dq_ref[pl.ds(first_row, ROWS), :] = low(jnp.transpose(query_total + query_part))
 
     @pl.when(causal == 0)
     def _():
-        def step(index, carry):
-            block(pl.multiple_of(index * ROWS, ROWS), slots, False)
-            return carry
-
-        lax.fori_loop(0, slots // ROWS, step, 0)
+        run(False)
 
     @pl.when(causal != 0)
     def _():
-        for first_row in range(0, slots, ROWS):
-            block(first_row, first_row + ROWS, True)
+        run(True)
 
 
 def fill_backward(length, keys_in, values, key_refs, plain_refs, value_refs):
@@ -998,10 +1016,13 @@
     def _():
         acc[...] = alpha_ref[0] * wide_ref[...] + down_shift_ref[...]
 
-    for first in range(0, slots, ROWS):
-        rows = pl.ds(first, ROWS)
-        pre_act = rows_nt(low_ref[rows, :], in_ref[...]) + bias_ref[...]
-        made, slope = gelu_and_slope(pre_act)
+    starts = list(range(0, slots, FEED_ROWS))
+    waiting = [rows_nt(low_ref[pl.ds(0, FEED_ROWS), :], in_ref[...])]
+    for first in starts:
+        rows = pl.ds(first, FEED_ROWS)
+        if first != starts[-1]:
+            waiting.append(rows_nt(low_ref[pl.ds(first + FEED_ROWS, FEED_ROWS), :], in_ref[...]))
+        made, slope = gelu_and_slope(waiting.pop(0) + bias_ref[...])
         hidden = low(made)
         hidden_ref[rows, :] = hidden
         slope_ref[rows, :] = low(slope)
@@ -1073,9 +1094,13 @@
         acc[...] = alpha_ref[0] * wide_ref[...]
 
     sums = None
-    for first in range(0, slots, ROWS):
-        rows = pl.ds(first, ROWS)
-        made = rows_nt(low_ref[rows, :], down_ref[...]) * wide(slope_ref[rows, :])
+    starts = list(range(0, slots, FEED_ROWS))
+    waiting = [rows_nt(low_ref[pl.ds(0, FEED_ROWS), :], down_ref[...])]
+    for first in starts:
+        rows = pl.ds(first, FEED_ROWS)
+        if first != starts[-1]:
+            waiting.append(rows_nt(low_ref[pl.ds(first + FEED_ROWS, FEED_ROWS), :], down_ref[...]))
+        made = waiting.pop(0) * wide(slope_ref[rows, :])
         grad_pre = low(made)
         pre_ref[rows, :] = grad_pre
         part = jnp.sum(wide(grad_pre), axis=0, keepdims=True)
@@ -1665,6 +1690,90 @@
     return (found[0], found[1], found[2:])
 
 
+def project_norm_kernel(parts, alpha_ref, *refs):
+    lefts, weights = (refs[:parts], refs[parts : 2 * parts])
+    wide_ref, gain_ref, shift_ref, made_ref, low_ref, norm_ref, factor_ref = refs[2 * parts :]
+    total = alpha_ref[0] * wide(wide_ref[...])
+    for left, weight in zip(lefts, weights):
+        total = total + rows_nn(left[...], weight[...])
+    made, normed, factor = layer_norm(total, gain_ref[...], shift_ref[...])
+    made_ref[...] = made
+    low_ref[...] = low(made)
+    norm_ref[...] = normed
+    factor_ref[...] = factor
+
+
+def project_norm(alpha, lefts, weight_rows, rows_wide, gain, shift):
+    slots, width = rows_wide.shape
+    parts = len(lefts)
+    depth = lefts[0].shape[1]
+
+    def rows(columns):
+        return pl.BlockSpec((ROWS, columns), lambda step: (step, 0))
+
+    def part_spec(part):
+        return pl.BlockSpec((depth, width), lambda step: (part, 0))
+
+    return pl.pallas_call(
+        functools.partial(project_norm_kernel, parts),
+        grid=(slots // ROWS,),
+        in_specs=[pl.BlockSpec(memory_space=pltpu.SMEM)]
+        + [rows(depth)] * parts
+        + [part_spec(part) for part in range(parts)]
+        + [rows(width), whole_spec((1, width)), whole_spec((1, width))],
+        out_specs=[rows(width), rows(width), rows(width), rows(1)],
+        out_shape=[
+            jax.ShapeDtypeStruct((slots, width), F32),
+            jax.ShapeDtypeStruct((slots, width), BF16),
+            jax.ShapeDtypeStruct((slots, width), F32),
+            jax.ShapeDtypeStruct((slots, 1), F32),
+        ],
+        compiler_params=pltpu.CompilerParams(
+            dimension_semantics=("arbitrary",), vmem_limit_bytes=32 * 1024 * 1024
+        ),
+        cost_estimate=pl.CostEstimate(
+            flops=2 * slots * width * depth * parts,
+            bytes_accessed=16 * slots * width,
+            transcendentals=slots,
+        ),
+    )(alpha, *lefts, *([weight_rows] * parts), rows_wide, gain, shift)
+
+
+def project_add_kernel(alpha_ref, left_ref, weight_ref, wide_ref, made_ref):
+    made_ref[...] = low(
+        alpha_ref[0] * wide(wide_ref[...]) + rows_nn(left_ref[...], weight_ref[...])
+    )
+
+
+def project_add(alpha, left, weight_rows, rows_wide):
+    slots, width = rows_wide.shape
+    depth = left.shape[1]
+
+    def rows(columns):
+        return pl.BlockSpec((ROWS, columns), lambda step: (step, 0))
+
+    return pl.pallas_call(
+        project_add_kernel,
+        grid=(slots // ROWS,),
+        in_specs=[
+            pl.BlockSpec(memory_space=pltpu.SMEM),
+            rows(depth),
+            whole_spec((depth, width)),
+            rows(width),
+        ],
+        out_specs=rows(width),
+        out_shape=jax.ShapeDtypeStruct((slots, width), BF16),
+        compiler_params=pltpu.CompilerParams(
+            dimension_semantics=("arbitrary",), vmem_limit_bytes=40 * 1024 * 1024
+        ),
+        cost_estimate=pl.CostEstimate(
+            flops=2 * slots * width * depth,
+            bytes_accessed=6 * slots * width + 2 * depth * (slots + width),
+            transcendentals=0,
+        ),
+    )(alpha, left, weight_rows, rows_wide)
+
+
 def after(value, *earlier):
     return lax.optimization_barrier((value, earlier))[0]
 
@@ -1736,10 +1845,9 @@
 
     qkv = low(rows_nt(x, qkv_rows))
     mixed, lse_self = self_attention(self_scalars, qkv, 0, pairs)
-    resid_a, norm_a, factor_a = layer_norm(
-        alpha * x.astype(jnp.float32) + rows_nn(mixed, out_rows), gains[0], shifts[0]
-    )
-    a_low = low(resid_a)
+    resid_a, a_low, norm_a, factor_a = project_norm(
+        alpha_row, [mixed], out_rows, x, gains[0:1], shifts[0:1]
+    )
 
     def zeros_like_of(branch):
         shapes = jax.eval_shape(branch)
@@ -1747,13 +1855,10 @@
 
     def dec_query():
         first = cross_parts[:, 0].reshape(-1, width)
-        made = low(rows_nt(a_low, first))
-        return (made[:, :half], made[:, half:], first, cross_parts[:, 1].reshape(-1, width))
-
-    query_left, query_right, cross_first, cross_second = lax.cond(
-        decoder, dec_query, zeros_like_of(dec_query)
-    )
-    query_held = [lax.ppermute(piece, "section", [(1, 0)]) for piece in (query_left, query_right)]
+        return tuple(low(rows_nt(a_low, first[side * half : side * half + half])) for side in sides)
+
+    query_sent = lax.cond(decoder, dec_query, zeros_like_of(dec_query))
+    query_held = [lax.ppermute(piece, "section", [(1, 0)]) for piece in query_sent]
     cotangent_rows = exchange_in(1, 2, after(cotangent, query_held)).reshape(slots, width)
 
     def feed(rows_low, rows_wide):
@@ -1800,11 +1905,10 @@
     mixed_held = after(mixed_held, outputs_e)
 
     def dec_middle():
-        crossed = rows_nn(mixed_held[0], cross_second[:half]) + rows_nn(
-            mixed_held[1], cross_second[half:]
-        )
-        resid_c, norm_c, factor_c = layer_norm(alpha * resid_a + crossed, gains[1], shifts[1])
-        c_low = low(resid_c)
+        cross_second = cross_parts[:, 1].reshape(-1, width)
+        resid_c, c_low, norm_c, factor_c = project_norm(
+            alpha_row, mixed_held, cross_second, resid_a, gains[1:2], shifts[1:2]
+        )
         hidden, slopes, decoded_low, norm_y, factor_y = feed(c_low, resid_c)
         grad_y, grad_low, sums_y = norm_back_call(
             target_len.reshape(1), cotangent_rows, norm_y, factor_y, gains[2:3]
@@ -1869,54 +1973,66 @@
         grad_kv.append(kv_made)
         grad_query_held.append(lax.ppermute(query_made, "section", [(0, 1)]))
 
+    def enc_back():
+        grad_memory = rows_nn(grad_kv[0], cross_rows[:width]) + rows_nn(
+            grad_kv[1], cross_rows[width:]
+        )
+        grad_y, grad_low, sums_y = norm_back_call(
+            no_limit, grad_memory, norm_e, factor_e, gains[2:3]
+        )
+        grad_pre, bias_sum, grad_a = feed_back_call(
+            alpha_row, grad_low, grad_y, in_rows, down_rows, slopes_e
+        )
+        return (grad_low, grad_pre, bias_sum, grad_a, sums_y)
+
+    grad_low_e, grad_pre_e, bias_sum_e, grad_a_e, sums_ye = lax.cond(
+        decoder, zeros_like_of(enc_back), enc_back
+    )
+
     outputs_d = exchange_in(1, 4, after(sharded(decoded_low), grad_mixed_held))
     grad_query_held = after(grad_query_held, outputs_d)
     outputs = jnp.where(decoder, outputs_d, outputs_e)
 
-    def enc_back():
-        grad_memory = rows_nn(grad_kv[0], cross_rows[:width]) + rows_nn(
-            grad_kv[1], cross_rows[width:]
-        )
-        grad_y, grad_low, sums_y = norm_back_call(
-            no_limit, grad_memory, norm_e, factor_e, gains[2:3]
-        )
-        grad_pre, bias_sum, grad_a = feed_back_call(
-            alpha_row, grad_low, grad_y, in_rows, down_rows, slopes_e
-        )
+    grad_query_held = after(grad_query_held, grad_a_e)
+
+    def enc_norm():
         made = [rows_tn(piece, memory_low) for piece in grad_kv]
-        return (grad_low, grad_pre, bias_sum, grad_a, sums_y, low(jnp.concatenate(made)))
-
-    def dec_back():
+        return tuple(norm_back_call(no_limit, grad_a_e, norm_a, factor_a, gains[0:1])) + (
+            low(jnp.concatenate(made)),
+        )
+
+    def dec_norm():
         grad_query = jnp.concatenate(grad_query_held, axis=1)
+        cross_first = cross_parts[:, 0].reshape(-1, width)
         grad_a = alpha * grad_mid + rows_nn(grad_query, cross_first)
         mixed_all = jnp.concatenate(mixed_held, axis=1)
         made = [rows_tn(grad_query, a_low), rows_tn(mixed_all, mid_low)]
         made = [piece.reshape(-1, 1, LANES, width) for piece in made]
-        cross_made = low(jnp.concatenate(made, axis=1)).reshape(-1, width)
-        return (grad_low_d, grad_pre_d, bias_sum_d, grad_a, sums_yd, cross_made)
-
-    grad_low, grad_pre, bias_sum, grad_a, sums_y, cross_made = lax.cond(
-        decoder, dec_back, enc_back
-    )
+        return tuple(norm_back_call(no_limit, grad_a, norm_a, factor_a, gains[0:1])) + (
+            low(jnp.concatenate(made, axis=1)).reshape(-1, width),
+        )
+
+    grad_r, r_low, sums_a, cross_made = lax.cond(decoder, dec_norm, enc_norm)
+    bias_sum = jnp.where(decoder, bias_sum_d, bias_sum_e)
+    sums_y = jnp.where(decoder, sums_yd, sums_ye)
 
     def down_grads():
         return lax.cond(
             decoder,
-            lambda: low(rows_tn(hidden_d, grad_low)),
-            lambda: low(rows_tn(hidden_e, grad_low)),
+            lambda: low(rows_tn(hidden_d, grad_low_d)),
+            lambda: low(rows_tn(hidden_e, grad_low_e)),
         )
 
     def in_grads():
         return lax.cond(
             decoder,
-            lambda: low(rows_tn(grad_pre, c_low)),
-            lambda: low(rows_tn(grad_pre, a_low)),
-        )
-
-    grad_r, r_low, sums_a = norm_back_call(no_limit, grad_a, norm_a, factor_a, gains[0:1])
+            lambda: low(rows_tn(grad_pre_d, c_low)),
+            lambda: low(rows_tn(grad_pre_e, a_low)),
+        )
+
     grad_mixed = low(rows_nt(r_low, out_rows))
     grad_qkv = self_attention_back(self_scalars, qkv, mixed, grad_mixed, lse_self, 0, pairs)
-    grad_x = low(alpha * grad_r + rows_nn(grad_qkv, qkv_rows))
+    grad_x = project_add(alpha_row, grad_qkv, qkv_rows, grad_r)
 
     slot_bits = jnp.asarray([0, 2, 1, 3], jnp.int32)[:, None]
     slot_unit = unit ^ slot_bits

time: 1090 us -> 1020 us (0.936)
  Pallas kernels: 790 us -> 747 us
  waiting for transfers between devices: 89.2 us -> 65 us
    pallas_call x6, Pallas kernels: 216 us -> 162 us  [head_call(): pl.pallas_call(kernel, grid_spec=pltpu.PrefetchScalarGridSpec(num_scalar_...]
    ppermute x4, waiting for transfers between devices: 52.9 us -> 36.4 us  [sequence_body(): lax.ppermute(piece, 'section', [(1, 0)])]
    pallas_call x0 -> x2, Pallas kernels: none -> 16.3 us  [the longest x1 10.2 us: project_add(): pl.pallas_call(project_add_kernel, grid=(slots // ROWS,), in_specs=[pl.Bl...]
    dot_general x4 -> x2, matrix products: 22.3 us -> 7.06 us  [rows_nn(): return jnp.dot(rows, weight_rows, preferred_element_type=jnp.float32)]
    ppermute x2, waiting for transfers between devices: 14.2 us -> 0.01 us  [sequence_body(): grad_query_held.append(lax.ppermute(query_made, 'section', [(0, 1)]))]
    another operation x15 -> x12, local copies, waits for them, and re-layouts: 23.3 us -> 19.8 us  [whole(): jax.shard_map(chosen, mesh=mesh, in_specs=placed, out_specs=returned, che...]
  transfers between devices with their start and end apart: 8 -> 8, of which waited for: 3 -> 3; matrix products, arithmetic and copies ran while one was open for 1% -> 5% of each run, Pallas kernels for 13% -> 14%
where the time goes in v4:
time: 1020 us
  Pallas kernels  747 us (73%)
  matrix products  87.4 us (9%)
  local copies, waits for them, and re-layouts  68 us (7%)
  waiting for transfers between devices  65 us (6%)
  other arithmetic  22.9 us (2%)
  starting transfers between devices  13.4 us (1%)
  loops' own time  10.3 us (1%)
    pallas_call x1, Pallas kernels, reduce_all(): pl.pallas_call(functools.partial(reduce_kernel, paired, depths), in_specs...  267 us
    pallas_call x1, Pallas kernels, gather_all(): pl.pallas_call(functools.partial(gather_kernel, paired), in_specs=[anywhe...  174 us
    pallas_call x6, Pallas kernels, head_call(): pl.pallas_call(kernel, grid_spec=pltpu.PrefetchScalarGridSpec(num_scalar_...  162 us
    pallas_call x3, Pallas kernels, exchange_in(): pl.pallas_call(functools.partial(exchange_kernel, active), in_specs=[anyw...  57.5 us
    dot_general x6, matrix products, rows_tn(): lax.dot_general(left_rows, right_rows, ROW_DIMS, preferred_element_type=j...  56.9 us
    ppermute x4, waiting for transfers between devices, sequence_body(): lax.ppermute(piece, 'section', [(1, 0)])  36.4 us
    pallas_call x1, Pallas kernels, feed_call(): pl.pallas_call(feed_kernel, grid=(hidden // block,), in_specs=[pl.BlockSp...  31.5 us
    ppermute x2, waiting for transfers between devices, sequence_body(): mixed_held.append(lax.ppermute(mix_made, 'section', [(0, 1)]))  28.6 us
  transfers between devices with their start and end apart: 8, of which 3 were waited for; matrix products, arithmetic and copies ran while one was open for 5% of the time, Pallas kernels for 14%

profile of v4, /device:TPU:9, one launch (start us, length us, event | category | flops | bytes accessed | tf_op | source)
XLA Modules:
  0.0 1016.4 jit_solution(14818282023237066157)
XLA Ops:
  13.8 173.6 %shard_map.230 = (bf16[4,256,1024]{2,1,0:T(8,128)(2,1)}, bf16[2,4,2,192,1024]{4,3,2,1,0:T(8,128)(2,1)}, bf16[2,4,2,64,1024]{4,3,2,1,0:T(8,128)(2,1)}, bf16[2,4,2...) custom-call(bf16[4,256,1024]{2,1,0:T(8,128)(2,1)} %bitcast.170, ...), custom_call_target="tpu_custom_call" | custom-call | tf_op jit(solution)/shard_map/pallas_call | solution.py:1356
  187.4 11.4 %convolution_convert_fusion.10.packed_ref = bf16[1024,3072]{1,0:T(8,128)(2,1)} fusion(bf16[1024,1024]{1,0:T(8,128)(2,1)} %bitcast.148, bf16[3072,1024]{1,0:T(8,128)(2,1)} %bitcast.194), kind=kOutput, calls=%fused_computation.27 | convolution fusion | flops 6445596672 | bytes 14680064 | tf_op jit(solution)/shard_map/dot_general | solution.py:976
  200.7 29.1 %shard_map.231 = (bf16[1024,1024]{1,0:T(8,128)(2,1)S(1)}, f32[1024,1024]{1,0:T(8,128)}) custom-call(s32[2]{0:T(128)S(1)} %pad_add_fusion.1.scalars, bf16[1024,3072]{1,0:T(8,128)(2,1)} %convolution_convert_fusion.10.packed_ref), custom_call_target="tpu_custom_call" | custom-call | flops 34359738368 | bytes 6291456 | tf_op jit(solution)/shard_map/pallas_call | solution.py:886
  234.9 6.1 shard_map.232
  245.7 40.9 %conditional.21 = (bf16[1024,4096]{1,0:T(8,128)(2,1)}, bf16[1024,4096]{1,0:T(8,128)(2,1)}, bf16[1024,1024]{1,0:T(8,128)(2,1)}, f32[1024,1024]{1,0:T(8,128)}, f32...) conditional(s32[]{:T(128)} %convert_element_type.102, (f32[3,1024]{1,0:T(4,128)S(1)}, f32[3,1024]{1,0:T(4,128)S(1)}, ...), branch_computations={%region_2.3_spmd, %region_3.4_spmd} | conditional | flops 21476933632 | bytes 60833868 | solution.py:1882
  246.9 31.5 %branch_0_fun.8 = (bf16[1024,4096]{1,0:T(8,128)(2,1)}, bf16[1024,4096]{1,0:T(8,128)(2,1)}, bf16[1024,1024]{1,0:T(8,128)(2,1)}, f32[1024,1024]{1,0:T(8,128)}, f32[1024,1]{1,0:T(8,128)S(1)}) custom-call(f32[1]{0:T(128)} %get-tuple-element.185.alpha_ref, bf16[1024,1024]{1,0:T(8,128)(2,1)} %get-tuple-element.186.low_ref, ...), custom_call_target="tpu_custom_call" | custom-call | flops 17179869184 | bytes 33554432 | tf_op jit(solution)/shard_map/cond/branch_0_fun/pallas_call | solution.py:1052
  278.4 7.8 convolution_convert_fusion.2
  287.4 14.6 %conditional.23 = ((bf16[1024,512]{1,0:T(8,128)(2,1)S(1)}, f32[1024,512]{1,0:T(8,128)})) conditional(s32[]{:T(128)} %convert_element_type.102, (s32[2]{0:T(128)S(1)}, bf16[1024,512]{1,0:T(8,128)(2,1)}, bf16[1024,2048]{1,0:T(8,128)(2,1)}) %tuple.119, () %tuple.120), branch_computations={%region_6.7_spmd, %region_7.8_spmd} | conditional | flops 17179869184 | bytes 3145758 | solution.py:1896
  287.4 14.6 %branch_0_fun.10 = (bf16[1024,512]{1,0:T(8,128)(2,1)S(1)}, f32[1024,512]{1,0:T(8,128)}) custom-call(s32[2]{0:T(128)S(1)} %get-tuple-element.203.scalars, bf16[1024,512]{1,0:T(8,128)(2,1)} %get-tuple-element.204.query_ref, bf16[1024,2048]{1,0:T(8,128)(2,1)} %get-tuple-element.205.key_ref.value_ref, bf16[1024,2048]{1,0:T(8,128)(2,1)} %get-tuple-element.205.key_ref.value_ref), custom_call_target="tpu_custom_call" | custom-call | flops 17179869184 | bytes 3145728 | tf_op jit(solution)/shard_map/cond/branch_0_fun/pallas_call | solution.py:886
  304.3 14.6 %conditional.22 = ((bf16[1024,512]{1,0:T(8,128)(2,1)}, f32[1024,512]{1,0:T(8,128)})) conditional(s32[]{:T(128)} %convert_element_type.102, (s32[2]{0:T(128)S(1)}, bf16[1024,512]{1,0:T(8,128)(2,1)}, bf16[1024,2048]{1,0:T(8,128)(2,1)}) %tuple.117, () %tuple.118), branch_computations={%region_4.5_spmd, %region_5.6_spmd} | conditional | flops 17179869184 | bytes 3145758 | solution.py:1896
  304.4 14.6 %branch_0_fun.9 = (bf16[1024,512]{1,0:T(8,128)(2,1)}, f32[1024,512]{1,0:T(8,128)}) custom-call(s32[2]{0:T(128)S(1)} %get-tuple-element.200.scalars, bf16[1024,512]{1,0:T(8,128)(2,1)} %get-tuple-element.201.query_ref, bf16[1024,2048]{1,0:T(8,128)(2,1)} %get-tuple-element.202.key_ref.value_ref, bf16[1024,2048]{1,0:T(8,128)(2,1)} %get-tuple-element.202.key_ref.value_ref), custom_call_target="tpu_custom_call" | custom-call | flops 17179869184 | bytes 3145728 | tf_op jit(solution)/shard_map/cond/branch_0_fun/pallas_call | solution.py:886
  321.3 6.1 collective-permute-done.3
  327.4 22.5 %collective-permute-done.1 = bf16[1024,512]{1,0:T(8,128)(2,1)} collective-permute-done((bf16[1024,512]{1,0:T(8,128)(2,1)}, bf16[1024,512]{1,0:T(8,128)(2,1)}, u32[]{:S(2)}, u32[]{:S(2)}) %collective-permute-start.1) | collective-permute-done | bytes 1048608 | tf_op jit(solution)/shard_map/ppermute | solution.py:1899
  349.9 57.4 %shard_map.233 = bf16[4,256,1024]{2,1,0:T(8,128)(2,1)} custom-call(bf16[4,256,1024]{2,1,0:T(8,128)(2,1)} %bitcast.53.blocks), custom_call_target="tpu_custom_call" | custom-call | tf_op jit(solution)/shard_map/pallas_call | solution.py:1407
  407.3 29.4 %conditional.24 = (bf16[1024,4096]{1,0:T(8,128)(2,1)}, bf16[1024,1024]{1,0:T(8,128)(2,1)}, bf16[1024,1024]{1,0:T(8,128)(2,1)}, bf16[1024,4096]{1,0:T(8,128)(2,1)...) conditional(s32[]{:T(128)} %convert_element_type.102, ...), branch_computations={%region_8.9_spmd, %region_9.10_spmd} | conditional | flops 38655754240 | bytes 209797472 | solution.py:1952
  407.3 4.3 broadcast.114
  411.6 4.3 broadcast.114.clone
  415.9 2.7 broadcast.117
  440.1 36.4 %collective-permute-done.5 = bf16[1024,512]{1,0:T(8,128)(2,1)} collective-permute-done((bf16[1024,512]{1,0:T(8,128)(2,1)}, bf16[1024,512]{1,0:T(8,128)(2,1)}, u32[]{:S(2)}, u32[]{:S(2)}) %collective-permute-start.5) | collective-permute-done | bytes 1048608 | tf_op jit(solution)/shard_map/ppermute | solution.py:1953
  476.5 25.8 %conditional.26 = ((bf16[1024,512]{1,0:T(8,128)(2,1)}, bf16[1024,1024]{1,0:T(8,128)(2,1)})) conditional(s32[]{:T(128)} %convert_element_type.102, (s32[2]{0:T(128)S(1)}, bf16[1024,512]{1,0:T(8,128)(2,1)}, bf16[1024,2048]{1,0:T(8,128)(2,1)}, bf16[1024,512]{1,0:T(8,128)(2,1)}, bf16[1024,512]{1,0:T(8,128)(2,1)}, ...), branch_computations={%region_12.13_spmd, %region_13.14_spmd} | conditional | flops 42949672960 | bytes 6291464 | solution.py:1972
  476.5 25.8 %branch_0_fun.12 = (bf16[1024,512]{1,0:T(8,128)(2,1)}, bf16[1024,1024]{1,0:T(8,128)(2,1)}) custom-call(s32[2]{0:T(128)S(1)} %get-tuple-element.243.scalars, bf16[1024,512]{1,0:T(8,128)(2,1)} %get-tuple-element.244.query_ref, bf16[1024,2048]{1,0:T(8,128)(2,1)} %get-tuple-element.245.key_ref.value_ref, ...), custom_call_target="tpu_custom_call" | custom-call | flops 42949672960 | bytes 6291456 | tf_op jit(solution)/shard_map/cond/branch_0_fun/pallas_call | solution.py:886
  504.6 25.8 %conditional.25 = ((bf16[1024,512]{1,0:T(8,128)(2,1)}, bf16[1024,1024]{1,0:T(8,128)(2,1)})) conditional(s32[]{:T(128)} %convert_element_type.102, (s32[2]{0:T(128)S(1)}, bf16[1024,512]{1,0:T(8,128)(2,1)}, bf16[1024,2048]{1,0:T(8,128)(2,1)}, bf16[1024,512]{1,0:T(8,128)(2,1)}, bf16[1024,512]{1,0:T(8,128)(2,1)}, ...), branch_computations={%region_10.11_spmd, %region_11.12_spmd} | conditional | flops 42949672960 | bytes 6291464 | solution.py:1972
  504.6 25.8 %branch_0_fun.11 = (bf16[1024,512]{1,0:T(8,128)(2,1)}, bf16[1024,1024]{1,0:T(8,128)(2,1)}) custom-call(s32[2]{0:T(128)S(1)} %get-tuple-element.237.scalars, bf16[1024,512]{1,0:T(8,128)(2,1)} %get-tuple-element.238.query_ref, bf16[1024,2048]{1,0:T(8,128)(2,1)} %get-tuple-element.239.key_ref.value_ref, ...), custom_call_target="tpu_custom_call" | custom-call | flops 42949672960 | bytes 6291456 | tf_op jit(solution)/shard_map/cond/branch_0_fun/pallas_call | solution.py:886
  533.3 42.0 %conditional.27 = (bf16[1024,1024]{1,0:T(8,128)(2,1)}, bf16[1024,4096]{1,0:T(8,128)(2,1)}, f32[1,4096]{1,0:T(1,128)S(1)}, f32[1024,1024]{1,0:T(8,128)}, f32[8,1024]{1,0:T(8,128)S(1)}) conditional(s32[]{:T(128)} %convert_element_type.102, (bf16[2048,1024]{1,0:T(8,128)(2,1)}, bf16[1024,1024]{1,0:T(8,128)(2,1)}, bf16[1024,1024]{1,0:T(8,128)(2,1)}, ...), branch_computations={%region_14.15_spmd, %region_15.16_spmd} | conditional | flops 21475885056 | bytes 96477304 | solution.py:1988
  533.7 4.7 fusion
  538.4 2.4 fusion.4.grad_ref
  540.8 5.5 branch_0_fun.13
  548.3 26.9 %branch_0_fun.14 = (bf16[1024,4096]{1,0:T(8,128)(2,1)}, f32[1,4096]{1,0:T(1,128)S(1)}, f32[1024,1024]{1,0:T(8,128)}) custom-call(f32[1]{0:T(128)} %get-tuple-element.256.alpha_ref, bf16[1024,1024]{1,0:T(8,128)(2,1)} %get-tuple-element.589.low_ref, f32[1024,1024]{1,0:T(8,128)} %copy-done.7, bf16[4096,1024]{1,0:T(8,128)(2,1)} %get-tuple-element.258.in_ref, ...), custom_call_target="tpu_custom_call" | custom-call | flops 17179869184 | bytes 33554432 | tf_op jit(solution)/shard_map/cond/branch_0_fun/pallas_call | solution.py:1123
  576.2 15.2 %conditional.30 = (bf16[2,4,2,256,1024]{4,3,2,1,0:T(8,128)(2,1)}) conditional(s32[]{:T(128)} %convert_element_type.102, (bf16[1024,4096]{1,0:T(8,128)(2,1)}, bf16[1024,1024]{1,0:T(8,128)(2,1)}) %tuple.138, (bf16[1024,4096]{1,0:T(8,128)(2,1)}, bf16[1024,1024]{1,0:T(8,128)(2,1)}) %tuple.139), branch_computations={%region_20.21_spmd, %region_21.22_spmd} | conditional | flops 8594128896 | bytes 18874376 | solution.py:2020
  576.3 15.0 %convolution_convert_fusion.7 = bf16[4096,1024]{1,0:T(8,128)(2,1)} fusion(bf16[1024,4096]{1,0:T(8,128)(2,1)} %get-tuple-element.294, bf16[1024,1024]{1,0:T(8,128)(2,1)} %get-tuple-element.295), kind=kOutput, calls=%fused_computation.24 | convolution fusion | flops 8594128896 | bytes 18874368 | tf_op jit(solution)/shard_map/cond/branch_0_fun/dot_general | solution.py:984
  591.4 15.2 %conditional.29 = (bf16[2,4,2,256,1024]{4,3,2,1,0:T(8,128)(2,1)}) conditional(s32[]{:T(128)} %convert_element_type.102, (bf16[1024,4096]{1,0:T(8,128)(2,1)}, bf16[1024,1024]{1,0:T(8,128)(2,1)}) %tuple.136, (bf16[1024,4096]{1,0:T(8,128)(2,1)}, bf16[1024,1024]{1,0:T(8,128)(2,1)}) %tuple.137), branch_computations={%region_18.19_spmd, %region_19.20_spmd} | conditional | flops 8594128896 | bytes 18874376 | solution.py:2027
  591.6 15.0 %convolution_convert_fusion.5 = bf16[4096,1024]{1,0:T(8,128)(2,1)} fusion(bf16[1024,4096]{1,0:T(8,128)(2,1)} %get-tuple-element.290, bf16[1024,1024]{1,0:T(8,128)(2,1)} %get-tuple-element.291), kind=kOutput, calls=%fused_computation.22 | convolution fusion | flops 8594128896 | bytes 18874368 | tf_op jit(solution)/shard_map/cond/branch_0_fun/dot_general | solution.py:984
  608.0 3.3 select_bitcast_fusion
  612.0 17.3 %conditional.28 = (f32[1024,1024]{1,0:T(8,128)}, bf16[1024,1024]{1,0:T(8,128)(2,1)S(1)}, f32[8,1024]{1,0:T(8,128)S(1)}, bf16[2,4,2,2,64,1024]{5,4,3,2,1,0:T(8,128)(2,1)S(1)}) conditional(s32[]{:T(128)} %convert_element_type.102, (f32[3,1024]{1,0:T(4,128)S(1)}, f32[1024,1024]{1,0:T(8,128)}, f32[1024,1024]{1,0:T(8,128)}, f32[1024,1]{1,0:T(8,128)S(1)}, ...), branch_computations={%region_16.17_spmd, %region_17.18_spmd} | conditional | flops 6450839552 | bytes 67117120 | solution.py:2124
  612.0 4.8 fusion.26
  616.8 4.0 fusion.27
  623.0 5.8 branch_0_fun.15
  630.6 6.2 convolution_convert_fusion.11
  636.8 4.1 convolution_convert_fusion.12.grad_ref
  641.0 52.4 %shard_map.236.left_ref = bf16[1024,3072]{1,0:T(8,128)(2,1)} custom-call(s32[2]{0:T(128)S(1)} %copy-done.12, bf16[1024,3072]{1,0:T(8,128)(2,1)} %convolution_convert_fusion.10.packed_ref, bf16[1024,1024]{1,0:T(8,128)(2,1)S(1)} %copy-done.15, bf16[1024,1024]{1,0:T(8,128)(2,1)S(1)} %convolution_convert_fusion.12.grad_ref, f32[1024,1024]{1,0:T(8,128)} %get-tuple-element.418.lse_ref), custom_call_target="tpu_custom_call" | custom-call | flops 85899345920 | bytes 12582912 | tf_op jit(solution)/shard_map/pallas_call | solution.py:886
  693.4 11.8 %convolution_convert_fusion.9 = bf16[3072,1024]{1,0:T(8,128)(2,1)} fusion(bf16[1024,3072]{1,0:T(8,128)(2,1)} %shard_map.236.left_ref, bf16[1024,1024]{1,0:T(8,128)(2,1)S(1)} %bitcast.150), kind=kOutput, calls=%fused_computation.26 | convolution fusion | flops 6445596672 | bytes 14680064 | tf_op jit(solution)/shard_map/dot_general | solution.py:984
  705.2 10.2 %shard_map.237 = bf16[1024,1024]{1,0:T(8,128)(2,1)S(1)} custom-call(f32[1]{0:T(128)} %bitcast.38.alpha_ref, bf16[1024,3072]{1,0:T(8,128)(2,1)S(1)} %copy-done.16, bf16[3072,1024]{1,0:T(8,128)(2,1)} %bitcast.195, f32[1024,1024]{1,0:T(8,128)S(1)} %copy-done.48), custom_call_target="tpu_custom_call" | custom-call | flops 6442450944 | bytes 18874368 | tf_op jit(solution)/shard_map/pallas_call | solution.py:1755
  718.1 267.4 %shard_map.238 = (bf16[4,256,1024]{2,1,0:T(8,128)(2,1)}, f32[16,1024]{1,0:T(8,128)}, bf16[4,192,1024]{2,1,0:T(8,128)(2,1)}, bf16[4,64,1024]{2,1,0:T(8,128)(2,1)}...) custom-call(bf16[4,256,1024]{2,1,0:T(8,128)(2,1)} %bitcast.147, ...), custom_call_target="tpu_custom_call" | custom-call | tf_op jit(solution)/shard_map/pallas_call | solution.py:1649
  987.7 4.1 bitcast_convert_fusion.1
  991.8 5.5 copy.49
  999.4 3.6 copy.47
  1005.1 4.2 bitcast_convert_fusion
  1009.4 2.5 bitcast_convert_fusion.2
  (168 shorter events, 71.2 us)
Async XLA Ops:
  2.0 4.3 copy-start.44
  6.2 3.8 copy-start.37
  8.1 3.7 copy-start.45
  8.1 3.7 copy-start.41
  8.1 3.7 copy-start.42
  8.1 3.7 copy-start.38
  200.7 31.0 %copy-start.8 = (bf16[4,256,1024]{2,1,0:T(8,128)(2,1)S(1)}, bf16[4,256,1024]{2,1,0:T(8,128)(2,1)}, u32[]{:S(2)}) copy-start(bf16[4,256,1024]{2,1,0:T(8,128)(2,1)} %get-tuple-element.376) | copy-start | bytes 6291460
  231.7 1.6 copy-start.9
  233.3 1.6 copy-start.14
  234.9 6.2 copy-start.17
  241.0 4.6 copy-start.43
  242.2 45.2 %collective-permute-start.2 = (bf16[1024,512]{1,0:T(8,128)(2,1)S(1)}, bf16[1024,512]{1,0:T(8,128)(2,1)}, u32[]{:S(2)}, u32[]{:S(2)}) collective-permute-start(bf16[1024,512]{1,0:T(8,128)(2,1)S(1)} %get-tuple-element.388), channel_id=1, source_target_pairs={{16,0},{17,1},{18,2},{19,3},{20,4},{21,5},{22,6},{23,7},{24,8},{25... | collective-permute-start | bytes 3145736 | tf_op jit(solution)/shard_map/ppermute | solution.py:1861
  243.5 60.8 %collective-permute-start = (bf16[1024,512]{1,0:T(8,128)(2,1)}, bf16[1024,512]{1,0:T(8,128)(2,1)}, u32[]{:S(2)}, u32[]{:S(2)}) collective-permute-start(bf16[1024,512]{1,0:T(8,128)(2,1)} %get-tuple-element.381), channel_id=1, source_target_pairs={{16,0},{17,1},{18,2},{19,3},{20,4},{21,5},{22,6},{23,7},{24,8},{25... | collective-permute-start | bytes 3145736 | tf_op jit(solution)/shard_map/ppermute | solution.py:1861
  246.9 31.5 %copy-start.19 = (bf16[2048,1024]{1,0:T(8,128)(2,1)S(1)}, bf16[2048,1024]{1,0:T(8,128)(2,1)}, u32[]{:S(2)}) copy-start(bf16[2048,1024]{1,0:T(8,128)(2,1)} %get-tuple-element.199) | copy-start | bytes 12582916 | tf_op jit(solution)/shard_map/cond
  303.0 24.4 %collective-permute-start.3 = (bf16[1024,512]{1,0:T(8,128)(2,1)}, bf16[1024,512]{1,0:T(8,128)(2,1)S(1)}, u32[]{:S(2)}, u32[]{:S(2)}) collective-permute-start(bf16[1024,512]{1,0:T(8,128)(2,1)} %copy-done.50), channel_id=1, source_target_pairs={{0,16},{1,17},{2,18},{3,19},{4,20},{5,21},{6,22},{7,23},{8,24},{9,... | collective-permute-start | bytes 3145736 | tf_op jit(solution)/shard_map/ppermute | solution.py:1899
  318.9 30.9 %collective-permute-start.1 = (bf16[1024,512]{1,0:T(8,128)(2,1)}, bf16[1024,512]{1,0:T(8,128)(2,1)}, u32[]{:S(2)}, u32[]{:S(2)}) collective-permute-start(bf16[1024,512]{1,0:T(8,128)(2,1)} %get-tuple-element.387), channel_id=1, source_target_pairs={{0,16},{1,17},{2,18},{3,19},{4,20},{5,21},{6,22},{7,23},{8,24},{9,... | collective-permute-start | bytes 3145736 | tf_op jit(solution)/shard_map/ppermute | solution.py:1899
  327.4 79.9 %copy-start.31 = (bf16[1024,512]{1,0:T(8,128)(2,1)}, bf16[1024,512]{1,0:T(8,128)(2,1)S(1)}, u32[]{:S(2)}) copy-start(bf16[1024,512]{1,0:T(8,128)(2,1)S(1)} %collective-permute-done.3) | copy-start | bytes 3145732
  407.2 32.1 %copy-start.47 = (s32[4]{0:T(128)S(1)}, s32[4]{0:T(128)}, u32[]{:S(2)}) copy-start(s32[4]{0:T(128)} %constant.136.clone) | copy-start | bytes 52
  436.7 39.8 %collective-permute-start.5 = (bf16[1024,512]{1,0:T(8,128)(2,1)}, bf16[1024,512]{1,0:T(8,128)(2,1)}, u32[]{:S(2)}, u32[]{:S(2)}) collective-permute-start(bf16[1024,512]{1,0:T(8,128)(2,1)} %get-tuple-element.397), channel_id=1, source_target_pairs={{16,0},{17,1},{18,2},{19,3},{20,4},{21,5},{22,6},{23,7},{24,8},{25... | collective-permute-start | bytes 3145736 | tf_op jit(solution)/shard_map/ppermute | solution.py:1953
  438.0 66.6 %collective-permute-start.4 = (bf16[1024,512]{1,0:T(8,128)(2,1)}, bf16[1024,512]{1,0:T(8,128)(2,1)}, u32[]{:S(2)}, u32[]{:S(2)}) collective-permute-start(bf16[1024,512]{1,0:T(8,128)(2,1)} %get-tuple-element.396), channel_id=1, source_target_pairs={{16,0},{17,1},{18,2},{19,3},{20,4},{21,5},{22,6},{23,7},{24,8},{25... | collective-permute-start | bytes 3145736 | tf_op jit(solution)/shard_map/ppermute | solution.py:1953
  502.3 108.9 %collective-permute-start.7 = (bf16[1024,512]{1,0:T(8,128)(2,1)}, bf16[1024,512]{1,0:T(8,128)(2,1)}, u32[]{:S(2)}, u32[]{:S(2)}) collective-permute-start(bf16[1024,512]{1,0:T(8,128)(2,1)} %get-tuple-element.411), channel_id=1, source_target_pairs={{0,16},{1,17},{2,18},{3,19},{4,20},{5,21},{6,22},{7,23},{8,24},{9,... | collective-permute-start | bytes 3145736 | tf_op jit(solution)/shard_map/ppermute | solution.py:1974
  504.6 28.1 %copy-start.46 = (s32[3]{0:T(128)S(1)}, s32[3]{0:T(128)}, u32[]{:S(2)}) copy-start(s32[3]{0:T(128)} %constant.156) | copy-start | bytes 40
  504.6 28.7 %copy-start.36 = (f32[1024,1]{1,0:T(8,128)S(1)}, f32[1024,1]{1,0:T(8,128)}, u32[]{:S(2)}) copy-start(f32[1024,1]{1,0:T(8,128)} %copy-done.35) | copy-start | bytes 12292
  530.4 80.9 %collective-permute-start.6 = (bf16[1024,512]{1,0:T(8,128)(2,1)}, bf16[1024,512]{1,0:T(8,128)(2,1)}, u32[]{:S(2)}, u32[]{:S(2)}) collective-permute-start(bf16[1024,512]{1,0:T(8,128)(2,1)} %get-tuple-element.410), channel_id=1, source_target_pairs={{0,16},{1,17},{2,18},{3,19},{4,20},{5,21},{6,22},{7,23},{8,24},{9,... | collective-permute-start | bytes 3145736 | tf_op jit(solution)/shard_map/ppermute | solution.py:1974
  533.7 4.7 copy-start.21
  533.7 4.7 copy-start.52
  546.3 2.1 copy-start.7
  608.0 3.3 copy-start.18
  608.0 3.3 copy-start.28
  608.0 4.0 copy-start.32
  612.0 4.8 copy-start.51
  620.8 2.2 copy-start.24
  629.3 1.3 copy-start.49
  629.3 7.5 copy-start.22
  630.6 6.2 copy-start.10
  636.8 4.1 copy-start.12
  636.8 4.2 copy-start.15
  693.4 11.9 %copy-start.16 = (bf16[1024,3072]{1,0:T(8,128)(2,1)S(1)}, bf16[1024,3072]{1,0:T(8,128)(2,1)}, u32[]{:S(2)}) copy-start(bf16[1024,3072]{1,0:T(8,128)(2,1)} %shard_map.236.left_ref) | copy-start | bytes 18874372
  693.4 11.9 %copy-start.48 = (f32[1024,1024]{1,0:T(8,128)S(1)}, f32[1024,1024]{1,0:T(8,128)}, u32[]{:S(2)}) copy-start(f32[1024,1024]{1,0:T(8,128)} %get-tuple-element.419.wide_ref) | copy-start | bytes 12582916
  705.2 11.6 %copy-start.39 = (f32[3,1024]{1,0:T(4,128)S(1)}, f32[3,1024]{1,0:T(4,128)}, u32[]{:S(2)}) copy-start(f32[3,1024]{1,0:T(4,128)} %slice_select_fusion) | copy-start | bytes 36868
  705.2 11.5 %copy-start.40 = (f32[4,1024]{1,0:T(4,128)S(1)}, f32[4,1024]{1,0:T(4,128)}, u32[]{:S(2)}) copy-start(f32[4,1024]{1,0:T(4,128)} %reshape.218) | copy-start | bytes 49156
  705.2 12.9 %copy-start.23 = (bf16[2,4,2,2,64,1024]{5,4,3,2,1,0:T(8,128)(2,1)S(1)}, bf16[2,4,2,2,64,1024]{5,4,3,2,1,0:T(8,128)(2,1)}, u32[]{:S(2)}) copy-start(bf16[2,4,2,2,64,1024]{5,4,3,2,1,0:T(8,128)(2,1)} %copy-done.22) | copy-start | bytes 12582916
  715.4 1.3 copy-start.2
  991.8 5.5 copy-start.29
  999.4 3.6 copy-start.33
  1005.1 4.2 copy-start.27
  1009.4 2.5 copy-start.34
  1009.4 3.6 copy-start.30
  (4 other events, 3.7 us)

commit v5 on v4

--- a/solution.py
+++ b/solution.py
@@ -19,7 +19,7 @@
 COL_DIMS = (((1,), (1,)), ((), ()))
 LANES = 2 * HS
 ROWS = 256
-CHUNK = 32
+CHUNK = 64
 AHEAD = 1
 FEED_ROWS = 512
 BLOCK = 1024
@@ -1774,6 +1774,58 @@
     )(alpha, left, weight_rows, rows_wide)
 
 
+def finish_kernel(*refs):
+    half = (len(refs) - 5) // 2
+    small_ref, gain_ref, shift_ref, down_ref, in_ref = (refs[half],) + refs[2 * half + 1 :]
+    rows_in_all = lax.axis_size("tensor")
+
+    @pl.when(pl.program_id(0) == 0)
+    def _():
+        gain_ref[...] = small_ref[0:3]
+        shift_ref[...] = small_ref[3:6]
+        down_ref[...] = small_ref[6:7]
+        candidates = small_ref[7 : 7 + rows_in_all]
+        row = lax.broadcasted_iota(jnp.int32, candidates.shape, 0)
+        mine = jnp.where(row == lax.axis_index("tensor"), candidates, 0.0)
+        in_ref[...] = jnp.sum(mine, axis=0, keepdims=True)
+
+    for source, made in zip(refs[:half], refs[half + 1 : 2 * half + 1]):
+        value = wide(source[...])
+        if source.shape != made.shape:
+            value = jnp.transpose(value)
+        made[...] = value
+
+
+def finish(arrays, turned, small):
+    steps = 4
+    width = small.shape[1]
+    in_specs, out_specs, out_shape = ([], [], [])
+    for array, turn in zip(arrays, turned):
+        rows, width = array.shape
+        if turn:
+            in_specs.append(pl.BlockSpec((rows, width // steps), lambda step: (0, step)))
+            out_specs.append(pl.BlockSpec((width // steps, rows), lambda step: (step, 0)))
+            out_shape.append(jax.ShapeDtypeStruct((width, rows), F32))
+        else:
+            spec = pl.BlockSpec((rows // steps, width), lambda step: (step, 0))
+            in_specs.append(spec)
+            out_specs.append(spec)
+            out_shape.append(jax.ShapeDtypeStruct((rows, width), F32))
+    for rows in (3, 3, 1, 1):
+        out_specs.append(whole_spec((rows, width)))
+        out_shape.append(jax.ShapeDtypeStruct((rows, width), F32))
+    return pl.pallas_call(
+        finish_kernel,
+        grid=(steps,),
+        in_specs=in_specs + [whole_spec(small.shape)],
+        out_specs=out_specs,
+        out_shape=out_shape,
+        compiler_params=pltpu.CompilerParams(
+            dimension_semantics=("arbitrary",), vmem_limit_bytes=48 * 1024 * 1024
+        ),
+    )(*arrays, small)
+
+
 def after(value, *earlier):
     return lax.optimization_barrier((value, earlier))[0]
 
@@ -2044,7 +2096,17 @@
     shift_abs = jnp.dot(
         hot, bias_sum.reshape(-1, bias_size), precision=lax.Precision.HIGHEST
     ).reshape(-1, width)
-    small = jnp.concatenate([sums_a[:2], sums_cd[:2], sums_y[:3], shift_abs])
+    small = jnp.concatenate(
+        [
+            sums_a[0:1],
+            sums_cd[0:1],
+            sums_y[0:1],
+            sums_a[1:2],
+            sums_cd[1:2],
+            sums_y[1:3],
+            shift_abs,
+        ]
+    )
     small = jnp.pad(small, ((0, -small.shape[0] % 8), (0, 0)))
     made = (
         low(rows_tn(grad_qkv, x)),
@@ -2059,29 +2121,26 @@
         [array.reshape(like.shape) for array, like in zip(made, filled)],
         (False, False, False, False, True),
     )
-    input_grad = input_rows.astype(jnp.float32)
-    qkv_grad, out_grad, in_grad, down_grad, cross_grad = [
-        array.astype(jnp.float32) for array in grads
-    ]
-    in_shift_grad = lax.dynamic_index_in_dim(
-        small[7:11].reshape(tensor_count, -1), tensor_index, 0, keepdims=False
-    )
-
-    def columns(ordered):
-        return ordered.reshape(-1, width).T[None]
+    finished = finish(
+        [array.reshape(-1, width) for array in list(grads) + [input_rows]],
+        (True, False, True, False, True, False),
+        small,
+    )
+    qkv_grad, out_grad, in_grad, down_grad, cross_grad, input_grad = finished[:6]
+    gain_grad, shift_grad, down_shift_grad, in_shift_grad = finished[6:]
 
     return (
         outputs[None],
-        input_grad[None],
-        columns(qkv_grad),
-        out_grad.reshape(1, -1, width),
-        columns(cross_grad),
-        columns(in_grad),
-        in_shift_grad[None],
-        down_grad.reshape(1, -1, width),
-        small[6][None],
-        small[jnp.asarray([0, 2, 4])][None],
-        small[jnp.asarray([1, 3, 5])][None],
+        sharded(input_grad)[None],
+        qkv_grad[None],
+        out_grad[None],
+        cross_grad[None],
+        in_grad[None],
+        in_shift_grad,
+        down_grad[None],
+        down_shift_grad,
+        gain_grad[None],
+        shift_grad[None],
     )
 
 

time: 1020 us -> 983 us (0.964)
  other arithmetic: 22.9 us -> 4.38 us
  local copies, waits for them, and re-layouts: 68 us -> 50.8 us
    broadcast_in_dim x3 -> x0, local copies, waits for them, and re-layouts: 10.9 us -> none  [columns(): return ordered.reshape(-1, width).T[None]]
    pallas_call x1, Pallas kernels: 267 us -> 257 us  [reduce_all(): pl.pallas_call(functools.partial(reduce_kernel, paired, depths), in_specs...]
  transfers between devices with their start and end apart: 8 -> 8, of which waited for: 3 -> 3; matrix products, arithmetic and copies ran while one was open for 5% -> 5% of each run, Pallas kernels for 14% -> 15%
where the time goes in v5:
time: 983 us; the launch traced here: 978 us
  Pallas kernels  745 us (76%)
  matrix products  86 us (9%)
  waiting for transfers between devices  65.6 us (7%)
  local copies, waits for them, and re-layouts  50.8 us (5%)
  starting transfers between devices  13.3 us (1%)
  loops' own time  10.2 us (1%)
    pallas_call x1, Pallas kernels, reduce_all(): pl.pallas_call(functools.partial(reduce_kernel, paired, depths), in_specs...  257 us
    pallas_call x1, Pallas kernels, gather_all(): pl.pallas_call(functools.partial(gather_kernel, paired), in_specs=[anywhe...  174 us
    pallas_call x6, Pallas kernels, head_call(): pl.pallas_call(kernel, grid_spec=pltpu.PrefetchScalarGridSpec(num_scalar_...  162 us
    pallas_call x3, Pallas kernels, exchange_in(): pl.pallas_call(functools.partial(exchange_kernel, active), in_specs=[anyw...  57.5 us
    dot_general x6, matrix products, rows_tn(): lax.dot_general(left_rows, right_rows, ROW_DIMS, preferred_element_type=j...  54.1 us
    ppermute x4, waiting for transfers between devices, sequence_body(): lax.ppermute(piece, 'section', [(1, 0)])  36.9 us
    pallas_call x1, Pallas kernels, feed_call(): pl.pallas_call(feed_kernel, grid=(hidden // block,), in_specs=[pl.BlockSp...  31.6 us
    ppermute x2, waiting for transfers between devices, sequence_body(): mixed_held.append(lax.ppermute(mix_made, 'section', [(0, 1)]))  28.7 us
  transfers between devices with their start and end apart: 8, of which 3 were waited for; matrix products, arithmetic and copies ran while one was open for 5% of the time, Pallas kernels for 15%

profile of v5, /device:TPU:9, one launch (start us, length us, event | category | flops | bytes accessed | tf_op | source)
XLA Modules:
  0.0 978.4 jit_solution(14894690728210577520)
XLA Ops:
  16.6 173.7 %shard_map.212 = (bf16[4,256,1024]{2,1,0:T(8,128)(2,1)}, bf16[2,4,2,192,1024]{4,3,2,1,0:T(8,128)(2,1)}, bf16[2,4,2,64,1024]{4,3,2,1,0:T(8,128)(2,1)}, bf16[2,4,2...) custom-call(bf16[4,256,1024]{2,1,0:T(8,128)(2,1)} %bitcast.155, ...), custom_call_target="tpu_custom_call" | custom-call | tf_op jit(solution)/shard_map/pallas_call | solution.py:1356
  190.3 11.5 %convolution_convert_fusion.10.packed_ref = bf16[1024,3072]{1,0:T(8,128)(2,1)} fusion(bf16[1024,1024]{1,0:T(8,128)(2,1)} %bitcast.137, bf16[3072,1024]{1,0:T(8,128)(2,1)} %bitcast.178), kind=kOutput, calls=%fused_computation.25 | convolution fusion | flops 6445596672 | bytes 14680064 | tf_op jit(solution)/shard_map/dot_general | solution.py:976
  201.8 29.3 %shard_map.213 = (bf16[1024,1024]{1,0:T(8,128)(2,1)S(1)}, f32[1024,1024]{1,0:T(8,128)}) custom-call(s32[2]{0:T(128)S(1)} %pad_add_fusion.1.scalars, bf16[1024,3072]{1,0:T(8,128)(2,1)} %convolution_convert_fusion.10.packed_ref), custom_call_target="tpu_custom_call" | custom-call | flops 34359738368 | bytes 6291456 | tf_op jit(solution)/shard_map/pallas_call | solution.py:886
  231.1 6.3 shard_map.214
  241.1 41.0 %conditional.21 = (bf16[1024,4096]{1,0:T(8,128)(2,1)}, bf16[1024,4096]{1,0:T(8,128)(2,1)}, bf16[1024,1024]{1,0:T(8,128)(2,1)}, f32[1024,1024]{1,0:T(8,128)}, f32...) conditional(s32[]{:T(128)} %convert_element_type.98, (f32[3,1024]{1,0:T(4,128)S(1)}, f32[3,1024]{1,0:T(4,128)S(1)}, ...), branch_computations={%region_2.3_spmd, %region_3.4_spmd} | conditional | flops 21476933632 | bytes 60833868 | solution.py:1934
  242.3 31.6 %branch_0_fun.8 = (bf16[1024,4096]{1,0:T(8,128)(2,1)}, bf16[1024,4096]{1,0:T(8,128)(2,1)}, bf16[1024,1024]{1,0:T(8,128)(2,1)}, f32[1024,1024]{1,0:T(8,128)}, f32[1024,1]{1,0:T(8,128)S(1)}) custom-call(f32[1]{0:T(128)} %get-tuple-element.217.alpha_ref, bf16[1024,1024]{1,0:T(8,128)(2,1)} %get-tuple-element.218.low_ref, ...), custom_call_target="tpu_custom_call" | custom-call | flops 17179869184 | bytes 33554432 | tf_op jit(solution)/shard_map/cond/branch_0_fun/pallas_call | solution.py:1052
  273.9 7.8 convolution_convert_fusion.2
  282.9 14.5 %conditional.22 = ((bf16[1024,512]{1,0:T(8,128)(2,1)}, f32[1024,512]{1,0:T(8,128)S(1)})) conditional(s32[]{:T(128)} %convert_element_type.98, (s32[2]{0:T(128)S(1)}, bf16[1024,512]{1,0:T(8,128)(2,1)}, bf16[1024,2048]{1,0:T(8,128)(2,1)}) %tuple.121, () %tuple.122), branch_computations={%region_4.5_spmd, %region_5.6_spmd} | conditional | flops 17179869184 | bytes 3145758 | solution.py:1948
  282.9 14.5 %branch_0_fun.9 = (bf16[1024,512]{1,0:T(8,128)(2,1)}, f32[1024,512]{1,0:T(8,128)S(1)}) custom-call(s32[2]{0:T(128)S(1)} %get-tuple-element.232.scalars, bf16[1024,512]{1,0:T(8,128)(2,1)} %get-tuple-element.233.query_ref, bf16[1024,2048]{1,0:T(8,128)(2,1)} %get-tuple-element.234.key_ref.value_ref, bf16[1024,2048]{1,0:T(8,128)(2,1)} %get-tuple-element.234.key_ref.value_ref), custom_call_target="tpu_custom_call" | custom-call | flops 17179869184 | bytes 3145728 | tf_op jit(solution)/shard_map/cond/branch_0_fun/pallas_call | solution.py:886
  300.0 14.5 %conditional.23 = ((bf16[1024,512]{1,0:T(8,128)(2,1)}, f32[1024,512]{1,0:T(8,128)S(1)})) conditional(s32[]{:T(128)} %convert_element_type.98, (s32[2]{0:T(128)S(1)}, bf16[1024,512]{1,0:T(8,128)(2,1)}, bf16[1024,2048]{1,0:T(8,128)(2,1)}) %tuple.123, () %tuple.124), branch_computations={%region_6.7_spmd, %region_7.8_spmd} | conditional | flops 17179869184 | bytes 3145758 | solution.py:1948
  300.0 14.5 %branch_0_fun.10 = (bf16[1024,512]{1,0:T(8,128)(2,1)}, f32[1024,512]{1,0:T(8,128)S(1)}) custom-call(s32[2]{0:T(128)S(1)} %get-tuple-element.235.scalars, bf16[1024,512]{1,0:T(8,128)(2,1)} %get-tuple-element.236.query_ref, bf16[1024,2048]{1,0:T(8,128)(2,1)} %get-tuple-element.237.key_ref.value_ref, bf16[1024,2048]{1,0:T(8,128)(2,1)} %get-tuple-element.237.key_ref.value_ref), custom_call_target="tpu_custom_call" | custom-call | flops 17179869184 | bytes 3145728 | tf_op jit(solution)/shard_map/cond/branch_0_fun/pallas_call | solution.py:886
  314.5 2.3 collective-permute-start.3
  316.8 6.2 collective-permute-done.1
  323.0 22.5 %collective-permute-done.3 = bf16[1024,512]{1,0:T(8,128)(2,1)} collective-permute-done((bf16[1024,512]{1,0:T(8,128)(2,1)}, bf16[1024,512]{1,0:T(8,128)(2,1)}, u32[]{:S(2)}, u32[]{:S(2)}) %collective-permute-start.3) | collective-permute-done | bytes 1048608 | tf_op jit(solution)/shard_map/ppermute | solution.py:1951
  345.5 57.4 %shard_map.215 = bf16[4,256,1024]{2,1,0:T(8,128)(2,1)} custom-call(bf16[4,256,1024]{2,1,0:T(8,128)(2,1)} %bitcast.53.blocks), custom_call_target="tpu_custom_call" | custom-call | tf_op jit(solution)/shard_map/pallas_call | solution.py:1407
  402.9 27.5 %conditional.24 = (bf16[1024,4096]{1,0:T(8,128)(2,1)}, bf16[1024,1024]{1,0:T(8,128)(2,1)}, bf16[1024,1024]{1,0:T(8,128)(2,1)}, bf16[1024,4096]{1,0:T(8,128)(2,1)...) conditional(s32[]{:T(128)} %convert_element_type.98, () %tuple.116, ...), branch_computations={%region_8.9_spmd, %region_9.10_spmd} | conditional | flops 38655754240 | bytes 218186144 | solution.py:2004
  405.7 1.6 broadcast.122.clone
  410.5 2.7 broadcast.124
  413.2 4.4 broadcast.121.clone
  417.5 4.3 broadcast.121
  433.1 36.9 %collective-permute-done.4 = bf16[1024,512]{1,0:T(8,128)(2,1)S(1)} collective-permute-done((bf16[1024,512]{1,0:T(8,128)(2,1)S(1)}, bf16[1024,512]{1,0:T(8,128)(2,1)S(1)}, u32[]{:S(2)}, u32[]{:S(2)}) %collective-permute-start.4) | collective-permute-done | bytes 1048608 | tf_op jit(solution)/shard_map/ppermute | solution.py:2005
  470.0 25.9 %conditional.25 = ((bf16[1024,512]{1,0:T(8,128)(2,1)}, bf16[1024,1024]{1,0:T(8,128)(2,1)})) conditional(s32[]{:T(128)} %convert_element_type.98, (s32[2]{0:T(128)S(1)}, bf16[1024,512]{1,0:T(8,128)(2,1)}, bf16[1024,2048]{1,0:T(8,128)(2,1)}, bf16[1024,512]{1,0:T(8,128)(2,1)}, bf16[1024,512]{1,0:T(8,128)(2,1)S(1)}, ...), branch_computations={%region_10.11_spmd, %region_11.12_spmd} | conditional | flops 42949672960 | bytes 6291464 | solution.py:2024
  470.0 25.9 %branch_0_fun.11 = (bf16[1024,512]{1,0:T(8,128)(2,1)}, bf16[1024,1024]{1,0:T(8,128)(2,1)}) custom-call(s32[2]{0:T(128)S(1)} %get-tuple-element.269.scalars, bf16[1024,512]{1,0:T(8,128)(2,1)} %get-tuple-element.270.query_ref, bf16[1024,2048]{1,0:T(8,128)(2,1)} %get-tuple-element.271.key_ref.value_ref, ...), custom_call_target="tpu_custom_call" | custom-call | flops 42949672960 | bytes 6291456 | tf_op jit(solution)/shard_map/cond/branch_0_fun/pallas_call | solution.py:886
  495.8 2.3 collective-permute-start.6
  498.1 26.0 %conditional.26 = ((bf16[1024,512]{1,0:T(8,128)(2,1)}, bf16[1024,1024]{1,0:T(8,128)(2,1)})) conditional(s32[]{:T(128)} %convert_element_type.98, (s32[2]{0:T(128)S(1)}, bf16[1024,512]{1,0:T(8,128)(2,1)}, bf16[1024,2048]{1,0:T(8,128)(2,1)}, bf16[1024,512]{1,0:T(8,128)(2,1)}, bf16[1024,512]{1,0:T(8,128)(2,1)S(1)}, ...), branch_computations={%region_12.13_spmd, %region_13.14_spmd} | conditional | flops 42949672960 | bytes 6291464 | solution.py:2024
  498.1 25.8 %branch_0_fun.12 = (bf16[1024,512]{1,0:T(8,128)(2,1)}, bf16[1024,1024]{1,0:T(8,128)(2,1)}) custom-call(s32[2]{0:T(128)S(1)} %get-tuple-element.275.scalars, bf16[1024,512]{1,0:T(8,128)(2,1)} %get-tuple-element.276.query_ref, bf16[1024,2048]{1,0:T(8,128)(2,1)} %get-tuple-element.277.key_ref.value_ref, ...), custom_call_target="tpu_custom_call" | custom-call | flops 42949672960 | bytes 6291456 | tf_op jit(solution)/shard_map/cond/branch_0_fun/pallas_call | solution.py:886
  524.1 2.3 collective-permute-start.7
  526.5 40.2 %conditional.27 = (bf16[1024,1024]{1,0:T(8,128)(2,1)S(1)}, bf16[1024,4096]{1,0:T(8,128)(2,1)}, f32[1,4096]{1,0:T(1,128)S(1)}, f32[1024,1024]{1,0:T(8,128)}, f32[8,1024]{1,0:T(8,128)S(1)}) conditional(s32[]{:T(128)} %convert_element_type.98, (bf16[2048,1024]{1,0:T(8,128)(2,1)}, bf16[1024,1024]{1,0:T(8,128)(2,1)}, bf16[1024,1024]{1,0:T(8,128)(2,1)}, ...), branch_computations={%region_14.15_spmd, %region_15.16_spmd} | conditional | flops 21475885056 | bytes 96477304 | solution.py:2040
  526.6 4.7 fusion
  531.3 2.4 fusion.4.grad_ref
  533.7 4.5 branch_0_fun.13
  538.2 2.0 copy-done.12
  540.2 26.5 %branch_0_fun.14 = (bf16[1024,4096]{1,0:T(8,128)(2,1)}, f32[1,4096]{1,0:T(1,128)S(1)}, f32[1024,1024]{1,0:T(8,128)}) custom-call(f32[1]{0:T(128)} %get-tuple-element.288.alpha_ref, bf16[1024,1024]{1,0:T(8,128)(2,1)S(1)} %get-tuple-element.649.low_ref, f32[1024,1024]{1,0:T(8,128)} %copy-done.12, bf16[4096,1024]{1,0:T(8,128)(2,1)} %get-tuple-element.290.in_ref, ...), custom_call_target="tpu_custom_call" | custom-call | flops 17179869184 | bytes 33554432 | tf_op jit(solution)/shard_map/cond/branch_0_fun/pallas_call | solution.py:1123
  568.9 15.3 %conditional.29 = (bf16[2,4,2,256,1024]{4,3,2,1,0:T(8,128)(2,1)}) conditional(s32[]{:T(128)} %convert_element_type.98, (bf16[1024,4096]{1,0:T(8,128)(2,1)}, bf16[1024,1024]{1,0:T(8,128)(2,1)}) %tuple.140, (bf16[1024,4096]{1,0:T(8,128)(2,1)}, bf16[1024,1024]{1,0:T(8,128)(2,1)}) %tuple.141), branch_computations={%region_18.19_spmd, %region_19.20_spmd} | conditional | flops 8594128896 | bytes 18874376 | solution.py:2079
  569.1 15.1 %convolution_convert_fusion.5 = bf16[4096,1024]{1,0:T(8,128)(2,1)} fusion(bf16[1024,4096]{1,0:T(8,128)(2,1)} %get-tuple-element.322, bf16[1024,1024]{1,0:T(8,128)(2,1)} %get-tuple-element.323), kind=kOutput, calls=%fused_computation.20 | convolution fusion | flops 8594128896 | bytes 18874368 | tf_op jit(solution)/shard_map/cond/branch_0_fun/dot_general | solution.py:984
  584.2 15.6 %conditional.30 = (bf16[2,4,2,256,1024]{4,3,2,1,0:T(8,128)(2,1)}) conditional(s32[]{:T(128)} %convert_element_type.98, (bf16[1024,4096]{1,0:T(8,128)(2,1)}, bf16[1024,1024]{1,0:T(8,128)(2,1)}) %tuple.220, (bf16[1024,4096]{1,0:T(8,128)(2,1)}, bf16[1024,1024]{1,0:T(8,128)(2,1)}) %tuple.143), branch_computations={%region_20.21_spmd, %region_21.22_spmd} | conditional | flops 8594128896 | bytes 18874376 | solution.py:2072
  584.6 15.2 %convolution_convert_fusion.7 = bf16[4096,1024]{1,0:T(8,128)(2,1)} fusion(bf16[1024,4096]{1,0:T(8,128)(2,1)} %get-tuple-element.326, bf16[1024,1024]{1,0:T(8,128)(2,1)} %get-tuple-element.327), kind=kOutput, calls=%fused_computation.22 | convolution fusion | flops 8594128896 | bytes 18874368 | tf_op jit(solution)/shard_map/cond/branch_0_fun/dot_general | solution.py:984
  603.2 16.4 %conditional.28 = (f32[1024,1024]{1,0:T(8,128)}, bf16[1024,1024]{1,0:T(8,128)(2,1)}, f32[8,1024]{1,0:T(8,128)S(1)}, bf16[2,4,2,2,64,1024]{5,4,3,2,1,0:T(8,128)(2,1)S(1)}) conditional(s32[]{:T(128)} %convert_element_type.98, (f32[3,1024]{1,0:T(4,128)S(1)}, f32[1024,1024]{1,0:T(8,128)}, f32[1024,1024]{1,0:T(8,128)}, f32[1024,1]{1,0:T(8,128)S(1)}, ...), branch_computations={%region_16.17_spmd, %region_17.18_spmd} | conditional | flops 6450839552 | bytes 67117120 | solution.py:2183
  603.2 7.6 branch_0_fun.15
  610.7 4.2 fusion.28
  614.9 4.0 fusion.29
  619.6 5.5 convolution_convert_fusion.12.grad_ref
  625.2 3.7 convolution_convert_fusion.11
  628.9 52.4 %shard_map.218.left_ref = bf16[1024,3072]{1,0:T(8,128)(2,1)} custom-call(s32[2]{0:T(128)S(1)} %copy-done.18, bf16[1024,3072]{1,0:T(8,128)(2,1)} %convolution_convert_fusion.10.packed_ref, bf16[1024,1024]{1,0:T(8,128)(2,1)S(1)} %copy-done.20, bf16[1024,1024]{1,0:T(8,128)(2,1)S(1)} %convolution_convert_fusion.12.grad_ref, f32[1024,1024]{1,0:T(8,128)} %get-tuple-element.461.lse_ref), custom_call_target="tpu_custom_call" | custom-call | flops 85899345920 | bytes 12582912 | tf_op jit(solution)/shard_map/pallas_call | solution.py:886
  681.3 12.0 %convolution_convert_fusion.9 = bf16[3072,1024]{1,0:T(8,128)(2,1)} fusion(bf16[1024,3072]{1,0:T(8,128)(2,1)} %shard_map.218.left_ref, bf16[1024,1024]{1,0:T(8,128)(2,1)S(1)} %bitcast.139), kind=kOutput, calls=%fused_computation.24 | convolution fusion | flops 6445596672 | bytes 14680064 | tf_op jit(solution)/shard_map/dot_general | solution.py:984
  693.3 10.0 %shard_map.219 = bf16[1024,1024]{1,0:T(8,128)(2,1)S(1)} custom-call(f32[1]{0:T(128)} %bitcast.38.alpha_ref, bf16[1024,3072]{1,0:T(8,128)(2,1)S(1)} %copy-done.21, bf16[3072,1024]{1,0:T(8,128)(2,1)} %bitcast.179, f32[1024,1024]{1,0:T(8,128)S(1)} %copy-done.51), custom_call_target="tpu_custom_call" | custom-call | flops 6442450944 | bytes 18874368 | tf_op jit(solution)/shard_map/pallas_call | solution.py:1755
  705.5 256.7 %shard_map.220 = (bf16[4,256,1024]{2,1,0:T(8,128)(2,1)}, f32[16,1024]{1,0:T(8,128)}, bf16[4,192,1024]{2,1,0:T(8,128)(2,1)}, bf16[4,64,1024]{2,1,0:T(8,128)(2,1)}...) custom-call(bf16[4,256,1024]{2,1,0:T(8,128)(2,1)} %bitcast.131, ...), custom_call_target="tpu_custom_call" | custom-call | tf_op jit(solution)/shard_map/pallas_call | solution.py:1649
  968.4 8.3 shard_map.221
  (164 shorter events, 47.1 us)
Async XLA Ops:
  0.6 5.0 copy-start.36
  5.6 2.3 copy-start.49
  8.0 3.5 copy-start.39
  10.4 4.2 copy-start.40
  14.6 187.2 %copy-start.17 = (s32[2]{0:T(128)}, s32[2]{0:T(128)S(1)}, u32[]{:S(2)}) copy-start(s32[2]{0:T(128)S(1)} %pad_add_fusion.1.scalars) | copy-start | bytes 28
  201.8 29.3 %copy-start.13 = (bf16[4,256,1024]{2,1,0:T(8,128)(2,1)S(1)}, bf16[4,256,1024]{2,1,0:T(8,128)(2,1)}, u32[]{:S(2)}) copy-start(bf16[4,256,1024]{2,1,0:T(8,128)(2,1)} %get-tuple-element.419) | copy-start | bytes 6291460
  201.8 29.3 %copy-start.15 = (bf16[2,4,2,64,1024]{4,3,2,1,0:T(8,128)(2,1)S(1)}, bf16[2,4,2,64,1024]{4,3,2,1,0:T(8,128)(2,1)}, u32[]{:S(2)}) copy-start(bf16[2,4,2,64,1024]{4,3,2,1,0:T(8,128)(2,1)} %get-tuple-element.422) | copy-start | bytes 6291460
  231.1 6.3 copy-start.19
  231.1 6.3 copy-start.22
  237.4 2.8 copy-start.48
  237.6 45.3 %collective-permute-start = (bf16[1024,512]{1,0:T(8,128)(2,1)S(1)}, bf16[1024,512]{1,0:T(8,128)(2,1)}, u32[]{:S(2)}, u32[]{:S(2)}) collective-permute-start(bf16[1024,512]{1,0:T(8,128)(2,1)S(1)} %get-tuple-element.424), channel_id=1, source_target_pairs={{16,0},{17,1},{18,2},{19,3},{20,4},{21,5},{22,6},{23,7},{24,8},{25... | collective-permute-start | bytes 3145736 | tf_op jit(solution)/shard_map/ppermute | solution.py:1913
  238.9 61.1 %collective-permute-start.2 = (bf16[1024,512]{1,0:T(8,128)(2,1)S(1)}, bf16[1024,512]{1,0:T(8,128)(2,1)}, u32[]{:S(2)}, u32[]{:S(2)}) collective-permute-start(bf16[1024,512]{1,0:T(8,128)(2,1)S(1)} %get-tuple-element.431), channel_id=1, source_target_pairs={{16,0},{17,1},{18,2},{19,3},{20,4},{21,5},{22,6},{23,7},{24,8},{25... | collective-permute-start | bytes 3145736 | tf_op jit(solution)/shard_map/ppermute | solution.py:1913
  242.3 31.6 %copy-start.24 = (bf16[2048,1024]{1,0:T(8,128)(2,1)S(1)}, bf16[2048,1024]{1,0:T(8,128)(2,1)}, u32[]{:S(2)}) copy-start(bf16[2048,1024]{1,0:T(8,128)(2,1)} %get-tuple-element.231) | copy-start | bytes 12582916 | tf_op jit(solution)/shard_map/cond
  298.6 24.4 %collective-permute-start.1 = (bf16[1024,512]{1,0:T(8,128)(2,1)}, bf16[1024,512]{1,0:T(8,128)(2,1)S(1)}, u32[]{:S(2)}, u32[]{:S(2)}) collective-permute-start(bf16[1024,512]{1,0:T(8,128)(2,1)} %get-tuple-element.430), channel_id=1, source_target_pairs={{0,16},{1,17},{2,18},{3,19},{4,20},{5,21},{6,22},{7,23},{8,24},{9,... | collective-permute-start | bytes 3145736 | tf_op jit(solution)/shard_map/ppermute | solution.py:1951
  314.5 2.3 copy-start.55
  314.5 31.0 %collective-permute-start.3 = (bf16[1024,512]{1,0:T(8,128)(2,1)}, bf16[1024,512]{1,0:T(8,128)(2,1)}, u32[]{:S(2)}, u32[]{:S(2)}) collective-permute-start(bf16[1024,512]{1,0:T(8,128)(2,1)} %get-tuple-element.432), channel_id=1, source_target_pairs={{0,16},{1,17},{2,18},{3,19},{4,20},{5,21},{6,22},{7,23},{8,24},{9,... | collective-permute-start | bytes 3145736 | tf_op jit(solution)/shard_map/ppermute | solution.py:1951
  323.0 79.9 %copy-start.32 = (bf16[1024,512]{1,0:T(8,128)(2,1)}, bf16[1024,512]{1,0:T(8,128)(2,1)S(1)}, u32[]{:S(2)}) copy-start(bf16[1024,512]{1,0:T(8,128)(2,1)S(1)} %collective-permute-done.1) | copy-start | bytes 3145732
  402.9 30.1 %copy-start.50 = (s32[4]{0:T(128)S(1)}, s32[4]{0:T(128)}, u32[]{:S(2)}) copy-start(s32[4]{0:T(128)} %constant.126.clone) | copy-start | bytes 52
  430.4 39.6 %copy-start.44 = (f32[1,1024]{1,0:T(1,128)}, f32[1,1024]{1,0:T(1,128)S(1)}, u32[]{:S(2)}) copy-start(f32[1,1024]{1,0:T(1,128)S(1)} %get-tuple-element.467) | copy-start | bytes 12292
  430.4 39.5 %copy-start.46 = (f32[1,1024]{1,0:T(1,128)}, f32[1,1024]{1,0:T(1,128)S(1)}, u32[]{:S(2)}) copy-start(f32[1,1024]{1,0:T(1,128)S(1)} %get-tuple-element.464) | copy-start | bytes 12292
  430.5 39.5 %collective-permute-start.4 = (bf16[1024,512]{1,0:T(8,128)(2,1)S(1)}, bf16[1024,512]{1,0:T(8,128)(2,1)S(1)}, u32[]{:S(2)}, u32[]{:S(2)}) collective-permute-start(bf16[1024,512]{1,0:T(8,128)(2,1)S(1)} %get-tuple-element.439), channel_id=1, source_target_pairs={{16,0},{17,1},{18,2},{19,3},{20,4},{21,5},{22,6},{23,7},{24,8},{25... | collective-permute-start | bytes 3145736 | tf_op jit(solution)/shard_map/ppermute | solution.py:2005
  431.8 66.4 %collective-permute-start.5 = (bf16[1024,512]{1,0:T(8,128)(2,1)}, bf16[1024,512]{1,0:T(8,128)(2,1)S(1)}, u32[]{:S(2)}, u32[]{:S(2)}) collective-permute-start(bf16[1024,512]{1,0:T(8,128)(2,1)} %get-tuple-element.440), channel_id=1, source_target_pairs={{16,0},{17,1},{18,2},{19,3},{20,4},{21,5},{22,6},{23,7},{24,8},{25... | collective-permute-start | bytes 3145736 | tf_op jit(solution)/shard_map/ppermute | solution.py:2005
  495.8 105.5 %collective-permute-start.6 = (bf16[1024,512]{1,0:T(8,128)(2,1)}, bf16[1024,512]{1,0:T(8,128)(2,1)}, u32[]{:S(2)}, u32[]{:S(2)}) collective-permute-start(bf16[1024,512]{1,0:T(8,128)(2,1)} %get-tuple-element.453), channel_id=1, source_target_pairs={{0,16},{1,17},{2,18},{3,19},{4,20},{5,21},{6,22},{7,23},{8,24},{9,... | collective-permute-start | bytes 3145736 | tf_op jit(solution)/shard_map/ppermute | solution.py:2026
  498.1 28.4 %copy-start.38 = (f32[1024,1]{1,0:T(8,128)S(1)}, f32[1024,1]{1,0:T(8,128)}, u32[]{:S(2)}) copy-start(f32[1024,1]{1,0:T(8,128)} %copy-done.37) | copy-start | bytes 12292
  524.1 77.2 %collective-permute-start.7 = (bf16[1024,512]{1,0:T(8,128)(2,1)}, bf16[1024,512]{1,0:T(8,128)(2,1)}, u32[]{:S(2)}, u32[]{:S(2)}) collective-permute-start(bf16[1024,512]{1,0:T(8,128)(2,1)} %get-tuple-element.454), channel_id=1, source_target_pairs={{0,16},{1,17},{2,18},{3,19},{4,20},{5,21},{6,22},{7,23},{8,24},{9,... | collective-permute-start | bytes 3145736 | tf_op jit(solution)/shard_map/ppermute | solution.py:2026
  526.6 4.7 copy-start.26
  526.6 4.7 copy-start.56
  538.2 2.1 copy-start.12
  584.2 15.6 %copy-start.29 = (bf16[4,256,1024]{2,1,0:T(8,128)(2,1)S(1)}, bf16[4,256,1024]{2,1,0:T(8,128)(2,1)}, u32[]{:S(2)}) copy-start(bf16[4,256,1024]{2,1,0:T(8,128)(2,1)} %shard_map.215) | copy-start | bytes 6291460
  599.8 2.9 copy-start.23
  599.8 3.1 copy-start.31
  599.8 3.4 copy-start.33
  603.2 16.4 %copy-start.16 = (bf16[2,4,2,64,1024]{4,3,2,1,0:T(8,128)(2,1)S(1)}, bf16[2,4,2,64,1024]{4,3,2,1,0:T(8,128)(2,1)}, u32[]{:S(2)}) copy-start(bf16[2,4,2,64,1024]{4,3,2,1,0:T(8,128)(2,1)} %get-tuple-element.422) | copy-start | bytes 6291460
  603.2 7.6 copy-start.57
  610.7 4.2 copy-start.58
  619.6 5.5 copy-start.27
  619.6 5.5 copy-start.20
  619.6 5.5 copy-start.53
  625.1 3.7 copy-start.18
  628.9 52.4 %copy-start.14 = (bf16[4,256,1024]{2,1,0:T(8,128)(2,1)S(1)}, bf16[4,256,1024]{2,1,0:T(8,128)(2,1)}, u32[]{:S(2)}) copy-start(bf16[4,256,1024]{2,1,0:T(8,128)(2,1)} %get-tuple-element.419) | copy-start | bytes 6291460
  681.3 12.0 %copy-start.21 = (bf16[1024,3072]{1,0:T(8,128)(2,1)S(1)}, bf16[1024,3072]{1,0:T(8,128)(2,1)}, u32[]{:S(2)}) copy-start(bf16[1024,3072]{1,0:T(8,128)(2,1)} %shard_map.218.left_ref) | copy-start | bytes 18874372
  681.3 12.0 %copy-start.51 = (f32[1024,1024]{1,0:T(8,128)S(1)}, f32[1024,1024]{1,0:T(8,128)}, u32[]{:S(2)}) copy-start(f32[1024,1024]{1,0:T(8,128)} %get-tuple-element.462.wide_ref) | copy-start | bytes 12582916
  693.3 11.4 %copy-start.41 = (f32[4,1024]{1,0:T(4,128)S(1)}, f32[4,1024]{1,0:T(4,128)}, u32[]{:S(2)}) copy-start(f32[4,1024]{1,0:T(4,128)} %reshape.217) | copy-start | bytes 49156
  693.3 11.4 %copy-start.42 = (f32[2,1024]{1,0:T(2,128)S(1)}, f32[2,1024]{1,0:T(2,128)}, u32[]{:S(2)}) copy-start(f32[2,1024]{1,0:T(2,128)} %slice.139) | copy-start | bytes 24580
  693.3 11.4 %copy-start.43 = (f32[1,1024]{1,0:T(1,128)S(1)}, f32[1,1024]{1,0:T(1,128)}, u32[]{:S(2)}) copy-start(f32[1,1024]{1,0:T(1,128)} %slice.138) | copy-start | bytes 12292
  693.3 11.4 %copy-start.45 = (f32[1,1024]{1,0:T(1,128)S(1)}, f32[1,1024]{1,0:T(1,128)}, u32[]{:S(2)}) copy-start(f32[1,1024]{1,0:T(1,128)} %copy-done.44) | copy-start | bytes 12292
  693.3 11.4 %copy-start.47 = (f32[1,1024]{1,0:T(1,128)S(1)}, f32[1,1024]{1,0:T(1,128)}, u32[]{:S(2)}) copy-start(f32[1,1024]{1,0:T(1,128)} %copy-done.46) | copy-start | bytes 12292
  962.3 1.6 copy-start.2
  (8 other events, 9.3 us)
